TPU v7x, 32 devices: a whole 2x2x4 slice. The times are simulated.
32 devices in a mesh: dom: 8 (over z, x), rep: 4 (over y, core).
Axes of the slice: x: 2, y: 2, z: 4, core: 2. Of those that a mesh axis runs over, the one named last changes fastest.
Arguments:
- features: float32 [128, 4096], P('rep', 'dom'), may hold values from -6 to 6
- tiles: bfloat16 [320, 128, 128], P('dom'), may hold values from -0.25 to 0.25
- tile_row: int32 [320], P('dom'), may hold values from 0 to 3
- tile_col: int32 [320], P('dom'), may hold values from 0 to 31, as said below
- tile_count: int32 [8], P('dom'), may hold values from 16 to 40, as said below
- dest_slot: int32 [4096], P('dom'), may hold values from 0 to 4095, as said below
- w_in: bfloat16 [128, 1024], replicated, may hold values from -0.5 to 0.5
- w_mid: bfloat16 [1024, 1024], replicated, may hold values from -0.1875 to 0.1875
- w_out: bfloat16 [172, 1024], replicated, may hold values from -0.1875 to 0.1875
- cotangent: bfloat16 [172, 4096], P(None, ('dom', 'rep')), may hold values from -0.09375 to 0.09375
Outputs:
- batch_features: float32 [128, 4096], P(None, ('dom', 'rep'))
- grad_w_in: float32 [128, 1024], replicated
- grad_w_mid: float32 [1024, 1024], P('dom')
- grad_w_out: float32 [172, 1024], replicated
Inputs may be any that keep to these rules, and one draw needn't show every extreme that they name: `tile_col`: every slot of partition p, live or not, names a block column within 4 blocks of p's own blocks p * 4 to (p+1) * 4 - 1, counted modulo 32; each of the 8 blocks just before and just after p's own is named by one of p's first 8 slots. `tile_count`: counts vary from partition to partition (several partitions may share a count); at least one partition holds exactly 40 live slots. `dest_slot`: A permutation of the batch positions; each graph partition sends exactly 16 node into each block of 128 consecutive batch positions.
All inputs are finite; a program needn't handle non-finite values.
Results may differ from a plain program's by a relative error of at most 0.006.
Values sent between devices are 32-bit elements; how exact they have to be, the bound alone decides.
No kernel may reach another device: no remote copies, remote signals or barrier semaphores. Data moves between devices by JAX's collectives and lax.ppermute only.
A program may use at most 64 MiB of HBM per device.

v0:
```python
import jax
import jax.numpy as jnp
from jax import lax
from jax.sharding import PartitionSpec as P

series_zero = 0.3085083
series_one = -0.4305395
series_two = 0.1864784
LEADING = (((0,), (0,)), ((), ()))
TRAILING = (((1,), (1,)), ((), ()))


def extended_2(cells, sides, width):
    for axis, dim in sides:
        count = lax.axis_size(axis)
        head = lax.slice_in_dim(cells, 0, width, axis=dim)
        tail = lax.slice_in_dim(cells, cells.shape[dim] - width, cells.shape[dim], axis=dim)
        cells = jnp.concatenate(
            [
                lax.ppermute(tail, axis, [(i, (i + 1) % count) for i in range(count)]),
                cells,
                lax.ppermute(head, axis, [((i + 1) % count, i) for i in range(count)]),
            ],
            axis=dim,
        )
    return cells


def silu_slope(pre):
    sigma = jax.nn.sigmoid(pre)
    return sigma * (1.0 + pre * (1.0 - sigma))


def neighbour_blocks(local, margin, tile_size):
    extended = extended_2(local, (("dom", 1),), margin * tile_size)
    return extended


def apply_operator(local, tiles_across, assignment_map, relative, margin):
    feature_count, node_count = local.shape
    tile_size = tiles_across.shape[1]
    extended = neighbour_blocks(local, margin, tile_size)
    blocks = extended.reshape(feature_count, -1, tile_size)
    input_values = jnp.take(blocks, relative, axis=1)
    block_products = jnp.einsum(
        "lkz,glz->glk", tiles_across, input_values, precision=lax.Precision.HIGHEST
    )
    final_result = jnp.einsum(
        "wy,kya->kwa", assignment_map, block_products, precision=lax.Precision.HIGHEST
    )
    return final_result.reshape(feature_count, node_count)


def shards(
    features, tiles, tile_row, tile_col, tile_count, dest_slot, w_in, w_mid, w_out, cotangent
):
    node_partition = lax.axis_index("dom")
    owners = lax.axis_size("dom")
    replicas = lax.axis_size("rep")
    feature_count, node_count = features.shape
    capacity = tiles.shape[0]
    tile_size = tiles.shape[1]
    block_count = node_count // tile_size
    total_blocks = block_count * owners
    relative = jnp.mod(tile_col - node_partition * block_count + block_count, total_blocks)
    live_mask = (jnp.arange(capacity, dtype=jnp.int32) < tile_count[0]).astype(jnp.float32)
    assignment_map = (
        tile_row[None, :] == jnp.arange(block_count, dtype=jnp.int32)[:, None]
    ).astype(jnp.float32) * live_mask[None, :]
    tiles_across = tiles.astype(jnp.float32)
    first = apply_operator(features, tiles_across, assignment_map, relative, block_count)
    second = (
        2.0 * apply_operator(first, tiles_across, assignment_map, relative, block_count) - features
    )
    diffused = series_zero * features + series_one * first + series_two * second
    segment = node_count // (owners * replicas)
    batch_rows = node_count // replicas
    sort_order = jnp.argsort(dest_slot)
    sorted_slots = jnp.take(dest_slot, sort_order)
    moved_rows = jnp.take(diffused, sort_order, axis=1).reshape(
        feature_count, owners, replicas, segment
    )
    moved_slots = sorted_slots.astype(jnp.float32).reshape(1, owners, replicas, segment)
    arrived, arrived_slots = (
        lax.all_to_all(
            lax.all_to_all(moved_rows, "dom", split_axis=1, concat_axis=1, tiled=True),
            "rep",
            split_axis=2,
            concat_axis=0,
            tiled=True,
        ),
        lax.all_to_all(
            lax.all_to_all(moved_slots, "dom", split_axis=1, concat_axis=1, tiled=True),
            "rep",
            split_axis=2,
            concat_axis=0,
            tiled=True,
        ),
    )
    owner_index = node_partition * replicas + lax.axis_index("rep")
    local_slots = arrived_slots[0].reshape(-1).astype(jnp.int32) - owner_index * batch_rows
    gathered = arrived.reshape(feature_count * replicas, -1)
    batch_features = jnp.zeros(gathered.shape, jnp.float32).at[:, local_slots].set(gathered)
    inputs_bf = batch_features.astype(jnp.bfloat16)
    pre_one = lax.dot_general(inputs_bf, w_in, LEADING, preferred_element_type=jnp.float32)
    hidden_one = jax.nn.silu(pre_one).astype(jnp.bfloat16)
    pre_two = jnp.dot(hidden_one, w_mid, preferred_element_type=jnp.float32)
    hidden_two = jax.nn.silu(pre_two).astype(jnp.bfloat16)
    grad_out = jnp.dot(cotangent, hidden_two, preferred_element_type=jnp.float32)
    back_two = lax.dot_general(cotangent, w_out, LEADING, preferred_element_type=jnp.float32)
    delta_two = (back_two * silu_slope(pre_two)).astype(jnp.bfloat16)
    back_one = lax.dot_general(delta_two, w_mid, TRAILING, preferred_element_type=jnp.float32)
    delta_one = (back_one * silu_slope(pre_one)).astype(jnp.bfloat16)
    grad_in = jnp.dot(inputs_bf, delta_one, preferred_element_type=jnp.float32)
    mid_shard = lax.psum_scatter(
        lax.dot_general(hidden_one, delta_two, LEADING, preferred_element_type=jnp.float32),
        "dom",
        scatter_dimension=0,
        tiled=True,
    )
    grad_mid = lax.psum(mid_shard, "rep")
    grad_in, grad_out = lax.psum((grad_in, grad_out), ("dom", "rep"))
    return (batch_features, grad_in, grad_mid, grad_out)


def solution(mesh):
    in_specs = (
        P("rep", "dom"),
        P("dom", None, None),
        P("dom"),
        P("dom"),
        P("dom"),
        P("dom"),
        P(),
        P(),
        P(),
        P(None, ("dom", "rep")),
    )
    out_specs = (P(None, ("dom", "rep")), P(), P("dom", None), P())
    return jax.shard_map(shards, mesh=mesh, in_specs=in_specs, out_specs=out_specs, check_vma=False)
```

profile of v0, /device:TPU:0, one launch (start us, length us, event | category | flops | bytes accessed | tf_op | source)
XLA Modules:
  0.0 305.1 jit_solution(16346657162458378972)
XLA Ops:
  8.0 3.0 collective-permute-start
  11.0 3.1 %collective-permute-start.1 = (f32[32,512]{1,0:T(8,128)}, f32[32,512]{1,0:T(8,128)}, u32[]{:S(2)}, u32[]{:S(2)}) collective-permute-start(f32[32,512]{1,0:T(8,128)} %param.12), channel_id=1, source_target_pairs={{4,0},{8,4},{12,8},{16,12},{20,16},{24,20},{28,24},{0,28},{5,1},{9... | collective-permute-start | bytes 196616 | tf_op jit(solution)/shard_map/ppermute | solution.py:22
  14.1 4.4 %sort.17 = (s32[512]{0:T(512)}, s32[512]{0:T(512)S(1)}) sort(s32[512]{0:T(512)} %param.17, s32[512]{0:T(512)S(1)} %iota.13), dimensions={0}, to_apply=%region_0.1 | sort | flops 4608 | bytes 8192 | tf_op jit(solution)/shard_map/jit(argsort)/sort | solution.py:78
  18.6 3.6 %gather_fusion = s32[512]{0:T(512)S(1)} fusion(s32[512]{0:T(512)} %param.17, s32[1024]{0:T(1024)S(1)} %pad_clamp_fusion.1), kind=kCustom, calls=%fused_computation.2 | custom fusion | bytes 6144 | tf_op jit(solution)/shard_map/jit(_take)/gather | solution.py:79
  22.9 3.3 %all-to-all-start = ((f32[1,8,4,16]{3,2,0,1:T(4,128)}), f32[1,8,4,16]{3,2,0,1:T(4,128)S(1)}, u32[]{:S(2)}, u32[]{:S(2)}) async-start(f32[1,8,4,16]{3,2,0,1:T(4,128)} %bitcast), calls=%async_computation | async-start | bytes 32768 | tf_op jit(solution)/shard_map/all_to_all | solution.py:93
  27.0 5.8 %all-to-all-done = f32[1,8,4,16]{3,2,0,1:T(4,128)S(1)} async-done(((f32[1,8,4,16]{3,2,0,1:T(4,128)}), f32[1,8,4,16]{3,2,0,1:T(4,128)S(1)}, u32[]{:S(2)}, u32[]{:S(2)}) %all-to-all-start) | async-done | bytes 2080 | tf_op jit(solution)/shard_map/all_to_all | solution.py:93
  33.5 3.2 %all-to-all-start.1 = ((f32[4,1,128]{2,1,0:T(1,128)}), f32[4,1,128]{2,1,0:T(1,128)S(1)}, u32[]{:S(2)}, u32[]{:S(2)}) async-start(f32[4,1,128]{2,1,0:T(1,128)} %reshape.155), calls=%async_computation.1 | async-start | bytes 4096 | tf_op jit(solution)/shard_map/all_to_all | solution.py:92
  37.4 2.9 all-to-all-done.1
  43.2 2.3 gather_fusion.2
  45.6 3.3 %convolution_bitcast_fusion.2 = f32[32,40,128]{2,0,1:T(8,128)S(1)} fusion(bf16[40,128,128]{2,1,0:T(8,128)(2,1)S(1)} %copy-done.1, f32[40,32,128]{2,1,0:T(8,128)} %gather_fusion.2, pred[40]{0:T(512)(128)(4,1)S(1)} %get-tuple-element.33), kind=kOutput, calls=%fused_computation.7 | convolution fusion | flops 251822080 | bytes 2621480 | tf_op jit(solution)/shard_map/lkz,glz->glk/dot_general | solution.py:45
  50.9 4.2 %collective-permute-start.3 = (f32[32,512]{1,0:T(8,128)}, f32[32,512]{1,0:T(8,128)}, u32[]{:S(2)}, u32[]{:S(2)}) collective-permute-start(f32[32,512]{1,0:T(8,128)} %bitcast.83), channel_id=1, source_target_pairs={{4,0},{8,4},{12,8},{16,12},{20,16},{24,20},{28,24},{0,28},{5,1},{9... | collective-permute-start | bytes 196616 | tf_op jit(solution)/shard_map/ppermute | solution.py:22
  55.1 2.6 collective-permute-done.2
  61.6 2.5 gather_fusion.3
  64.1 3.3 %convolution_bitcast_fusion.1 = f32[32,40,128]{2,0,1:T(8,128)S(1)} fusion(bf16[40,128,128]{2,1,0:T(8,128)(2,1)S(1)} %copy-done.1, f32[40,32,128]{2,1,0:T(8,128)} %gather_fusion.3, pred[40]{0:T(512)(128)(4,1)} %copy-done.8), kind=kOutput, calls=%fused_computation.6 | convolution fusion | flops 251822080 | bytes 2621480 | tf_op jit(solution)/shard_map/lkz,glz->glk/dot_general | solution.py:45
  71.3 5.1 %all-to-all-start.2 = ((f32[8,1,2048]{2,1,0:T(1,128)}), f32[8,1,2048]{2,1,0:T(1,128)S(1)}, u32[]{:S(2)}, u32[]{:S(2)}) async-start(f32[8,1,2048]{2,1,0:T(1,128)} %reshape.157), calls=%async_computation.2 | async-start | bytes 131072 | tf_op jit(solution)/shard_map/all_to_all | solution.py:86
  76.5 6.8 %all-to-all-done.2 = f32[8,1,2048]{2,1,0:T(1,128)S(1)} async-done(((f32[8,1,2048]{2,1,0:T(1,128)}), f32[8,1,2048]{2,1,0:T(1,128)S(1)}, u32[]{:S(2)}, u32[]{:S(2)}) %all-to-all-start.2) | async-done | bytes 65568 | tf_op jit(solution)/shard_map/all_to_all | solution.py:86
  85.0 3.3 %all-to-all-start.3 = ((f32[4,1,4096]{2,1,0:T(1,128)}), f32[4,1,4096]{2,1,0:T(1,128)S(1)}, u32[]{:S(2)}, u32[]{:S(2)}) async-start(f32[4,1,4096]{2,1,0:T(1,128)} %reshape.159), calls=%async_computation.3 | async-start | bytes 131072 | tf_op jit(solution)/shard_map/all_to_all | solution.py:85
  88.4 4.0 %all-to-all-done.3 = f32[4,1,4096]{2,1,0:T(1,128)S(1)} async-done(((f32[4,1,4096]{2,1,0:T(1,128)}), f32[4,1,4096]{2,1,0:T(1,128)S(1)}, u32[]{:S(2)}, u32[]{:S(2)}) %all-to-all-start.3) | async-done | bytes 65568 | tf_op jit(solution)/shard_map/all_to_all | solution.py:85
  96.1 2.7 fusion.47
  102.0 87.3 %reduce-scatter.2.cloned.1.call-done = f32[128,1024]{1,0:T(8,128)} async-done(((f32[1024,1024]{1,0:T(8,128)}), f32[128,1024]{1,0:T(8,128)}) %reduce-scatter.2.cloned.1.call-update) | async-done | bytes 524304 | tf_op jit(solution)/shard_map/reduce_scatter | solution.py:115
  190.1 67.4 %all-reduce.6.cloned.1.call-done = (f32[128,1024]{1,0:T(8,128)}, f32[172,1024]{1,0:T(8,128)}) async-done(((f32[128,1024]{1,0:T(8,128)}, f32[172,1024]{1,0:T(8,128)}), (f32[128,1024]{1,0:T(8,128)}, f32[172,1024]{1,0:T(8,128)})) %all-reduce.6.cloned.1.call-update) | async-done | bytes 1228816 | tf_op jit(solution)/shard_map/psum | solution.py:122
  257.5 35.5 %all-reduce.4.cloned.1.call-done = f32[128,1024]{1,0:T(8,128)} async-done(((f32[128,1024]{1,0:T(8,128)}), f32[128,1024]{1,0:T(8,128)}) %all-reduce.4.cloned.1.call-update) | async-done | bytes 524304 | tf_op jit(solution)/shard_map/psum | solution.py:121
  293.0 1.9 copy.97
  294.9 1.9 copy.98
  (90 shorter events, 25.0 us)
Async XLA Ops:
  8.0 86.8 %copy-start = (bf16[1024,1024]{1,0:T(8,128)(2,1)S(1)}, bf16[1024,1024]{1,0:T(8,128)(2,1)}, u32[]{:S(2)}) copy-start(bf16[1024,1024]{1,0:T(8,128)(2,1)} %param.19) | copy-start | bytes 6291460
  8.0 33.6 %copy-start.4 = (f32[32,512]{1,0:T(8,128)S(1)}, f32[32,512]{1,0:T(8,128)}, u32[]{:S(2)}) copy-start(f32[32,512]{1,0:T(8,128)} %param.12) | copy-start | bytes 196612
  8.0 18.3 %copy-start.13 = (s32[40]{0:T(128)S(1)}, s32[40]{0:T(128)}, u32[]{:S(2)}) copy-start(s32[40]{0:T(128)} %param.15) | copy-start | bytes 484
  8.0 37.5 %copy-start.1 = (bf16[40,128,128]{2,1,0:T(8,128)(2,1)S(1)}, bf16[40,128,128]{2,1,0:T(8,128)(2,1)}, u32[]{:S(2)}) copy-start(bf16[40,128,128]{2,1,0:T(8,128)(2,1)} %param.13) | copy-start | bytes 3932164
  8.0 33.6 %collective-permute-start = (f32[32,512]{1,0:T(8,128)}, f32[32,512]{1,0:T(8,128)}, u32[]{:S(2)}, u32[]{:S(2)}) collective-permute-start(f32[32,512]{1,0:T(8,128)} %param.12), channel_id=1, source_target_pairs={{0,4},{4,8},{8,12},{12,16},{16,20},{20,24},{24,28},{28,0},{1,5},{5... | collective-permute-start | bytes 196616 | tf_op jit(solution)/shard_map/ppermute | solution.py:20
  11.0 30.6 %collective-permute-start.1 = (f32[32,512]{1,0:T(8,128)}, f32[32,512]{1,0:T(8,128)}, u32[]{:S(2)}, u32[]{:S(2)}) collective-permute-start(f32[32,512]{1,0:T(8,128)} %param.12), channel_id=1, source_target_pairs={{4,0},{8,4},{12,8},{16,12},{20,16},{24,20},{28,24},{0,28},{5,1},{9... | collective-permute-start | bytes 196616 | tf_op jit(solution)/shard_map/ppermute | solution.py:22
  18.6 4.3 %copy-start.6 = (s32[1024]{0:T(1024)}, s32[1024]{0:T(1024)S(1)}, u32[]{:S(2)}) copy-start(s32[1024]{0:T(1024)S(1)} %pad_clamp_fusion.1) | copy-start | bytes 12292
  22.9 9.9 %all-to-all-start = ((f32[1,8,4,16]{3,2,0,1:T(4,128)}), f32[1,8,4,16]{3,2,0,1:T(4,128)S(1)}, u32[]{:S(2)}, u32[]{:S(2)}) async-start(f32[1,8,4,16]{3,2,0,1:T(4,128)} %bitcast), calls=%async_computation | async-start | bytes 32768 | tf_op jit(solution)/shard_map/all_to_all | solution.py:93
  26.3 22.5 %copy-start.8 = (pred[40]{0:T(512)(128)(4,1)}, pred[40]{0:T(512)(128)(4,1)S(1)}, u32[]{:S(2)}) copy-start(pred[40]{0:T(512)(128)(4,1)S(1)} %get-tuple-element.33) | copy-start | bytes 124
  26.4 22.5 %copy-start.7 = (s32[1024]{0:T(1024)}, s32[1024]{0:T(1024)S(1)}, u32[]{:S(2)}) copy-start(s32[1024]{0:T(1024)S(1)} %pad_clamp_fusion) | copy-start | bytes 12292
  33.5 6.9 %all-to-all-start.1 = ((f32[4,1,128]{2,1,0:T(1,128)}), f32[4,1,128]{2,1,0:T(1,128)S(1)}, u32[]{:S(2)}, u32[]{:S(2)}) async-start(f32[4,1,128]{2,1,0:T(1,128)} %reshape.155), calls=%async_computation.1 | async-start | bytes 4096 | tf_op jit(solution)/shard_map/all_to_all | solution.py:92
  36.7 12.2 %copy-start.11 = (f32[40]{0:T(128)}, f32[40]{0:T(128)S(1)}, u32[]{:S(2)}) copy-start(f32[40]{0:T(128)S(1)} %compare_convert_fusion) | copy-start | bytes 484
  41.6 7.2 %copy-start.9 = (s32[40]{0:T(128)S(1)}, s32[40]{0:T(128)}, u32[]{:S(2)}) copy-start(s32[40]{0:T(128)} %param.14) | copy-start | bytes 484
  50.4 7.3 %collective-permute-start.2 = (f32[32,512]{1,0:T(8,128)}, f32[32,512]{1,0:T(8,128)}, u32[]{:S(2)}, u32[]{:S(2)}) collective-permute-start(f32[32,512]{1,0:T(8,128)} %bitcast.83), channel_id=1, source_target_pairs={{0,4},{4,8},{8,12},{12,16},{16,20},{20,24},{24,28},{28,0},{1,5},{5... | collective-permute-start | bytes 196616 | tf_op jit(solution)/shard_map/ppermute | solution.py:20
  50.9 7.6 %collective-permute-start.3 = (f32[32,512]{1,0:T(8,128)}, f32[32,512]{1,0:T(8,128)}, u32[]{:S(2)}, u32[]{:S(2)}) collective-permute-start(f32[32,512]{1,0:T(8,128)} %bitcast.83), channel_id=1, source_target_pairs={{4,0},{8,4},{12,8},{16,12},{20,16},{24,20},{28,24},{0,28},{5,1},{9... | collective-permute-start | bytes 196616 | tf_op jit(solution)/shard_map/ppermute | solution.py:22
  61.6 6.6 %copy-start.5 = (f32[32,512]{1,0:T(8,128)S(1)}, f32[32,512]{1,0:T(8,128)}, u32[]{:S(2)}) copy-start(f32[32,512]{1,0:T(8,128)} %param.12) | copy-start | bytes 196612
  64.1 3.3 %copy-start.12 = (f32[40]{0:T(128)S(1)}, f32[40]{0:T(128)}, u32[]{:S(2)}) copy-start(f32[40]{0:T(128)} %copy-done.11) | copy-start | bytes 484
  69.6 25.0 %copy-start.3 = (bf16[128,1024]{1,0:T(8,128)(2,1)S(1)}, bf16[128,1024]{1,0:T(8,128)(2,1)}, u32[]{:S(2)}) copy-start(bf16[128,1024]{1,0:T(8,128)(2,1)} %param.18) | copy-start | bytes 786436
  71.3 12.0 %all-to-all-start.2 = ((f32[8,1,2048]{2,1,0:T(1,128)}), f32[8,1,2048]{2,1,0:T(1,128)S(1)}, u32[]{:S(2)}, u32[]{:S(2)}) async-start(f32[8,1,2048]{2,1,0:T(1,128)} %reshape.157), calls=%async_computation.2 | async-start | bytes 131072 | tf_op jit(solution)/shard_map/all_to_all | solution.py:86
  85.0 7.4 %all-to-all-start.3 = ((f32[4,1,4096]{2,1,0:T(1,128)}), f32[4,1,4096]{2,1,0:T(1,128)S(1)}, u32[]{:S(2)}, u32[]{:S(2)}) async-start(f32[4,1,4096]{2,1,0:T(1,128)} %reshape.159), calls=%async_computation.3 | async-start | bytes 131072 | tf_op jit(solution)/shard_map/all_to_all | solution.py:85
  88.3 101.0 %reduce-scatter.2.cloned.1.call-start = ((), (), s32[]{:S(2)}) async-start(), calls=%async_computation.5 | async-start | bytes 4718592 | tf_op jit(solution)/shard_map/reduce_scatter | solution.py:115
  98.9 158.6 %all-reduce.6.cloned.1.call-start = ((), (), s32[]{:S(2)}) async-start(), calls=%async_computation.7 | async-start | bytes 2490368 | tf_op jit(solution)/shard_map/psum | solution.py:122
  102.0 191.0 %all-reduce.4.cloned.1.call-start = ((), (), s32[]{:S(2)}) async-start(), calls=%async_computation.6 | async-start | bytes 1048576 | tf_op jit(solution)/shard_map/psum | solution.py:121
  257.5 39.3 %copy-start.2 = (f32[172,1024]{1,0:T(8,128)S(1)}, f32[172,1024]{1,0:T(8,128)}, u32[]{:S(2)}) copy-start(f32[172,1024]{1,0:T(8,128)} %get-tuple-element.40) | copy-start | bytes 2113540
  (3 other events, 5.3 us)
Sparse Core Ops, SparseCore 0:
  99.0 90.3 reduce-scatter.1
Sparse Core Ops, SparseCore 1:
  105.4 152.0 all-reduce.5
  259.9 33.1 all-reduce.3
where the time goes:
time: 306 us; the launch traced here: 305 us
  waiting for transfers between devices  212 us (69%)
  starting transfers between devices  25.9 us (8%)
  local copies, waits for them, and re-layouts  25.3 us (8%)
  between operations  16.5 us (5%)
  matrix products  14.9 us (5%)
  other arithmetic  10 us (3%)
    reduce_scatter x1, waiting for transfers between devices, shards(): lax.psum_scatter(lax.dot_general(hidden_one, delta_two, LEADING, preferre...  87.3 us
    psum x1, waiting for transfers between devices, shards(): grad_in, grad_out = lax.psum((grad_in, grad_out), ('dom', 'rep'))  67.4 us
    psum x1, waiting for transfers between devices, shards(): grad_mid = lax.psum(mid_shard, 'rep')  35.5 us
    unnamed x44, local copies, waits for them, and re-layouts  9.16 us
    ppermute x2, starting transfers between devices, extended_2(): lax.ppermute(head, axis, [((i + 1) % count, i) for i in range(count)])  7.31 us
    all_to_all x1, waiting for transfers between devices, shards(): lax.all_to_all(moved_rows, 'dom', split_axis=1, concat_axis=1, tiled=True)  6.82 us
    dot_general x2, matrix products, apply_operator(): jnp.einsum('lkz,glz->glk', tiles_across, input_values, precision=lax.Prec...  6.55 us
  transfers between devices with their start and end apart: 11, of which 8 were waited for; matrix products, arithmetic and copies ran while one was open for 5% of the time, Pallas kernels for 0%

commit v1 on v0

--- a/solution.py
+++ b/solution.py
@@ -1,6 +1,10 @@
+import functools
+
 import jax
 import jax.numpy as jnp
 from jax import lax
+from jax.experimental import pallas as pl
+from jax.experimental.pallas import tpu as pltpu
 from jax.sharding import PartitionSpec as P
 
 series_zero = 0.3085083
@@ -8,6 +12,350 @@
 series_two = 0.1864784
 LEADING = (((0,), (0,)), ((), ()))
 TRAILING = (((1,), (1,)), ((), ()))
+AXES = ("dom", "rep")
+F32 = jnp.float32
+BF16 = jnp.bfloat16
+VMEM = pl.BlockSpec(memory_space=pltpu.VMEM)
+SMEM = pl.BlockSpec(memory_space=pltpu.SMEM)
+
+
+def pieces(value):
+    high = value.astype(BF16)
+    rest = value - high.astype(F32)
+    middle = rest.astype(BF16)
+    low = (rest - middle.astype(F32)).astype(BF16)
+    return jnp.concatenate([high, middle, low], axis=0)
+
+
+def whole(parts):
+    rows = parts.shape[0] // 3
+    return parts[:rows] + parts[rows : 2 * rows] + parts[2 * rows :]
+
+
+def prepare_kernel(segment, block, place, slots, cot, packed, rank_row):
+    nodes = slots.shape[1]
+    half = nodes // 2
+    row = slots[...]
+    lane = lax.broadcasted_iota(jnp.int32, (nodes, nodes), 1)
+    sublane = lax.broadcasted_iota(jnp.int32, (nodes, nodes), 0)
+    wide = jnp.broadcast_to(row, (nodes, nodes))
+    column = jnp.sum(jnp.where(lane == sublane, wide, 0), axis=1, keepdims=True)
+
+    def position(slot, order):
+        target = slot // block
+        return (target % 2) * half + (target // 2) * segment + order - target * segment
+
+    below_row = jnp.sum((column < wide).astype(jnp.int32), axis=0, keepdims=True)
+    below_column = jnp.sum((wide < column).astype(jnp.int32), axis=1, keepdims=True)
+    rank_row[...] = position(row, below_row)
+    rank_column = position(column, below_column)
+    placed = jnp.where(rank_column == lane, column, 0)
+    ordered = jnp.sum(placed, axis=0, keepdims=True).astype(F32)
+    core = place[1] % 2
+    mine = jnp.where(core == 0, ordered[:, :half], ordered[:, half:])
+    classes, width = cot.shape
+    packed[0:classes, :] = cot[...].astype(F32)
+    extra = packed.shape[0] - classes
+    rows = half // width
+    for index in range(rows):
+        packed[classes + index : classes + index + 1, :] = mine[:, index * width : (index + 1) * width]
+    if extra > rows:
+        packed[classes + rows :, :] = jnp.zeros((extra - rows, width), F32)
+
+
+def operate(place, tile_row, tile_col, tile_count, own, near, far, tiles, field, owners):
+    capacity, size, _ = tiles.shape
+    count = own.shape[1] // size
+    dom = place[0]
+    odd = dom % 2
+    near_base = (1 - odd) * 2 * count
+    far_base = odd * 2 * count
+    for index in range(count):
+        cut = slice(index * size, (index + 1) * size)
+        field[count + index] = pieces(own[:, cut])
+        field[near_base + index] = pieces(near[:, cut])
+        field[far_base + index] = pieces(far[:, cut])
+    total = count * owners
+    live = tile_count[0]
+    sums = [jnp.zeros((own.shape[0], size), F32) for _ in range(count)]
+    for slot in range(capacity):
+        relative = lax.rem(tile_col[slot] - dom * count + count + total, total)
+        target = jnp.where(slot < live, tile_row[slot], -1)
+        product = whole(
+            lax.dot_general(field[relative], tiles[slot], TRAILING, preferred_element_type=F32)
+        )
+        for index in range(count):
+            sums[index] = sums[index] + jnp.where(target == index, product, 0.0)
+    return jnp.concatenate(sums, axis=1)
+
+
+def first_kernel(owners, place, row, col, live, own, near, far, tiles, first, field):
+    first[...] = operate(place, row, col, live, own, near, far, tiles, field, owners)
+
+
+def second_kernel(
+    owners, place, row, col, live, own, near, far, tiles, features, rank_row, mine, other, field
+):
+    applied = operate(place, row, col, live, own, near, far, tiles, field, owners)
+    base = features[...]
+    second = 2.0 * applied - base
+    diffused = series_zero * base + series_one * own[...] + series_two * second
+    nodes = base.shape[1]
+    spot = lax.broadcasted_iota(jnp.int32, (nodes, nodes), 0)
+    chosen = jnp.where(spot == rank_row[...], 1.0, 0.0).astype(BF16)
+    ordered = whole(lax.dot_general(pieces(diffused), chosen, TRAILING, preferred_element_type=F32))
+    low, high = ordered[:, : nodes // 2], ordered[:, nodes // 2 :]
+    core = place[1] % 2
+    mine[...] = jnp.where(core == 0, low, high)
+    other[...] = jnp.where(core == 0, high, low)
+
+
+def cotangent_kernel(orders, classes, segment, place, *refs):
+    sources = refs[: len(orders)]
+    arranged, slot_rows, held, listed = refs[len(orders) :]
+    me = place[0] * 2 + place[1] // 2
+    core = place[1] % 2
+    blocks = held.shape[0]
+    width = held.shape[2]
+    parts = arranged.shape[0]
+    rows = listed.shape[1]
+    for source, order in zip(sources, orders):
+        for index, mask in enumerate(order):
+            block = jnp.bitwise_xor(me, mask)
+            held[block] = source[index, 0:classes, :].astype(BF16)
+            listed[block] = source[index, classes : classes + rows, :]
+    lists = []
+    for part in range(parts):
+        listing = listed[2 * part]
+        row = jnp.concatenate([listing[i : i + 1] for i in range(rows)], axis=1)
+        slot_rows[part] = row
+        lists.append(row)
+    columns = jnp.concatenate(lists, axis=0).T
+    lane = lax.broadcasted_iota(jnp.int32, (segment, width), 1).astype(F32)
+    for block in range(blocks):
+        start = ((2 * block + core) * width).astype(F32)
+        cut = slice(block * segment, (block + 1) * segment)
+        chosen = jnp.concatenate(
+            [
+                jnp.where(columns[cut, part : part + 1] - start == lane, 1.0, 0.0)
+                for part in range(parts)
+            ],
+            axis=0,
+        ).astype(BF16)
+        moved = lax.dot_general(chosen, held[block], TRAILING, preferred_element_type=F32)
+        for part in range(parts):
+            arranged[part, cut, :] = moved[part * segment : (part + 1) * segment].astype(BF16)
+
+
+def train_kernel(counts, masks, again, place, *refs):
+    sources = refs[: len(counts)]
+    refs = refs[len(counts) :]
+    arranged, slot_rows, w_in, w_mid, w_out = refs[:5]
+    refs = refs[5:]
+    if again:
+        grads_before, batch_before = refs[:2]
+        refs = refs[2:]
+    grads, batch, held = refs
+    feats = w_in.shape[0]
+    classes = w_out.shape[0]
+    mid_rows = grads.shape[0] - feats - arranged.shape[2]
+    if again:
+        grads[...] = grads_before[...]
+        batch[...] = batch_before[...]
+    else:
+        grads[...] = jnp.zeros_like(grads)
+        batch[...] = jnp.zeros_like(batch)
+    slot = 0
+    for source, count in zip(sources, counts):
+        for index in range(count):
+            held[slot] = source[index]
+            slot += 1
+    dom, rep = place[0], place[1]
+    replicas = held.shape[1]
+    width = batch.shape[1]
+    own_start = (dom * replicas + rep) * width
+
+    def one_part(step, carry):
+        mask = jnp.int32(masks[0])
+        for index in range(1, len(masks)):
+            mask = jnp.where(step == index, masks[index], mask)
+        part = jnp.bitwise_xor(dom, mask)
+        value = jnp.concatenate(
+            [held[step, jnp.bitwise_xor(rep, index)] for index in range(replicas)], axis=0
+        )
+        spot = lax.broadcasted_iota(jnp.int32, (width, value.shape[1]), 0) + own_start
+        chosen = jnp.where(spot.astype(F32) == slot_rows[part], 1.0, 0.0).astype(BF16)
+        batch[...] += whole(
+            lax.dot_general(pieces(value), chosen, TRAILING, preferred_element_type=F32)
+        )
+        inputs = value.astype(BF16)
+        cot = arranged[part]
+        pre_one = lax.dot_general(inputs, w_in[...], LEADING, preferred_element_type=F32)
+        gate_one = 0.5 * jnp.tanh(0.5 * pre_one) + 0.5
+        act_one = pre_one * gate_one
+        hidden_one = act_one.astype(BF16)
+        slope_one = gate_one + act_one * (1.0 - gate_one)
+        pre_two = jnp.dot(hidden_one, w_mid[...], preferred_element_type=F32)
+        gate_two = 0.5 * jnp.tanh(0.5 * pre_two) + 0.5
+        act_two = pre_two * gate_two
+        hidden_two = act_two.astype(BF16)
+        slope_two = gate_two + act_two * (1.0 - gate_two)
+        grads[feats + mid_rows :, :] += lax.dot_general(
+            cot, hidden_two, LEADING, preferred_element_type=F32
+        )
+        back_two = jnp.dot(cot, w_out[...], preferred_element_type=F32)
+        delta_two = (back_two * slope_two).astype(BF16)
+        own_pre = lax.dot_general(
+            inputs,
+            w_in[:, pl.ds(pl.multiple_of(dom * mid_rows, mid_rows), mid_rows)],
+            LEADING,
+            preferred_element_type=F32,
+        )
+        own_hidden = (own_pre * (0.5 * jnp.tanh(0.5 * own_pre) + 0.5)).astype(BF16)
+        grads[feats : feats + mid_rows, :] += lax.dot_general(
+            own_hidden, delta_two, LEADING, preferred_element_type=F32
+        )
+        back_one = lax.dot_general(delta_two, w_mid[...], TRAILING, preferred_element_type=F32)
+        delta_one = (back_one * slope_one).astype(BF16)
+        grads[0:feats, :] += jnp.dot(inputs, delta_one, preferred_element_type=F32)
+        return carry
+
+    lax.fori_loop(0, len(masks), one_part, 0)
+
+
+def add_kernel(mine, theirs, grad_in, grad_mid, grad_out):
+    start = 0
+    for out in (grad_in, grad_mid, grad_out):
+        rows = out.shape[0]
+        out[...] = mine[start : start + rows, :] + theirs[start : start + rows, :]
+        start += rows
+
+
+def call(kernel, outs, scalars, arrays, scratch=(), cost=None, aliases=None):
+    return pl.pallas_call(
+        kernel,
+        out_shape=outs,
+        in_specs=[SMEM] * len(scalars) + [VMEM] * len(arrays),
+        out_specs=jax.tree.map(lambda _: VMEM, outs),
+        scratch_shapes=list(scratch),
+        compiler_params=pltpu.CompilerParams(vmem_limit_bytes=48 * 2**20),
+        cost_estimate=cost,
+        input_output_aliases=aliases or {},
+    )(*scalars, *arrays)
+
+
+def exchanged(value, mask, devices):
+    return lax.ppermute(value, AXES, [(i, i ^ mask) for i in range(devices)])
+
+
+def gathered_plan(
+    features, tiles, tile_row, tile_col, tile_count, dest_slot, w_in, w_mid, w_out, cotangent
+):
+    owners, replicas = lax.axis_size("dom"), lax.axis_size("rep")
+    devices = owners * replicas
+    place = jnp.stack([lax.axis_index("dom"), lax.axis_index("rep")]).astype(jnp.int32)
+    feature_count, node_count = features.shape
+    size = tiles.shape[1]
+    classes, width = cotangent.shape
+    hidden = w_in.shape[1]
+    segment = node_count // devices
+    half = node_count // 2
+    count = node_count // size
+    send = functools.partial(exchanged, devices=devices)
+    far_pairs = [
+        (d * replicas + r, ((d + 1 if d % 2 else d - 1) % owners) * replicas + r)
+        for d in range(owners)
+        for r in range(replicas)
+    ]
+
+    def far(value):
+        return lax.ppermute(value, AXES, far_pairs)
+
+    rows = half // width
+    padded = classes + rows + (-(classes + rows)) % 8
+    near_one, far_one = send(features, replicas), far(features)
+    packed, rank_row = call(
+        functools.partial(prepare_kernel, segment, width),
+        (
+            jax.ShapeDtypeStruct((padded, width), F32),
+            jax.ShapeDtypeStruct((1, node_count), jnp.int32),
+        ),
+        [place],
+        [dest_slot.reshape(1, -1), cotangent],
+    )
+    field = pltpu.VMEM((3 * count, 3 * feature_count, size), BF16)
+    scalars = [place, tile_row, tile_col, tile_count]
+    first = call(
+        functools.partial(first_kernel, owners),
+        jax.ShapeDtypeStruct(features.shape, F32),
+        scalars,
+        [features, near_one, far_one, tiles],
+        [field],
+    )
+    line = [packed] + [send(packed, m) for m in (8, 16, 24)]
+    column = jnp.stack(line)
+    near_two, far_two = send(first, replicas), far(first)
+    across_x, across_y = send(column, 4), send(column, 2)
+    corner_one, corner_two = send(across_y[0:2], 4), send(across_x[2:4], 2)
+    mine, other = call(
+        functools.partial(second_kernel, owners),
+        tuple(jax.ShapeDtypeStruct((feature_count, half), F32) for _ in range(2)),
+        scalars,
+        [first, near_two, far_two, tiles, features, rank_row],
+        [field],
+    )
+    own = jnp.stack([mine, send(other, 1), send(mine, 2), send(other, 3)])
+    parts = {0: own[None]}
+    parts[1] = send(own, 4)[None]
+    ring = [send(own, m) for m in (8, 16, 24)]
+    last = send(jnp.stack(ring), 4)
+    orders = ((0, 4, 8, 12), (2, 6, 10, 14), (1, 5, 9, 13), (3, 7), (11, 15))
+    arranged, slot_rows = call(
+        functools.partial(cotangent_kernel, orders, classes, segment),
+        (
+            jax.ShapeDtypeStruct((owners, half, classes), BF16),
+            jax.ShapeDtypeStruct((owners, 1, half), F32),
+        ),
+        [place],
+        [column, across_x, across_y, corner_one, corner_two],
+        [
+            pltpu.VMEM((devices // 2, classes, width), BF16),
+            pltpu.VMEM((devices // 2, rows, width), F32),
+        ],
+    )
+    mid_rows = hidden // owners
+    total_rows = feature_count * replicas + mid_rows + classes
+
+    def train(sources, masks, before=()):
+        counts = tuple(s.shape[0] for s in sources)
+        inputs = [*sources, arranged, slot_rows, w_in, w_mid, w_out, *before]
+        return call(
+            functools.partial(train_kernel, counts, masks, bool(before)),
+            (
+                jax.ShapeDtypeStruct((total_rows, hidden), F32),
+                jax.ShapeDtypeStruct((feature_count * replicas, width), F32),
+            ),
+            [place],
+            inputs,
+            [pltpu.VMEM((len(masks), replicas, feature_count, half), F32)],
+            pl.CostEstimate(
+                flops=5_800_000 * half * len(masks), bytes_accessed=8 * 2**20, transcendentals=0
+            ),
+        )
+
+    state = train([parts[0], parts[1]], (0, 1))
+    state = train([r[None] for r in ring], (2, 4, 6), state)
+    grads, batch_features = train([last], (3, 5, 7), state)
+    grad_in, grad_mid, grad_out = call(
+        add_kernel,
+        tuple(
+            jax.ShapeDtypeStruct((n, hidden), F32)
+            for n in (feature_count * replicas, mid_rows, classes)
+        ),
+        [],
+        [grads, send(grads, 1)],
+    )
+    return batch_features, grad_in, grad_mid, grad_out
 
 
 def extended_2(cells, sides, width):
@@ -51,7 +399,7 @@
     return final_result.reshape(feature_count, node_count)
 
 
-def shards(
+def split_plan(
     features, tiles, tile_row, tile_col, tile_count, dest_slot, w_in, w_mid, w_out, cotangent
 ):
     node_partition = lax.axis_index("dom")
@@ -124,6 +472,8 @@
 
 
 def solution(mesh):
+    compact = mesh.shape["dom"] == 8 and mesh.shape["rep"] == 4
+    shards = gathered_plan if compact else split_plan
     in_specs = (
         P("rep", "dom"),
         P("dom", None, None),

time: 306 us -> 84.5 us (0.28)
  waiting for transfers between devices: 212 us -> 19.5 us
  Pallas kernels: 0 us -> 30.3 us
  local copies, waits for them, and re-layouts: 25.3 us -> 4.98 us
  between operations: 16.5 us -> 1.49 us
  matrix products: 14.9 us -> 0 us
  other arithmetic: 10 us -> 0.14 us
    psum x2 -> x0, waiting for transfers between devices: 103 us -> none  [the longest x1 67.4 us: shards(): grad_in, grad_out = lax.psum((grad_in, grad_out), ('dom', 'rep'))]
    reduce_scatter x1 -> x0, waiting for transfers between devices: 87.3 us -> none  [shards(): lax.psum_scatter(lax.dot_general(hidden_one, delta_two, LEADING, preferre...]
    pallas_call x0 -> x8, Pallas kernels: none -> 30.3 us  [call(): pl.pallas_call(kernel, out_shape=outs, in_specs=[SMEM] * len(scalars) + [...]
    all_to_all x4 -> x0, waiting for transfers between devices: 19.6 us -> none  [the longest x1 6.82 us: shards(): lax.all_to_all(moved_rows, 'dom', split_axis=1, concat_axis=1, tiled=True)]
    ppermute x4 -> x20, waiting for transfers between devices: 2.56 us -> 19.5 us  [the longest x18 16.8 us: exchanged(): return lax.ppermute(value, AXES, [(i, i ^ mask) for i in range(devices)])]
    ppermute x4 -> x20, starting transfers between devices: 10.8 us -> 27.7 us  [the longest x18 21.4 us: exchanged(): return lax.ppermute(value, AXES, [(i, i ^ mask) for i in range(devices)])]
    all_to_all x4 -> x0, starting transfers between devices: 15 us -> none  [the longest x1 5.12 us: shards(): lax.all_to_all(moved_rows, 'dom', split_axis=1, concat_axis=1, tiled=True)]
    dot_general x10 -> x0, matrix products: 14.9 us -> none  [the longest x2 6.55 us: apply_operator(): jnp.einsum('lkz,glz->glk', tiles_across, input_values, precision=lax.Prec...]
  transfers between devices with their start and end apart: 11 -> 20, of which waited for: 8 -> 7; matrix products, arithmetic and copies ran while one was open for 5% -> 0% of each run, Pallas kernels for 0% -> 22%
where the time goes in v1:
time: 84.5 us; the launch traced here: 84.2 us
  Pallas kernels  30.3 us (36%)
  starting transfers between devices  27.7 us (33%)
  waiting for transfers between devices  19.5 us (23%)
  local copies, waits for them, and re-layouts  4.98 us (6%)
  between operations  1.49 us (2%)
    pallas_call x8, Pallas kernels, call(): pl.pallas_call(kernel, out_shape=outs, in_specs=[SMEM] * len(scalars) + [...  30.3 us
    ppermute x18, starting transfers between devices, exchanged(): return lax.ppermute(value, AXES, [(i, i ^ mask) for i in range(devices)])  21.4 us
    ppermute x18, waiting for transfers between devices, exchanged(): return lax.ppermute(value, AXES, [(i, i ^ mask) for i in range(devices)])  16.8 us
    ppermute x2, starting transfers between devices, far(): return lax.ppermute(value, AXES, far_pairs)  6.29 us
    unnamed x20, local copies, waits for them, and re-layouts  4.95 us
    ppermute x2, waiting for transfers between devices, far(): return lax.ppermute(value, AXES, far_pairs)  2.78 us
  transfers between devices with their start and end apart: 20, of which 7 were waited for; matrix products, arithmetic and copies ran while one was open for 0% of the time, Pallas kernels for 22%

profile of v1, /device:TPU:0, one launch (start us, length us, event | category | flops | bytes accessed | tf_op | source)
XLA Modules:
  0.0 84.2 jit_solution(16410680905986446804)
XLA Ops:
  2.2 1.5 %shard_map.130 = (f32[176,128]{1,0:T(8,128)S(1)}, s32[1,512]{1,0:T(1,128)S(1)}) custom-call(s32[2]{0:T(128)S(1)} %pad_add_fusion.place, s32[1,512]{1,0:T(1,128)S(1)} %bitcast.25, bf16[172,128]{1,0:T(8,128)(2,1)S(1)} %copy-done.3), custom_call_target="tpu_custom_call" | custom-call | tf_op jit(solution)/shard_map/pallas_call | solution.py:235
  3.6 3.1 %collective-permute-start.11 = (f32[176,128]{1,0:T(8,128)S(1)}, f32[176,128]{1,0:T(8,128)S(1)}, u32[]{:S(2)}, u32[]{:S(2)}) collective-permute-start(f32[176,128]{1,0:T(8,128)S(1)} %get-tuple-element.22), channel_id=1, source_target_pairs={{0,8},{1,9},{2,10},{3,11},{4,12},{5,13},{6,14},{7,15},{8,0},{9,1},... | collective-permute-start | bytes 270344 | tf_op jit(solution)/shard_map/ppermute | solution.py:248
  6.7 2.6 %collective-permute-start.12 = (f32[176,128]{1,0:T(8,128)S(1)}, f32[176,128]{1,0:T(8,128)S(1)}, u32[]{:S(2)}, u32[]{:S(2)}) collective-permute-start(f32[176,128]{1,0:T(8,128)S(1)} %get-tuple-element.22), channel_id=1, source_target_pairs={{0,16},{1,17},{2,18},{3,19},{4,20},{5,21},{6,22},{7,23},{8,24},{9,... | collective-permute-start | bytes 270344 | tf_op jit(solution)/shard_map/ppermute | solution.py:248
  9.3 1.7 %collective-permute-start = (f32[32,512]{1,0:T(8,128)}, f32[32,512]{1,0:T(8,128)S(1)}, u32[]{:S(2)}, u32[]{:S(2)}) collective-permute-start(f32[32,512]{1,0:T(8,128)} %features.1), channel_id=1, source_target_pairs={{0,4},{1,5},{2,6},{3,7},{4,0},{5,1},{6,2},{7,3},{8,12},{9,13},{10,... | collective-permute-start | bytes 196616 | tf_op jit(solution)/shard_map/ppermute | solution.py:248
  11.0 3.6 %collective-permute-start.1 = (f32[32,512]{1,0:T(8,128)}, f32[32,512]{1,0:T(8,128)S(1)}, u32[]{:S(2)}, u32[]{:S(2)}) collective-permute-start(f32[32,512]{1,0:T(8,128)} %features.1), channel_id=1, source_target_pairs={{0,28},{1,29},{2,30},{3,31},{4,8},{5,9},{6,10},{7,11},{8,4},{9,5},... | collective-permute-start | bytes 196616 | tf_op jit(solution)/shard_map/ppermute | solution.py:272
  14.6 2.0 %collective-permute-done.12 = f32[176,128]{1,0:T(8,128)S(1)} collective-permute-done((f32[176,128]{1,0:T(8,128)S(1)}, f32[176,128]{1,0:T(8,128)S(1)}, u32[]{:S(2)}, u32[]{:S(2)}) %collective-permute-start.12) | collective-permute-done | bytes 90144 | tf_op jit(solution)/shard_map/ppermute | solution.py:248
  16.7 1.6 %collective-permute-start.15 = (f32[4,176,128]{2,1,0:T(8,128)S(1)}, f32[4,176,128]{2,1,0:T(8,128)S(1)}, u32[]{:S(2)}, u32[]{:S(2)}) collective-permute-start(f32[4,176,128]{2,1,0:T(8,128)S(1)} %pad_maximum_fusion.1.refs_0_), channel_id=1, source_target_pairs={{0,2},{1,3},{2,0},{3,1},{4,6},{5,7},{6,4},{7,5},{8,10},{9,11},{10,... | collective-permute-start | bytes 1081352 | tf_op jit(solution)/shard_map/ppermute | solution.py:248
  18.2 2.8 %collective-permute-start.14 = (f32[4,176,128]{2,1,0:T(8,128)S(1)}, f32[4,176,128]{2,1,0:T(8,128)S(1)}, u32[]{:S(2)}, u32[]{:S(2)}) collective-permute-start(f32[4,176,128]{2,1,0:T(8,128)S(1)} %pad_maximum_fusion.1.refs_0_), channel_id=1, source_target_pairs={{0,4},{1,5},{2,6},{3,7},{4,0},{5,1},{6,2},{7,3},{8,12},{9,13},{10,... | collective-permute-start | bytes 1081352 | tf_op jit(solution)/shard_map/ppermute | solution.py:248
  21.7 1.3 %copy-done = bf16[40,128,128]{2,1,0:T(8,128)(2,1)S(1)} copy-done((bf16[40,128,128]{2,1,0:T(8,128)(2,1)S(1)}, bf16[40,128,128]{2,1,0:T(8,128)(2,1)}, u32[]{:S(2)}) %copy-start) | copy-done | bytes 1310744
  25.2 1.5 %shard_map.129.own = f32[32,512]{1,0:T(8,128)S(1)} custom-call(s32[2]{0:T(128)S(1)} %pad_add_fusion.place, s32[40]{0:T(128)S(1)} %copy-done.4, s32[40]{0:T(128)S(1)} %copy-done.5, s32[1]{0:T(128)S(6)} %copy.14.live, f32[32,512]{1,0:T(8,128)S(1)} %copy-done.2, f32[32,512]{1,0:T(8,128)S(1)} %collective-permute-done.near, ...), custom_call_target="tpu_custom_call" | custom-call | tf_op jit(solution)/shard_map/pallas_call | solution.py:235
  26.8 2.7 %collective-permute-start.3 = (f32[32,512]{1,0:T(8,128)S(1)}, f32[32,512]{1,0:T(8,128)S(1)}, u32[]{:S(2)}, u32[]{:S(2)}) collective-permute-start(f32[32,512]{1,0:T(8,128)S(1)} %shard_map.129.own), channel_id=1, source_target_pairs={{0,28},{1,29},{2,30},{3,31},{4,8},{5,9},{6,10},{7,11},{8,4},{9,5},... | collective-permute-start | bytes 196616 | tf_op jit(solution)/shard_map/ppermute | solution.py:272
  29.5 1.5 %collective-permute-done.2.near = f32[32,512]{1,0:T(8,128)S(1)} collective-permute-done((f32[32,512]{1,0:T(8,128)S(1)}, f32[32,512]{1,0:T(8,128)S(1)}, u32[]{:S(2)}, u32[]{:S(2)}) %collective-permute-start.2) | collective-permute-done | bytes 65568 | tf_op jit(solution)/shard_map/ppermute | solution.py:248
  31.0 2.8 %collective-permute-done.3.far = f32[32,512]{1,0:T(8,128)S(1)} collective-permute-done((f32[32,512]{1,0:T(8,128)S(1)}, f32[32,512]{1,0:T(8,128)S(1)}, u32[]{:S(2)}, u32[]{:S(2)}) %collective-permute-start.3) | collective-permute-done | bytes 65568 | tf_op jit(solution)/shard_map/ppermute | solution.py:272
  33.8 1.7 %shard_map.131 = (f32[32,256]{1,0:T(8,128)S(1)}, f32[32,256]{1,0:T(8,128)S(1)}) custom-call(s32[2]{0:T(128)S(1)} %pad_add_fusion.place, s32[40]{0:T(128)S(1)} %copy-done.4, s32[40]{0:T(128)S(1)} %copy-done.5, s32[1]{0:T(128)S(6)} %copy.14.live, f32[32,512]{1,0:T(8,128)S(1)} %shard_map.129.own, f32[32,512]{1,0:T(8,128)S(1)} %collective-permute-done.2.near, ...), custom_call_target="tpu_custom_call" | custom-call | tf_op jit(solution)/shard_map/pallas_call | solution.py:235
  37.5 2.4 %collective-permute-done.5 = f32[32,256]{1,0:T(8,128)S(1)} collective-permute-done((f32[32,256]{1,0:T(8,128)S(1)}, f32[32,256]{1,0:T(8,128)S(1)}, u32[]{:S(2)}, u32[]{:S(2)}) %collective-permute-start.5) | collective-permute-done | bytes 32800 | tf_op jit(solution)/shard_map/ppermute | solution.py:248
  41.3 3.1 %collective-permute-start.9 = (f32[4,32,256]{2,1,0:T(8,128)S(1)}, f32[4,32,256]{2,1,0:T(8,128)S(1)}, u32[]{:S(2)}, u32[]{:S(2)}) collective-permute-start(f32[4,32,256]{2,1,0:T(8,128)S(1)} %get-tuple-element.35), channel_id=1, source_target_pairs={{0,24},{1,25},{2,26},{3,27},{4,28},{5,29},{6,30},{7,31},{8,16},{9,... | collective-permute-start | bytes 393224 | tf_op jit(solution)/shard_map/ppermute | solution.py:248
  45.9 2.0 %collective-permute-done.7 = f32[4,32,256]{2,1,0:T(8,128)S(1)} collective-permute-done((f32[4,32,256]{2,1,0:T(8,128)S(1)}, f32[4,32,256]{2,1,0:T(8,128)S(1)}, u32[]{:S(2)}, u32[]{:S(2)}) %collective-permute-start.7) | collective-permute-done | bytes 131104 | tf_op jit(solution)/shard_map/ppermute | solution.py:248
  47.9 5.1 %collective-permute-done.8 = f32[4,32,256]{2,1,0:T(8,128)S(1)} collective-permute-done((f32[4,32,256]{2,1,0:T(8,128)S(1)}, f32[4,32,256]{2,1,0:T(8,128)S(1)}, u32[]{:S(2)}, u32[]{:S(2)}) %collective-permute-start.8) | collective-permute-done | bytes 131104 | tf_op jit(solution)/shard_map/ppermute | solution.py:248
  53.0 1.7 %collective-permute-start.10 = (f32[3,4,32,256]{3,2,1,0:T(8,128)S(1)}, f32[3,4,32,256]{3,2,1,0:T(8,128)S(1)}, u32[]{:S(2)}, u32[]{:S(2)}) collective-permute-start(f32[3,4,32,256]{3,2,1,0:T(8,128)S(1)} %pad_maximum_fusion), channel_id=1, source_target_pairs={{0,4},{1,5},{2,6},{3,7},{4,0},{5,1},{6,2},{7,3},{8,12},{9,13},{10,... | collective-permute-start | bytes 1179656 | tf_op jit(solution)/shard_map/ppermute | solution.py:248
  56.0 5.4 %shard_map.133 = (f32[428,1024]{1,0:T(8,128)S(1)}, f32[128,128]{1,0:T(8,128)S(1)}) custom-call(s32[2]{0:T(128)S(1)} %pad_add_fusion.place, f32[1,4,32,256]{3,2,1,0:T(8,128)S(1)} %get-tuple-element.34.refs_0_, f32[1,4,32,256]{3,2,1,0:T(8,128)S(1)} %bitcast.26, bf16[8,256,172]{2,1,0:T(8,128)(2,1)S(1)} %get-tuple-element.23.refs_2_.refs_3_.refs_1_, ...), custom_call_target="tpu_custom_call" | custom-call | flops 2969600000 | bytes 8388608 | tf_op jit(solution)/shard_map/pallas_call | solution.py:235
  61.4 8.7 %shard_map.134 = (f32[428,1024]{1,0:T(8,128)S(1)}, f32[128,128]{1,0:T(8,128)S(1)}) custom-call(s32[2]{0:T(128)S(1)} %pad_add_fusion.place, f32[1,4,32,256]{3,2,1,0:T(8,128)S(1)} %bitcast.18, f32[1,4,32,256]{3,2,1,0:T(8,128)S(1)} %bitcast.20, f32[1,4,32,256]{3,2,1,0:T(8,128)S(1)} %bitcast.22, ...), custom_call_target="tpu_custom_call" | custom-call | flops 4454400000 | bytes 8388608 | tf_op jit(solution)/shard_map/pallas_call | solution.py:235
  70.1 8.8 %shard_map.135 = (f32[428,1024]{1,0:T(8,128)S(1)}, f32[128,128]{1,0:T(8,128)}) custom-call(s32[2]{0:T(128)S(1)} %pad_add_fusion.place, f32[3,4,32,256]{3,2,1,0:T(8,128)S(1)} %collective-permute-done.10.refs_0_, bf16[8,256,172]{2,1,0:T(8,128)(2,1)S(1)} %get-tuple-element.23.refs_2_.refs_3_.refs_1_, ...), custom_call_target="tpu_custom_call" | custom-call | flops 4454400000 | bytes 8388608 | tf_op jit(solution)/shard_map/pallas_call | solution.py:235
  79.0 3.7 %collective-permute-done.19.theirs = f32[428,1024]{1,0:T(8,128)S(1)} collective-permute-done((f32[428,1024]{1,0:T(8,128)S(1)}, f32[428,1024]{1,0:T(8,128)S(1)}, u32[]{:S(2)}, u32[]{:S(2)}) %collective-permute-start.19) | collective-permute-done | bytes 1753120 | tf_op jit(solution)/shard_map/ppermute | solution.py:248
  82.7 1.5 %shard_map.136 = (f32[128,1024]{1,0:T(8,128)}, f32[128,1024]{1,0:T(8,128)}, f32[172,1024]{1,0:T(8,128)}) custom-call(f32[428,1024]{1,0:T(8,128)S(1)} %get-tuple-element.30.mine, f32[428,1024]{1,0:T(8,128)S(1)} %collective-permute-done.19.theirs), custom_call_target="tpu_custom_call" | custom-call | tf_op jit(solution)/shard_map/pallas_call | solution.py:235
  (50 shorter events, 10.0 us)
Async XLA Ops:
  3.6 11.0 %collective-permute-start.11 = (f32[176,128]{1,0:T(8,128)S(1)}, f32[176,128]{1,0:T(8,128)S(1)}, u32[]{:S(2)}, u32[]{:S(2)}) collective-permute-start(f32[176,128]{1,0:T(8,128)S(1)} %get-tuple-element.22), channel_id=1, source_target_pairs={{0,8},{1,9},{2,10},{3,11},{4,12},{5,13},{6,14},{7,15},{8,0},{9,1},... | collective-permute-start | bytes 270344 | tf_op jit(solution)/shard_map/ppermute | solution.py:248
  6.7 9.9 %collective-permute-start.12 = (f32[176,128]{1,0:T(8,128)S(1)}, f32[176,128]{1,0:T(8,128)S(1)}, u32[]{:S(2)}, u32[]{:S(2)}) collective-permute-start(f32[176,128]{1,0:T(8,128)S(1)} %get-tuple-element.22), channel_id=1, source_target_pairs={{0,16},{1,17},{2,18},{3,19},{4,20},{5,21},{6,22},{7,23},{8,24},{9,... | collective-permute-start | bytes 270344 | tf_op jit(solution)/shard_map/ppermute | solution.py:248
  9.3 7.3 %collective-permute-start.13 = (f32[176,128]{1,0:T(8,128)S(1)}, f32[176,128]{1,0:T(8,128)S(1)}, u32[]{:S(2)}, u32[]{:S(2)}) collective-permute-start(f32[176,128]{1,0:T(8,128)S(1)} %get-tuple-element.22), channel_id=1, source_target_pairs={{0,24},{1,25},{2,26},{3,27},{4,28},{5,29},{6,30},{7,31},{8,16},{9,... | collective-permute-start | bytes 270344 | tf_op jit(solution)/shard_map/ppermute | solution.py:248
  9.3 12.4 %collective-permute-start = (f32[32,512]{1,0:T(8,128)}, f32[32,512]{1,0:T(8,128)S(1)}, u32[]{:S(2)}, u32[]{:S(2)}) collective-permute-start(f32[32,512]{1,0:T(8,128)} %features.1), channel_id=1, source_target_pairs={{0,4},{1,5},{2,6},{3,7},{4,0},{5,1},{6,2},{7,3},{8,12},{9,13},{10,... | collective-permute-start | bytes 196616 | tf_op jit(solution)/shard_map/ppermute | solution.py:248
  11.0 10.7 %collective-permute-start.1 = (f32[32,512]{1,0:T(8,128)}, f32[32,512]{1,0:T(8,128)S(1)}, u32[]{:S(2)}, u32[]{:S(2)}) collective-permute-start(f32[32,512]{1,0:T(8,128)} %features.1), channel_id=1, source_target_pairs={{0,28},{1,29},{2,30},{3,31},{4,8},{5,9},{6,10},{7,11},{8,4},{9,5},... | collective-permute-start | bytes 196616 | tf_op jit(solution)/shard_map/ppermute | solution.py:272
  16.7 27.7 %collective-permute-start.15 = (f32[4,176,128]{2,1,0:T(8,128)S(1)}, f32[4,176,128]{2,1,0:T(8,128)S(1)}, u32[]{:S(2)}, u32[]{:S(2)}) collective-permute-start(f32[4,176,128]{2,1,0:T(8,128)S(1)} %pad_maximum_fusion.1.refs_0_), channel_id=1, source_target_pairs={{0,2},{1,3},{2,0},{3,1},{4,6},{5,7},{6,4},{7,5},{8,10},{9,11},{10,... | collective-permute-start | bytes 1081352 | tf_op jit(solution)/shard_map/ppermute | solution.py:248
  18.2 26.4 %collective-permute-start.14 = (f32[4,176,128]{2,1,0:T(8,128)S(1)}, f32[4,176,128]{2,1,0:T(8,128)S(1)}, u32[]{:S(2)}, u32[]{:S(2)}) collective-permute-start(f32[4,176,128]{2,1,0:T(8,128)S(1)} %pad_maximum_fusion.1.refs_0_), channel_id=1, source_target_pairs={{0,4},{1,5},{2,6},{3,7},{4,0},{5,1},{6,2},{7,3},{8,12},{9,13},{10,... | collective-permute-start | bytes 1081352 | tf_op jit(solution)/shard_map/ppermute | solution.py:248
  25.2 8.6 %copy-start.1 = (bf16[40,128,128]{2,1,0:T(8,128)(2,1)S(1)}, bf16[40,128,128]{2,1,0:T(8,128)(2,1)}, u32[]{:S(2)}) copy-start(bf16[40,128,128]{2,1,0:T(8,128)(2,1)} %tiles.3) | copy-start | bytes 3932164
  26.7 4.3 %collective-permute-start.2 = (f32[32,512]{1,0:T(8,128)S(1)}, f32[32,512]{1,0:T(8,128)S(1)}, u32[]{:S(2)}, u32[]{:S(2)}) collective-permute-start(f32[32,512]{1,0:T(8,128)S(1)} %shard_map.129.own), channel_id=1, source_target_pairs={{0,4},{1,5},{2,6},{3,7},{4,0},{5,1},{6,2},{7,3},{8,12},{9,13},{10,... | collective-permute-start | bytes 196616 | tf_op jit(solution)/shard_map/ppermute | solution.py:248
  26.8 7.0 %collective-permute-start.3 = (f32[32,512]{1,0:T(8,128)S(1)}, f32[32,512]{1,0:T(8,128)S(1)}, u32[]{:S(2)}, u32[]{:S(2)}) collective-permute-start(f32[32,512]{1,0:T(8,128)S(1)} %shard_map.129.own), channel_id=1, source_target_pairs={{0,28},{1,29},{2,30},{3,31},{4,8},{5,9},{6,10},{7,11},{8,4},{9,5},... | collective-permute-start | bytes 196616 | tf_op jit(solution)/shard_map/ppermute | solution.py:272
  35.5 20.5 %copy-start.7 = (bf16[1024,1024]{1,0:T(8,128)(2,1)S(1)}, bf16[1024,1024]{1,0:T(8,128)(2,1)}, u32[]{:S(2)}) copy-start(bf16[1024,1024]{1,0:T(8,128)(2,1)} %refs_4_.3) | copy-start | bytes 6291460
  35.5 20.5 %copy-start.8 = (bf16[172,1024]{1,0:T(8,128)(2,1)S(1)}, bf16[172,1024]{1,0:T(8,128)(2,1)}, u32[]{:S(2)}) copy-start(bf16[172,1024]{1,0:T(8,128)(2,1)} %refs_5_.5) | copy-start | bytes 1056772
  35.6 20.5 %copy-start.9 = (bf16[128,1024]{1,0:T(8,128)(2,1)S(1)}, bf16[128,1024]{1,0:T(8,128)(2,1)}, u32[]{:S(2)}) copy-start(bf16[128,1024]{1,0:T(8,128)(2,1)} %refs_3_.1) | copy-start | bytes 786436
  35.6 1.9 %collective-permute-start.4 = (f32[32,256]{1,0:T(8,128)S(1)}, f32[32,256]{1,0:T(8,128)S(1)}, u32[]{:S(2)}, u32[]{:S(2)}) collective-permute-start(f32[32,256]{1,0:T(8,128)S(1)} %get-tuple-element.21), channel_id=1, source_target_pairs={{0,1},{1,0},{2,3},{3,2},{4,5},{5,4},{6,7},{7,6},{8,9},{9,8},{10,11... | collective-permute-start | bytes 98312 | tf_op jit(solution)/shard_map/ppermute | solution.py:248
  35.6 4.3 %collective-permute-start.5 = (f32[32,256]{1,0:T(8,128)S(1)}, f32[32,256]{1,0:T(8,128)S(1)}, u32[]{:S(2)}, u32[]{:S(2)}) collective-permute-start(f32[32,256]{1,0:T(8,128)S(1)} %get-tuple-element.20), channel_id=1, source_target_pairs={{0,2},{1,3},{2,0},{3,1},{4,6},{5,7},{6,4},{7,5},{8,10},{9,11},{10,... | collective-permute-start | bytes 98312 | tf_op jit(solution)/shard_map/ppermute | solution.py:248
  36.2 3.7 %collective-permute-start.6 = (f32[32,256]{1,0:T(8,128)S(1)}, f32[32,256]{1,0:T(8,128)S(1)}, u32[]{:S(2)}, u32[]{:S(2)}) collective-permute-start(f32[32,256]{1,0:T(8,128)S(1)} %get-tuple-element.21), channel_id=1, source_target_pairs={{0,3},{1,2},{2,1},{3,0},{4,7},{5,6},{6,5},{7,4},{8,11},{9,10},{10,... | collective-permute-start | bytes 98312 | tf_op jit(solution)/shard_map/ppermute | solution.py:248
  39.9 7.9 %collective-permute-start.7 = (f32[4,32,256]{2,1,0:T(8,128)S(1)}, f32[4,32,256]{2,1,0:T(8,128)S(1)}, u32[]{:S(2)}, u32[]{:S(2)}) collective-permute-start(f32[4,32,256]{2,1,0:T(8,128)S(1)} %get-tuple-element.35), channel_id=1, source_target_pairs={{0,8},{1,9},{2,10},{3,11},{4,12},{5,13},{6,14},{7,15},{8,0},{9,1},... | collective-permute-start | bytes 393224 | tf_op jit(solution)/shard_map/ppermute | solution.py:248
  40.0 13.0 %collective-permute-start.8 = (f32[4,32,256]{2,1,0:T(8,128)S(1)}, f32[4,32,256]{2,1,0:T(8,128)S(1)}, u32[]{:S(2)}, u32[]{:S(2)}) collective-permute-start(f32[4,32,256]{2,1,0:T(8,128)S(1)} %get-tuple-element.35), channel_id=1, source_target_pairs={{0,16},{1,17},{2,18},{3,19},{4,20},{5,21},{6,22},{7,23},{8,24},{9,... | collective-permute-start | bytes 393224 | tf_op jit(solution)/shard_map/ppermute | solution.py:248
  41.3 11.7 %collective-permute-start.9 = (f32[4,32,256]{2,1,0:T(8,128)S(1)}, f32[4,32,256]{2,1,0:T(8,128)S(1)}, u32[]{:S(2)}, u32[]{:S(2)}) collective-permute-start(f32[4,32,256]{2,1,0:T(8,128)S(1)} %get-tuple-element.35), channel_id=1, source_target_pairs={{0,24},{1,25},{2,26},{3,27},{4,28},{5,29},{6,30},{7,31},{8,16},{9,... | collective-permute-start | bytes 393224 | tf_op jit(solution)/shard_map/ppermute | solution.py:248
  44.4 10.3 %collective-permute-start.16 = (f32[2,176,128]{2,1,0:T(8,128)S(1)}, f32[2,176,128]{2,1,0:T(8,128)S(1)}, u32[]{:S(2)}, u32[]{:S(2)}) collective-permute-start(f32[2,176,128]{2,1,0:T(8,128)S(1)} %slice.8), channel_id=1, source_target_pairs={{0,4},{1,5},{2,6},{3,7},{4,0},{5,1},{6,2},{7,3},{8,12},{9,13},{10,... | collective-permute-start | bytes 540680 | tf_op jit(solution)/shard_map/ppermute | solution.py:248
  44.7 10.0 %collective-permute-start.17 = (f32[2,176,128]{2,1,0:T(8,128)S(1)}, f32[2,176,128]{2,1,0:T(8,128)S(1)}, u32[]{:S(2)}, u32[]{:S(2)}) collective-permute-start(f32[2,176,128]{2,1,0:T(8,128)S(1)} %slice.9), channel_id=1, source_target_pairs={{0,2},{1,3},{2,0},{3,1},{4,6},{5,7},{6,4},{7,5},{8,10},{9,11},{10,... | collective-permute-start | bytes 540680 | tf_op jit(solution)/shard_map/ppermute | solution.py:248
  47.9 8.1 %collective-permute-start.18 = (f32[4,32,256]{2,1,0:T(8,128)S(1)}, f32[4,32,256]{2,1,0:T(8,128)S(1)}, u32[]{:S(2)}, u32[]{:S(2)}) collective-permute-start(f32[4,32,256]{2,1,0:T(8,128)S(1)} %get-tuple-element.35), channel_id=1, source_target_pairs={{0,4},{1,5},{2,6},{3,7},{4,0},{5,1},{6,2},{7,3},{8,12},{9,13},{10,... | collective-permute-start | bytes 393224 | tf_op jit(solution)/shard_map/ppermute | solution.py:248
  53.0 17.1 %collective-permute-start.10 = (f32[3,4,32,256]{3,2,1,0:T(8,128)S(1)}, f32[3,4,32,256]{3,2,1,0:T(8,128)S(1)}, u32[]{:S(2)}, u32[]{:S(2)}) collective-permute-start(f32[3,4,32,256]{3,2,1,0:T(8,128)S(1)} %pad_maximum_fusion), channel_id=1, source_target_pairs={{0,4},{1,5},{2,6},{3,7},{4,0},{5,1},{6,2},{7,3},{8,12},{9,13},{10,... | collective-permute-start | bytes 1179656 | tf_op jit(solution)/shard_map/ppermute | solution.py:248
  78.9 3.8 %collective-permute-start.19 = (f32[428,1024]{1,0:T(8,128)S(1)}, f32[428,1024]{1,0:T(8,128)S(1)}, u32[]{:S(2)}, u32[]{:S(2)}) collective-permute-start(f32[428,1024]{1,0:T(8,128)S(1)} %get-tuple-element.30.mine), channel_id=1, source_target_pairs={{0,1},{1,0},{2,3},{3,2},{4,5},{5,4},{6,7},{7,6},{8,9},{9,8},{10,11... | collective-permute-start | bytes 5259272 | tf_op jit(solution)/shard_map/ppermute | solution.py:248
  (6 other events, 4.9 us)

commit v2 on v1

--- a/solution.py
+++ b/solution.py
@@ -32,28 +32,27 @@
     return parts[:rows] + parts[rows : 2 * rows] + parts[2 * rows :]
 
 
-def prepare_kernel(segment, block, place, slots, cot, packed, rank_row):
+def prepare_kernel(segment, block, place, slots_hbm, cot_hbm, packed, rank_row, slots, cot, sems):
+    fetch_slots = pltpu.make_async_copy(slots_hbm, slots, sems.at[0])
+    fetch_cot = pltpu.make_async_copy(cot_hbm, cot, sems.at[1])
+    fetch_slots.start()
+    fetch_cot.start()
+    fetch_slots.wait()
     nodes = slots.shape[1]
     half = nodes // 2
-    row = slots[...]
-    lane = lax.broadcasted_iota(jnp.int32, (nodes, nodes), 1)
-    sublane = lax.broadcasted_iota(jnp.int32, (nodes, nodes), 0)
+    row = slots[...].astype(F32)
+    column = jnp.broadcast_to(row, (8, nodes)).T[:, 0:1]
     wide = jnp.broadcast_to(row, (nodes, nodes))
-    column = jnp.sum(jnp.where(lane == sublane, wide, 0), axis=1, keepdims=True)
-
-    def position(slot, order):
-        target = slot // block
-        return (target % 2) * half + (target // 2) * segment + order - target * segment
-
-    below_row = jnp.sum((column < wide).astype(jnp.int32), axis=0, keepdims=True)
-    below_column = jnp.sum((wide < column).astype(jnp.int32), axis=1, keepdims=True)
-    rank_row[...] = position(row, below_row)
-    rank_column = position(column, below_column)
-    placed = jnp.where(rank_column == lane, column, 0)
-    ordered = jnp.sum(placed, axis=0, keepdims=True).astype(F32)
-    core = place[1] % 2
-    mine = jnp.where(core == 0, ordered[:, :half], ordered[:, half:])
+    order = jnp.sum(jnp.where(column < wide, 1.0, 0.0), axis=0, keepdims=True).astype(jnp.int32)
+    target = slots[...] // block
+    rank = (target % 2) * half + (target // 2) * segment + order - target * segment
+    rank_row[...] = rank
+    rank_column = jnp.broadcast_to(rank.astype(F32), (8, nodes)).T[:, 0:1]
+    lane = lax.broadcasted_iota(jnp.int32, (nodes, nodes), 1).astype(F32)
+    ordered = jnp.sum(jnp.where(rank_column == lane, column, 0.0), axis=0, keepdims=True)
+    mine = jnp.where(place[1] % 2 == 0, ordered[:, :half], ordered[:, half:])
     classes, width = cot.shape
+    fetch_cot.wait()
     packed[0:classes, :] = cot[...].astype(F32)
     extra = packed.shape[0] - classes
     rows = half // width
@@ -63,7 +62,7 @@
         packed[classes + rows :, :] = jnp.zeros((extra - rows, width), F32)
 
 
-def operate(place, tile_row, tile_col, tile_count, own, near, far, tiles, field, owners):
+def operate(place, live, row, col, own, near, far, tiles, field, owners):
     capacity, size, _ = tiles.shape
     count = own.shape[1] // size
     dom = place[0]
@@ -76,11 +75,10 @@
         field[near_base + index] = pieces(near[:, cut])
         field[far_base + index] = pieces(far[:, cut])
     total = count * owners
-    live = tile_count[0]
     sums = [jnp.zeros((own.shape[0], size), F32) for _ in range(count)]
     for slot in range(capacity):
-        relative = lax.rem(tile_col[slot] - dom * count + count + total, total)
-        target = jnp.where(slot < live, tile_row[slot], -1)
+        relative = lax.rem(col[slot] - dom * count + count + total, total)
+        target = jnp.where(slot < live[0], row[slot], -1)
         product = whole(
             lax.dot_general(field[relative], tiles[slot], TRAILING, preferred_element_type=F32)
         )
@@ -89,14 +87,14 @@
     return jnp.concatenate(sums, axis=1)
 
 
-def first_kernel(owners, place, row, col, live, own, near, far, tiles, first, field):
-    first[...] = operate(place, row, col, live, own, near, far, tiles, field, owners)
+def first_kernel(owners, place, live, row, col, own, near, far, tiles, first, field):
+    first[...] = operate(place, live, row, col, own, near, far, tiles, field, owners)
 
 
 def second_kernel(
-    owners, place, row, col, live, own, near, far, tiles, features, rank_row, mine, other, field
+    owners, place, live, row, col, own, near, far, tiles, features, rank_row, mine, other, field
 ):
-    applied = operate(place, row, col, live, own, near, far, tiles, field, owners)
+    applied = operate(place, live, row, col, own, near, far, tiles, field, owners)
     base = features[...]
     second = 2.0 * applied - base
     diffused = series_zero * base + series_one * own[...] + series_two * second
@@ -147,80 +145,97 @@
             arranged[part, cut, :] = moved[part * segment : (part + 1) * segment].astype(BF16)
 
 
-def train_kernel(counts, masks, again, place, *refs):
-    sources = refs[: len(counts)]
-    refs = refs[len(counts) :]
-    arranged, slot_rows, w_in, w_mid, w_out = refs[:5]
-    refs = refs[5:]
+def activated(pre):
+    gate = 0.5 * jnp.tanh(0.5 * pre) + 0.5
+    value = pre * gate
+    return value.astype(BF16), gate + value * (1.0 - gate)
+
+
+def feature_rows(source, rep):
+    replicas = source.shape[0]
+    return jnp.concatenate([source[jnp.bitwise_xor(rep, i)] for i in range(replicas)], axis=0)
+
+
+def forward(inputs, dom, mid_rows, w_in, w_mid):
+    pre_one = lax.dot_general(inputs, w_in[...], LEADING, preferred_element_type=F32)
+    hidden_one, slope_one = activated(pre_one)
+    own_pre = lax.dot_general(
+        inputs,
+        w_in[:, pl.ds(pl.multiple_of(dom * mid_rows, mid_rows), mid_rows)],
+        LEADING,
+        preferred_element_type=F32,
+    )
+    own_hidden, _ = activated(own_pre)
+    pre_two = jnp.dot(hidden_one, w_mid[...], preferred_element_type=F32)
+    hidden_two, slope_two = activated(pre_two)
+    return own_hidden, hidden_two, slope_one, slope_two
+
+
+def forward_kernel(mid_rows, place, *refs):
+    *sources, w_in, w_mid, own_hidden, hidden_two, slope_one, slope_two = refs
+    dom, rep = place[0], place[1]
+    values = [feature_rows(source, rep).astype(BF16) for source in sources]
+    results = forward(jnp.concatenate(values, axis=1), dom, mid_rows, w_in, w_mid)
+    for out, result in zip((own_hidden, hidden_two, slope_one, slope_two), results):
+        out[...] = result
+
+
+def train_kernel(fresh, masks, begun, again, place, *refs):
     if again:
         grads_before, batch_before = refs[:2]
         refs = refs[2:]
-    grads, batch, held = refs
+    sources = refs[: len(masks)]
+    refs = refs[len(masks) :]
+    states = refs[:4] if begun else ()
+    arranged, slot_rows, w_in, w_mid, w_out, grads, batch = refs[len(states) :]
     feats = w_in.shape[0]
-    classes = w_out.shape[0]
     mid_rows = grads.shape[0] - feats - arranged.shape[2]
-    if again:
-        grads[...] = grads_before[...]
-        batch[...] = batch_before[...]
-    else:
-        grads[...] = jnp.zeros_like(grads)
-        batch[...] = jnp.zeros_like(batch)
-    slot = 0
-    for source, count in zip(sources, counts):
-        for index in range(count):
-            held[slot] = source[index]
-            slot += 1
     dom, rep = place[0], place[1]
-    replicas = held.shape[1]
     width = batch.shape[1]
+    replicas = sources[0].shape[0]
     own_start = (dom * replicas + rep) * width
-
-    def one_part(step, carry):
-        mask = jnp.int32(masks[0])
-        for index in range(1, len(masks)):
-            mask = jnp.where(step == index, masks[index], mask)
+    values, cots = [], []
+    moved = batch_before[...] if again else jnp.zeros(batch.shape, F32)
+    for source, mask in zip(sources, masks):
         part = jnp.bitwise_xor(dom, mask)
-        value = jnp.concatenate(
-            [held[step, jnp.bitwise_xor(rep, index)] for index in range(replicas)], axis=0
-        )
+        value = feature_rows(source, rep)
         spot = lax.broadcasted_iota(jnp.int32, (width, value.shape[1]), 0) + own_start
         chosen = jnp.where(spot.astype(F32) == slot_rows[part], 1.0, 0.0).astype(BF16)
-        batch[...] += whole(
+        moved = moved + whole(
             lax.dot_general(pieces(value), chosen, TRAILING, preferred_element_type=F32)
         )
-        inputs = value.astype(BF16)
-        cot = arranged[part]
-        pre_one = lax.dot_general(inputs, w_in[...], LEADING, preferred_element_type=F32)
-        gate_one = 0.5 * jnp.tanh(0.5 * pre_one) + 0.5
-        act_one = pre_one * gate_one
-        hidden_one = act_one.astype(BF16)
-        slope_one = gate_one + act_one * (1.0 - gate_one)
-        pre_two = jnp.dot(hidden_one, w_mid[...], preferred_element_type=F32)
-        gate_two = 0.5 * jnp.tanh(0.5 * pre_two) + 0.5
-        act_two = pre_two * gate_two
-        hidden_two = act_two.astype(BF16)
-        slope_two = gate_two + act_two * (1.0 - gate_two)
-        grads[feats + mid_rows :, :] += lax.dot_general(
-            cot, hidden_two, LEADING, preferred_element_type=F32
-        )
-        back_two = jnp.dot(cot, w_out[...], preferred_element_type=F32)
-        delta_two = (back_two * slope_two).astype(BF16)
-        own_pre = lax.dot_general(
-            inputs,
-            w_in[:, pl.ds(pl.multiple_of(dom * mid_rows, mid_rows), mid_rows)],
-            LEADING,
-            preferred_element_type=F32,
-        )
-        own_hidden = (own_pre * (0.5 * jnp.tanh(0.5 * own_pre) + 0.5)).astype(BF16)
-        grads[feats : feats + mid_rows, :] += lax.dot_general(
-            own_hidden, delta_two, LEADING, preferred_element_type=F32
-        )
-        back_one = lax.dot_general(delta_two, w_mid[...], TRAILING, preferred_element_type=F32)
-        delta_one = (back_one * slope_one).astype(BF16)
-        grads[0:feats, :] += jnp.dot(inputs, delta_one, preferred_element_type=F32)
-        return carry
-
-    lax.fori_loop(0, len(masks), one_part, 0)
+        values.append(value.astype(BF16))
+        cots.append(arranged[part])
+    batch[...] = moved
+    inputs = jnp.concatenate(values, axis=1)
+    cot = jnp.concatenate(cots, axis=0)
+    done = inputs.shape[1] - fresh
+    results = forward(inputs[:, done:], dom, mid_rows, w_in, w_mid)
+    if begun:
+        results = [
+            jnp.concatenate([state[...], result], axis=0) for state, result in zip(states, results)
+        ]
+    own_hidden, hidden_two, slope_one, slope_two = results
+
+    def add(first_row, last_row, term):
+        cut = slice(first_row, last_row)
+        grads[cut, :] = grads_before[cut, :] + term if again else term
+
+    add(
+        feats + mid_rows,
+        grads.shape[0],
+        lax.dot_general(cot, hidden_two, LEADING, preferred_element_type=F32),
+    )
+    back_two = jnp.dot(cot, w_out[...], preferred_element_type=F32)
+    delta_two = (back_two * slope_two).astype(BF16)
+    add(
+        feats,
+        feats + mid_rows,
+        lax.dot_general(own_hidden, delta_two, LEADING, preferred_element_type=F32),
+    )
+    back_one = lax.dot_general(delta_two, w_mid[...], TRAILING, preferred_element_type=F32)
+    delta_one = (back_one * slope_one).astype(BF16)
+    add(0, feats, jnp.dot(inputs, delta_one, preferred_element_type=F32))
 
 
 def add_kernel(mine, theirs, grad_in, grad_mid, grad_out):
@@ -231,16 +246,18 @@
         start += rows
 
 
-def call(kernel, outs, scalars, arrays, scratch=(), cost=None, aliases=None):
+def call(kernel, outs, scalars, arrays, scratch=(), micros=1.5, space=pltpu.VMEM):
+    cost = pl.CostEstimate(
+        flops=int(micros * 1e9), bytes_accessed=int(micros * 3.6e6), transcendentals=0
+    )
     return pl.pallas_call(
         kernel,
         out_shape=outs,
-        in_specs=[SMEM] * len(scalars) + [VMEM] * len(arrays),
+        in_specs=[SMEM] * len(scalars) + [pl.BlockSpec(memory_space=space)] * len(arrays),
         out_specs=jax.tree.map(lambda _: VMEM, outs),
         scratch_shapes=list(scratch),
         compiler_params=pltpu.CompilerParams(vmem_limit_bytes=48 * 2**20),
         cost_estimate=cost,
-        input_output_aliases=aliases or {},
     )(*scalars, *arrays)
 
 
@@ -254,6 +271,7 @@
     owners, replicas = lax.axis_size("dom"), lax.axis_size("rep")
     devices = owners * replicas
     place = jnp.stack([lax.axis_index("dom"), lax.axis_index("rep")]).astype(jnp.int32)
+    scalars = [place, tile_count, tile_row, tile_col]
     feature_count, node_count = features.shape
     size = tiles.shape[1]
     classes, width = cotangent.shape
@@ -282,9 +300,14 @@
         ),
         [place],
         [dest_slot.reshape(1, -1), cotangent],
+        [
+            pltpu.VMEM((1, node_count), jnp.int32),
+            pltpu.VMEM((classes, width), BF16),
+            pltpu.SemaphoreType.DMA((2,)),
+        ],
+        space=pl.ANY,
     )
     field = pltpu.VMEM((3 * count, 3 * feature_count, size), BF16)
-    scalars = [place, tile_row, tile_col, tile_count]
     first = call(
         functools.partial(first_kernel, owners),
         jax.ShapeDtypeStruct(features.shape, F32),
@@ -305,10 +328,8 @@
         [field],
     )
     own = jnp.stack([mine, send(other, 1), send(mine, 2), send(other, 3)])
-    parts = {0: own[None]}
-    parts[1] = send(own, 4)[None]
+    facing = send(own, 4)
     ring = [send(own, m) for m in (8, 16, 24)]
-    last = send(jnp.stack(ring), 4)
     orders = ((0, 4, 8, 12), (2, 6, 10, 14), (1, 5, 9, 13), (3, 7), (11, 15))
     arranged, slot_rows = call(
         functools.partial(cotangent_kernel, orders, classes, segment),
@@ -326,26 +347,37 @@
     mid_rows = hidden // owners
     total_rows = feature_count * replicas + mid_rows + classes
 
-    def train(sources, masks, before=()):
-        counts = tuple(s.shape[0] for s in sources)
-        inputs = [*sources, arranged, slot_rows, w_in, w_mid, w_out, *before]
+    begun = call(
+        functools.partial(forward_kernel, mid_rows),
+        (
+            jax.ShapeDtypeStruct((2 * half, mid_rows), BF16),
+            jax.ShapeDtypeStruct((2 * half, hidden), BF16),
+            jax.ShapeDtypeStruct((2 * half, hidden), F32),
+            jax.ShapeDtypeStruct((2 * half, hidden), F32),
+        ),
+        [place],
+        [own, facing, w_in, w_mid],
+        micros=2.5,
+    )
+    *ring, gate = lax.optimization_barrier((*ring, begun[0]))
+    begun = (gate, *begun[1:])
+    last = send(jnp.stack(ring), 4)
+
+    def train(before, sources, masks, states):
+        fresh = half * (len(masks) - 2 * bool(states))
         return call(
-            functools.partial(train_kernel, counts, masks, bool(before)),
+            functools.partial(train_kernel, fresh, masks, bool(states), bool(before)),
             (
                 jax.ShapeDtypeStruct((total_rows, hidden), F32),
                 jax.ShapeDtypeStruct((feature_count * replicas, width), F32),
             ),
             [place],
-            inputs,
-            [pltpu.VMEM((len(masks), replicas, feature_count, half), F32)],
-            pl.CostEstimate(
-                flops=5_800_000 * half * len(masks), bytes_accessed=8 * 2**20, transcendentals=0
-            ),
+            [*before, *sources, *states, arranged, slot_rows, w_in, w_mid, w_out],
+            micros=2.5 * len(masks),
         )
 
-    state = train([parts[0], parts[1]], (0, 1))
-    state = train([r[None] for r in ring], (2, 4, 6), state)
-    grads, batch_features = train([last], (3, 5, 7), state)
+    state = train((), [own, facing, *ring], (0, 1, 2, 4, 6), begun)
+    grads, batch_features = train(state, [last[0], last[1], last[2]], (3, 5, 7), ())
     grad_in, grad_mid, grad_out = call(
         add_kernel,
         tuple(

time: 84.5 us -> 71.4 us (0.84)
  waiting for transfers between devices: 19.5 us -> 11 us
  local copies, waits for them, and re-layouts: 4.98 us -> 2.9 us
  Pallas kernels: 30.3 us -> 29.1 us
  starting transfers between devices: 27.7 us -> 26.6 us
    ppermute x18, waiting for transfers between devices: 16.8 us -> 9.67 us  [exchanged(): return lax.ppermute(value, AXES, [(i, i ^ mask) for i in range(devices)])]
    ppermute x18, starting transfers between devices: 21.4 us -> 18.5 us  [exchanged(): return lax.ppermute(value, AXES, [(i, i ^ mask) for i in range(devices)])]
    unnamed x20, local copies, waits for them, and re-layouts: 4.95 us -> 2.85 us
    ppermute x2, starting transfers between devices: 6.29 us -> 8.01 us  [far(): return lax.ppermute(value, AXES, far_pairs)]
    ppermute x2, waiting for transfers between devices: 2.78 us -> 1.31 us  [far(): return lax.ppermute(value, AXES, far_pairs)]
    pallas_call x8, Pallas kernels: 30.3 us -> 29.1 us  [call(): pl.pallas_call(kernel, out_shape=outs, in_specs=[SMEM] * len(scalars) + [...]
  transfers between devices with their start and end apart: 20 -> 20, of which waited for: 7 -> 6; matrix products, arithmetic and copies ran while one was open for 0% -> 0% of each run, Pallas kernels for 22% -> 29%
where the time goes in v2:
time: 71.4 us; the launch traced here: 71.1 us
  Pallas kernels  29.1 us (41%)
  starting transfers between devices  26.6 us (37%)
  waiting for transfers between devices  11 us (15%)
  local copies, waits for them, and re-layouts  2.9 us (4%)
  between operations  1.51 us (2%)
    pallas_call x8, Pallas kernels, call(): pl.pallas_call(kernel, out_shape=outs, in_specs=[SMEM] * len(scalars) + [...  29.1 us
    ppermute x18, starting transfers between devices, exchanged(): return lax.ppermute(value, AXES, [(i, i ^ mask) for i in range(devices)])  18.5 us
    ppermute x18, waiting for transfers between devices, exchanged(): return lax.ppermute(value, AXES, [(i, i ^ mask) for i in range(devices)])  9.67 us
    ppermute x2, starting transfers between devices, far(): return lax.ppermute(value, AXES, far_pairs)  8.01 us
    unnamed x20, local copies, waits for them, and re-layouts  2.85 us
  transfers between devices with their start and end apart: 20, of which 6 were waited for; matrix products, arithmetic and copies ran while one was open for 0% of the time, Pallas kernels for 29%

profile of v2, /device:TPU:0, one launch (start us, length us, event | category | flops | bytes accessed | tf_op | source)
XLA Modules:
  0.0 71.1 jit_solution(5427864874901182909)
XLA Ops:
  0.6 6.0 %collective-permute-start.1 = (f32[32,512]{1,0:T(8,128)}, f32[32,512]{1,0:T(8,128)S(1)}, u32[]{:S(2)}, u32[]{:S(2)}) collective-permute-start(f32[32,512]{1,0:T(8,128)} %features.1), channel_id=1, source_target_pairs={{0,28},{1,29},{2,30},{3,31},{4,8},{5,9},{6,10},{7,11},{8,4},{9,5},... | collective-permute-start | bytes 196616 | tf_op jit(solution)/shard_map/ppermute | solution.py:290
  8.2 1.2 %shard_map.130 = (f32[176,128]{1,0:T(8,128)S(1)}, s32[1,512]{1,0:T(1,128)S(1)}) custom-call(s32[2]{0:T(128)S(1)} %pad_add_fusion.place, s32[1,512]{1,0:T(1,128)S(1)} %bitcast.25, bf16[172,128]{1,0:T(8,128)(2,1)S(1)} %copy-done.4), custom_call_target="tpu_custom_call" | custom-call | flops 1500000000 | bytes 5400000 | tf_op jit(solution)/shard_map/pallas_call | solution.py:253
  10.1 0.9 %collective-permute-start.12 = (f32[176,128]{1,0:T(8,128)S(1)}, f32[176,128]{1,0:T(8,128)S(1)}, u32[]{:S(2)}, u32[]{:S(2)}) collective-permute-start(f32[176,128]{1,0:T(8,128)S(1)} %get-tuple-element.36), channel_id=1, source_target_pairs={{0,16},{1,17},{2,18},{3,19},{4,20},{5,21},{6,22},{7,23},{8,24},{9,... | collective-permute-start | bytes 270344 | tf_op jit(solution)/shard_map/ppermute | solution.py:265
  11.0 2.8 %collective-permute-start.11 = (f32[176,128]{1,0:T(8,128)S(1)}, f32[176,128]{1,0:T(8,128)S(1)}, u32[]{:S(2)}, u32[]{:S(2)}) collective-permute-start(f32[176,128]{1,0:T(8,128)S(1)} %get-tuple-element.36), channel_id=1, source_target_pairs={{0,8},{1,9},{2,10},{3,11},{4,12},{5,13},{6,14},{7,15},{8,0},{9,1},... | collective-permute-start | bytes 270344 | tf_op jit(solution)/shard_map/ppermute | solution.py:265
  14.6 1.5 %shard_map.129.own = f32[32,512]{1,0:T(8,128)S(1)} custom-call(s32[2]{0:T(128)S(1)} %pad_add_fusion.place, s32[1]{0:T(128)S(6)} %copy.14.live, s32[40]{0:T(128)S(1)} %copy-done.6, s32[40]{0:T(128)S(1)} %copy-done.7, f32[32,512]{1,0:T(8,128)S(1)} %copy-done.3, f32[32,512]{1,0:T(8,128)S(1)} %collective-permute-done.near, ...), custom_call_target="tpu_custom_call" | custom-call | flops 1500000000 | bytes 5400000 | tf_op jit(solution)/shard_map/pallas_call | solution.py:253
  16.1 2.0 %collective-permute-start.3 = (f32[32,512]{1,0:T(8,128)S(1)}, f32[32,512]{1,0:T(8,128)S(1)}, u32[]{:S(2)}, u32[]{:S(2)}) collective-permute-start(f32[32,512]{1,0:T(8,128)S(1)} %shard_map.129.own), channel_id=1, source_target_pairs={{0,28},{1,29},{2,30},{3,31},{4,8},{5,9},{6,10},{7,11},{8,4},{9,5},... | collective-permute-start | bytes 196616 | tf_op jit(solution)/shard_map/ppermute | solution.py:290
  18.3 1.7 %collective-permute-done.12 = f32[176,128]{1,0:T(8,128)S(1)} collective-permute-done((f32[176,128]{1,0:T(8,128)S(1)}, f32[176,128]{1,0:T(8,128)S(1)}, u32[]{:S(2)}, u32[]{:S(2)}) %collective-permute-start.12) | collective-permute-done | bytes 90144 | tf_op jit(solution)/shard_map/ppermute | solution.py:265
  20.0 1.6 %collective-permute-start.15 = (f32[4,176,128]{2,1,0:T(8,128)S(1)}, f32[4,176,128]{2,1,0:T(8,128)S(1)}, u32[]{:S(2)}, u32[]{:S(2)}) collective-permute-start(f32[4,176,128]{2,1,0:T(8,128)S(1)} %pad_maximum_fusion.1.refs_0_), channel_id=1, source_target_pairs={{0,2},{1,3},{2,0},{3,1},{4,6},{5,7},{6,4},{7,5},{8,10},{9,11},{10,... | collective-permute-start | bytes 1081352 | tf_op jit(solution)/shard_map/ppermute | solution.py:265
  21.9 1.3 %collective-permute-done.3.far = f32[32,512]{1,0:T(8,128)S(1)} collective-permute-done((f32[32,512]{1,0:T(8,128)S(1)}, f32[32,512]{1,0:T(8,128)S(1)}, u32[]{:S(2)}, u32[]{:S(2)}) %collective-permute-start.3) | collective-permute-done | bytes 65568 | tf_op jit(solution)/shard_map/ppermute | solution.py:290
  23.2 1.7 %shard_map.131 = (f32[32,256]{1,0:T(8,128)S(1)}, f32[32,256]{1,0:T(8,128)S(1)}) custom-call(s32[2]{0:T(128)S(1)} %pad_add_fusion.place, s32[1]{0:T(128)S(6)} %copy.14.live, s32[40]{0:T(128)S(1)} %copy-done.6, s32[40]{0:T(128)S(1)} %copy-done.7, f32[32,512]{1,0:T(8,128)S(1)} %shard_map.129.own, f32[32,512]{1,0:T(8,128)S(1)} %collective-permute-done.2.near, ...), custom_call_target="tpu_custom_call" | custom-call | flops 1500000000 | bytes 5400000 | tf_op jit(solution)/shard_map/pallas_call | solution.py:253
  24.9 2.1 %collective-permute-start.5 = (f32[32,256]{1,0:T(8,128)S(1)}, f32[32,256]{1,0:T(8,128)S(1)}, u32[]{:S(2)}, u32[]{:S(2)}) collective-permute-start(f32[32,256]{1,0:T(8,128)S(1)} %get-tuple-element.26), channel_id=1, source_target_pairs={{0,2},{1,3},{2,0},{3,1},{4,6},{5,7},{6,4},{7,5},{8,10},{9,11},{10,... | collective-permute-start | bytes 98312 | tf_op jit(solution)/shard_map/ppermute | solution.py:265
  27.2 2.7 %collective-permute-done.5 = f32[32,256]{1,0:T(8,128)S(1)} collective-permute-done((f32[32,256]{1,0:T(8,128)S(1)}, f32[32,256]{1,0:T(8,128)S(1)}, u32[]{:S(2)}, u32[]{:S(2)}) %collective-permute-start.5) | collective-permute-done | bytes 32800 | tf_op jit(solution)/shard_map/ppermute | solution.py:265
  30.7 3.1 %collective-permute-start.10 = (f32[4,32,256]{2,1,0:T(8,128)S(1)}, f32[4,32,256]{2,1,0:T(8,128)S(1)}, u32[]{:S(2)}, u32[]{:S(2)}) collective-permute-start(f32[4,32,256]{2,1,0:T(8,128)S(1)} %pad_maximum_fusion.2.refs_0_), channel_id=1, source_target_pairs={{0,24},{1,25},{2,26},{3,27},{4,28},{5,29},{6,30},{7,31},{8,16},{9,... | collective-permute-start | bytes 393224 | tf_op jit(solution)/shard_map/ppermute | solution.py:265
  33.8 1.4 %collective-permute-start.8 = (f32[4,32,256]{2,1,0:T(8,128)S(1)}, f32[4,32,256]{2,1,0:T(8,128)S(1)}, u32[]{:S(2)}, u32[]{:S(2)}) collective-permute-start(f32[4,32,256]{2,1,0:T(8,128)S(1)} %pad_maximum_fusion.2.refs_0_), channel_id=1, source_target_pairs={{0,8},{1,9},{2,10},{3,11},{4,12},{5,13},{6,14},{7,15},{8,0},{9,1},... | collective-permute-start | bytes 393224 | tf_op jit(solution)/shard_map/ppermute | solution.py:265
  35.2 2.0 %collective-permute-start.16 = (f32[2,176,128]{2,1,0:T(8,128)S(1)}, f32[2,176,128]{2,1,0:T(8,128)S(1)}, u32[]{:S(2)}, u32[]{:S(2)}) collective-permute-start(f32[2,176,128]{2,1,0:T(8,128)S(1)} %slice.20), channel_id=1, source_target_pairs={{0,4},{1,5},{2,6},{3,7},{4,0},{5,1},{6,2},{7,3},{8,12},{9,13},{10,... | collective-permute-start | bytes 540680 | tf_op jit(solution)/shard_map/ppermute | solution.py:265
  37.2 1.2 %collective-permute-start.17 = (f32[2,176,128]{2,1,0:T(8,128)S(1)}, f32[2,176,128]{2,1,0:T(8,128)S(1)}, u32[]{:S(2)}, u32[]{:S(2)}) collective-permute-start(f32[2,176,128]{2,1,0:T(8,128)S(1)} %slice.21), channel_id=1, source_target_pairs={{0,2},{1,3},{2,0},{3,1},{4,6},{5,7},{6,4},{7,5},{8,10},{9,11},{10,... | collective-permute-start | bytes 540680 | tf_op jit(solution)/shard_map/ppermute | solution.py:265
  38.5 3.8 %shard_map.132 = (bf16[512,128]{1,0:T(8,128)(2,1)S(1)}, bf16[512,1024]{1,0:T(8,128)(2,1)S(1)}, f32[512,1024]{1,0:T(8,128)S(1)}, f32[512,1024]{1,0:T(8,128)S(1)}) custom-call(s32[2]{0:T(128)S(1)} %pad_add_fusion.place, f32[4,32,256]{2,1,0:T(8,128)S(1)} %pad_maximum_fusion.2.refs_0_, f32[4,32,256]{2,1,0:T(8,128)S(1)} %collective-permute-done.7.refs_1_, ...), custom_call_target="tpu_custom_call" | custom-call | flops 2500000000 | bytes 9000000 | tf_op jit(solution)/shard_map/pallas_call | solution.py:253
  42.3 1.3 %copy-done.8 = f32[512,1024]{1,0:T(8,128)} copy-done((f32[512,1024]{1,0:T(8,128)}, f32[512,1024]{1,0:T(8,128)S(1)}, u32[]{:S(2)}) %copy-start.8) | copy-done | bytes 2097176
  44.5 1.9 %collective-permute-start.18 = (f32[3,4,32,256]{3,2,1,0:T(8,128)S(1)}, f32[3,4,32,256]{3,2,1,0:T(8,128)S(1)}, u32[]{:S(2)}, u32[]{:S(2)}) collective-permute-start(f32[3,4,32,256]{3,2,1,0:T(8,128)S(1)} %pad_maximum_fusion), channel_id=1, source_target_pairs={{0,4},{1,5},{2,6},{3,7},{4,0},{5,1},{6,2},{7,3},{8,12},{9,13},{10,... | collective-permute-start | bytes 1179656 | tf_op jit(solution)/shard_map/ppermute | solution.py:265
  46.4 1.3 %shard_map.133 = (bf16[8,256,172]{2,1,0:T(8,128)(2,1)S(1)}, f32[8,1,256]{2,1,0:T(1,128)S(1)}) custom-call(s32[2]{0:T(128)S(1)} %pad_add_fusion.place, f32[4,176,128]{2,1,0:T(8,128)S(1)} %pad_maximum_fusion.1.refs_0_, f32[4,176,128]{2,1,0:T(8,128)S(1)} %collective-permute-done.14.refs_1_, f32[4,176,128]{2,1,0:T(8,128)S(1)} %collective-permute-done.15.refs_2_, ...), custom_call_target="tpu_custom_call" | custom-call | flops 1500000000 | bytes 5400000 | tf_op jit(solution)/shard_map/pallas_call | solution.py:253
  47.7 10.8 %shard_map.134 = (f32[428,1024]{1,0:T(8,128)S(1)}, f32[128,128]{1,0:T(8,128)S(1)}) custom-call(s32[2]{0:T(128)S(1)} %pad_add_fusion.place, f32[4,32,256]{2,1,0:T(8,128)S(1)} %pad_maximum_fusion.2.refs_0_, f32[4,32,256]{2,1,0:T(8,128)S(1)} %collective-permute-done.7.refs_1_, f32[4,32,256]{2,1,0:T(8,128)S(1)} %collective-permute-done.8.refs_2_, ...), custom_call_target="tpu_custom_call" | custom-call | flops 12499999744 | bytes 45000000 | tf_op jit(solution)/shard_map/pallas_call | solution.py:253
  58.6 7.3 %shard_map.135 = (f32[428,1024]{1,0:T(8,128)S(1)}, f32[128,128]{1,0:T(8,128)}) custom-call(s32[2]{0:T(128)S(1)} %pad_add_fusion.place, f32[428,1024]{1,0:T(8,128)S(1)} %get-tuple-element.39.refs_0_, f32[128,128]{1,0:T(8,128)S(1)} %get-tuple-element.40.refs_1_, f32[4,32,256]{2,1,0:T(8,128)S(1)} %get-tuple-element.48.refs_2_, ...), custom_call_target="tpu_custom_call" | custom-call | flops 7500000256 | bytes 27000000 | tf_op jit(solution)/shard_map/pallas_call | solution.py:253
  66.0 3.7 %collective-permute-done.19.theirs = f32[428,1024]{1,0:T(8,128)S(1)} collective-permute-done((f32[428,1024]{1,0:T(8,128)S(1)}, f32[428,1024]{1,0:T(8,128)S(1)}, u32[]{:S(2)}, u32[]{:S(2)}) %collective-permute-start.19) | collective-permute-done | bytes 1753120 | tf_op jit(solution)/shard_map/ppermute | solution.py:265
  69.7 1.5 %shard_map.136 = (f32[128,1024]{1,0:T(8,128)}, f32[128,1024]{1,0:T(8,128)}, f32[172,1024]{1,0:T(8,128)}) custom-call(f32[428,1024]{1,0:T(8,128)S(1)} %get-tuple-element.42.mine, f32[428,1024]{1,0:T(8,128)S(1)} %collective-permute-done.19.theirs), custom_call_target="tpu_custom_call" | custom-call | flops 1500000000 | bytes 5400000 | tf_op jit(solution)/shard_map/pallas_call | solution.py:253
  (51 shorter events, 4.8 us)
Async XLA Ops:
  0.6 13.9 %collective-permute-start.1 = (f32[32,512]{1,0:T(8,128)}, f32[32,512]{1,0:T(8,128)S(1)}, u32[]{:S(2)}, u32[]{:S(2)}) collective-permute-start(f32[32,512]{1,0:T(8,128)} %features.1), channel_id=1, source_target_pairs={{0,28},{1,29},{2,30},{3,31},{4,8},{5,9},{6,10},{7,11},{8,4},{9,5},... | collective-permute-start | bytes 196616 | tf_op jit(solution)/shard_map/ppermute | solution.py:290
  6.7 7.9 %collective-permute-start = (f32[32,512]{1,0:T(8,128)}, f32[32,512]{1,0:T(8,128)S(1)}, u32[]{:S(2)}, u32[]{:S(2)}) collective-permute-start(f32[32,512]{1,0:T(8,128)} %features.1), channel_id=1, source_target_pairs={{0,4},{1,5},{2,6},{3,7},{4,0},{5,1},{6,2},{7,3},{8,12},{9,13},{10,... | collective-permute-start | bytes 196616 | tf_op jit(solution)/shard_map/ppermute | solution.py:265
  8.2 6.3 %copy-start.3 = (f32[32,512]{1,0:T(8,128)S(1)}, f32[32,512]{1,0:T(8,128)}, u32[]{:S(2)}) copy-start(f32[32,512]{1,0:T(8,128)} %features.1) | copy-start | bytes 196612
  8.2 6.3 %copy-start.6 = (s32[40]{0:T(128)S(1)}, s32[40]{0:T(128)}, u32[]{:S(2)}) copy-start(s32[40]{0:T(128)} %row.3) | copy-start | bytes 484
  8.2 6.4 %copy-start.7 = (s32[40]{0:T(128)S(1)}, s32[40]{0:T(128)}, u32[]{:S(2)}) copy-start(s32[40]{0:T(128)} %col.3) | copy-start | bytes 484
  9.4 8.8 %collective-permute-start.13 = (f32[176,128]{1,0:T(8,128)S(1)}, f32[176,128]{1,0:T(8,128)S(1)}, u32[]{:S(2)}, u32[]{:S(2)}) collective-permute-start(f32[176,128]{1,0:T(8,128)S(1)} %get-tuple-element.36), channel_id=1, source_target_pairs={{0,24},{1,25},{2,26},{3,27},{4,28},{5,29},{6,30},{7,31},{8,16},{9,... | collective-permute-start | bytes 270344 | tf_op jit(solution)/shard_map/ppermute | solution.py:265
  10.1 9.8 %collective-permute-start.12 = (f32[176,128]{1,0:T(8,128)S(1)}, f32[176,128]{1,0:T(8,128)S(1)}, u32[]{:S(2)}, u32[]{:S(2)}) collective-permute-start(f32[176,128]{1,0:T(8,128)S(1)} %get-tuple-element.36), channel_id=1, source_target_pairs={{0,16},{1,17},{2,18},{3,19},{4,20},{5,21},{6,22},{7,23},{8,24},{9,... | collective-permute-start | bytes 270344 | tf_op jit(solution)/shard_map/ppermute | solution.py:265
  11.0 8.9 %collective-permute-start.11 = (f32[176,128]{1,0:T(8,128)S(1)}, f32[176,128]{1,0:T(8,128)S(1)}, u32[]{:S(2)}, u32[]{:S(2)}) collective-permute-start(f32[176,128]{1,0:T(8,128)S(1)} %get-tuple-element.36), channel_id=1, source_target_pairs={{0,8},{1,9},{2,10},{3,11},{4,12},{5,13},{6,14},{7,15},{8,0},{9,1},... | collective-permute-start | bytes 270344 | tf_op jit(solution)/shard_map/ppermute | solution.py:265
  16.1 7.1 %collective-permute-start.3 = (f32[32,512]{1,0:T(8,128)S(1)}, f32[32,512]{1,0:T(8,128)S(1)}, u32[]{:S(2)}, u32[]{:S(2)}) collective-permute-start(f32[32,512]{1,0:T(8,128)S(1)} %shard_map.129.own), channel_id=1, source_target_pairs={{0,28},{1,29},{2,30},{3,31},{4,8},{5,9},{6,10},{7,11},{8,4},{9,5},... | collective-permute-start | bytes 196616 | tf_op jit(solution)/shard_map/ppermute | solution.py:290
  18.1 5.1 %collective-permute-start.2 = (f32[32,512]{1,0:T(8,128)S(1)}, f32[32,512]{1,0:T(8,128)S(1)}, u32[]{:S(2)}, u32[]{:S(2)}) collective-permute-start(f32[32,512]{1,0:T(8,128)S(1)} %shard_map.129.own), channel_id=1, source_target_pairs={{0,4},{1,5},{2,6},{3,7},{4,0},{5,1},{6,2},{7,3},{8,12},{9,13},{10,... | collective-permute-start | bytes 196616 | tf_op jit(solution)/shard_map/ppermute | solution.py:265
  20.0 13.8 %collective-permute-start.15 = (f32[4,176,128]{2,1,0:T(8,128)S(1)}, f32[4,176,128]{2,1,0:T(8,128)S(1)}, u32[]{:S(2)}, u32[]{:S(2)}) collective-permute-start(f32[4,176,128]{2,1,0:T(8,128)S(1)} %pad_maximum_fusion.1.refs_0_), channel_id=1, source_target_pairs={{0,2},{1,3},{2,0},{3,1},{4,6},{5,7},{6,4},{7,5},{8,10},{9,11},{10,... | collective-permute-start | bytes 1081352 | tf_op jit(solution)/shard_map/ppermute | solution.py:265
  21.6 13.6 %collective-permute-start.14 = (f32[4,176,128]{2,1,0:T(8,128)S(1)}, f32[4,176,128]{2,1,0:T(8,128)S(1)}, u32[]{:S(2)}, u32[]{:S(2)}) collective-permute-start(f32[4,176,128]{2,1,0:T(8,128)S(1)} %pad_maximum_fusion.1.refs_0_), channel_id=1, source_target_pairs={{0,4},{1,5},{2,6},{3,7},{4,0},{5,1},{6,2},{7,3},{8,12},{9,13},{10,... | collective-permute-start | bytes 1081352 | tf_op jit(solution)/shard_map/ppermute | solution.py:265
  23.2 15.3 %copy-start.2 = (bf16[128,1024]{1,0:T(8,128)(2,1)S(1)}, bf16[128,1024]{1,0:T(8,128)(2,1)}, u32[]{:S(2)}) copy-start(bf16[128,1024]{1,0:T(8,128)(2,1)} %refs_7_.1) | copy-start | bytes 786436
  24.9 5.0 %collective-permute-start.5 = (f32[32,256]{1,0:T(8,128)S(1)}, f32[32,256]{1,0:T(8,128)S(1)}, u32[]{:S(2)}, u32[]{:S(2)}) collective-permute-start(f32[32,256]{1,0:T(8,128)S(1)} %get-tuple-element.26), channel_id=1, source_target_pairs={{0,2},{1,3},{2,0},{3,1},{4,6},{5,7},{6,4},{7,5},{8,10},{9,11},{10,... | collective-permute-start | bytes 98312 | tf_op jit(solution)/shard_map/ppermute | solution.py:265
  27.0 3.6 %collective-permute-start.6 = (f32[32,256]{1,0:T(8,128)S(1)}, f32[32,256]{1,0:T(8,128)S(1)}, u32[]{:S(2)}, u32[]{:S(2)}) collective-permute-start(f32[32,256]{1,0:T(8,128)S(1)} %get-tuple-element.27), channel_id=1, source_target_pairs={{0,3},{1,2},{2,1},{3,0},{4,7},{5,6},{6,5},{7,4},{8,11},{9,10},{10,... | collective-permute-start | bytes 98312 | tf_op jit(solution)/shard_map/ppermute | solution.py:265
  27.0 3.6 %collective-permute-start.4 = (f32[32,256]{1,0:T(8,128)S(1)}, f32[32,256]{1,0:T(8,128)S(1)}, u32[]{:S(2)}, u32[]{:S(2)}) collective-permute-start(f32[32,256]{1,0:T(8,128)S(1)} %get-tuple-element.27), channel_id=1, source_target_pairs={{0,1},{1,0},{2,3},{3,2},{4,5},{5,4},{6,7},{7,6},{8,9},{9,8},{10,11... | collective-permute-start | bytes 98312 | tf_op jit(solution)/shard_map/ppermute | solution.py:265
  30.6 6.6 %collective-permute-start.7 = (f32[4,32,256]{2,1,0:T(8,128)S(1)}, f32[4,32,256]{2,1,0:T(8,128)S(1)}, u32[]{:S(2)}, u32[]{:S(2)}) collective-permute-start(f32[4,32,256]{2,1,0:T(8,128)S(1)} %pad_maximum_fusion.2.refs_0_), channel_id=1, source_target_pairs={{0,4},{1,5},{2,6},{3,7},{4,0},{5,1},{6,2},{7,3},{8,12},{9,13},{10,... | collective-permute-start | bytes 393224 | tf_op jit(solution)/shard_map/ppermute | solution.py:265
  30.7 12.9 %collective-permute-start.10 = (f32[4,32,256]{2,1,0:T(8,128)S(1)}, f32[4,32,256]{2,1,0:T(8,128)S(1)}, u32[]{:S(2)}, u32[]{:S(2)}) collective-permute-start(f32[4,32,256]{2,1,0:T(8,128)S(1)} %pad_maximum_fusion.2.refs_0_), channel_id=1, source_target_pairs={{0,24},{1,25},{2,26},{3,27},{4,28},{5,29},{6,30},{7,31},{8,16},{9,... | collective-permute-start | bytes 393224 | tf_op jit(solution)/shard_map/ppermute | solution.py:265
  33.8 10.7 %collective-permute-start.9 = (f32[4,32,256]{2,1,0:T(8,128)S(1)}, f32[4,32,256]{2,1,0:T(8,128)S(1)}, u32[]{:S(2)}, u32[]{:S(2)}) collective-permute-start(f32[4,32,256]{2,1,0:T(8,128)S(1)} %pad_maximum_fusion.2.refs_0_), channel_id=1, source_target_pairs={{0,16},{1,17},{2,18},{3,19},{4,20},{5,21},{6,22},{7,23},{8,24},{9,... | collective-permute-start | bytes 393224 | tf_op jit(solution)/shard_map/ppermute | solution.py:265
  33.8 10.7 %collective-permute-start.8 = (f32[4,32,256]{2,1,0:T(8,128)S(1)}, f32[4,32,256]{2,1,0:T(8,128)S(1)}, u32[]{:S(2)}, u32[]{:S(2)}) collective-permute-start(f32[4,32,256]{2,1,0:T(8,128)S(1)} %pad_maximum_fusion.2.refs_0_), channel_id=1, source_target_pairs={{0,8},{1,9},{2,10},{3,11},{4,12},{5,13},{6,14},{7,15},{8,0},{9,1},... | collective-permute-start | bytes 393224 | tf_op jit(solution)/shard_map/ppermute | solution.py:265
  35.2 11.2 %collective-permute-start.16 = (f32[2,176,128]{2,1,0:T(8,128)S(1)}, f32[2,176,128]{2,1,0:T(8,128)S(1)}, u32[]{:S(2)}, u32[]{:S(2)}) collective-permute-start(f32[2,176,128]{2,1,0:T(8,128)S(1)} %slice.20), channel_id=1, source_target_pairs={{0,4},{1,5},{2,6},{3,7},{4,0},{5,1},{6,2},{7,3},{8,12},{9,13},{10,... | collective-permute-start | bytes 540680 | tf_op jit(solution)/shard_map/ppermute | solution.py:265
  37.2 9.2 %collective-permute-start.17 = (f32[2,176,128]{2,1,0:T(8,128)S(1)}, f32[2,176,128]{2,1,0:T(8,128)S(1)}, u32[]{:S(2)}, u32[]{:S(2)}) collective-permute-start(f32[2,176,128]{2,1,0:T(8,128)S(1)} %slice.21), channel_id=1, source_target_pairs={{0,2},{1,3},{2,0},{3,1},{4,6},{5,7},{6,4},{7,5},{8,10},{9,11},{10,... | collective-permute-start | bytes 540680 | tf_op jit(solution)/shard_map/ppermute | solution.py:265
  44.5 14.0 %collective-permute-start.18 = (f32[3,4,32,256]{3,2,1,0:T(8,128)S(1)}, f32[3,4,32,256]{3,2,1,0:T(8,128)S(1)}, u32[]{:S(2)}, u32[]{:S(2)}) collective-permute-start(f32[3,4,32,256]{3,2,1,0:T(8,128)S(1)} %pad_maximum_fusion), channel_id=1, source_target_pairs={{0,4},{1,5},{2,6},{3,7},{4,0},{5,1},{6,2},{7,3},{8,12},{9,13},{10,... | collective-permute-start | bytes 1179656 | tf_op jit(solution)/shard_map/ppermute | solution.py:265
  65.9 3.8 %collective-permute-start.19 = (f32[428,1024]{1,0:T(8,128)S(1)}, f32[428,1024]{1,0:T(8,128)S(1)}, u32[]{:S(2)}, u32[]{:S(2)}) collective-permute-start(f32[428,1024]{1,0:T(8,128)S(1)} %get-tuple-element.42.mine), channel_id=1, source_target_pairs={{0,1},{1,0},{2,3},{3,2},{4,5},{5,4},{6,7},{7,6},{8,9},{9,8},{10,11... | collective-permute-start | bytes 5259272 | tf_op jit(solution)/shard_map/ppermute | solution.py:265
  (6 other events, 16.5 us)

commit v3 on v2

--- a/solution.py
+++ b/solution.py
@@ -180,16 +180,15 @@
         out[...] = result
 
 
-def train_kernel(fresh, masks, begun, again, place, *refs):
+def train_kernel(fresh, masks, begun, again, finish, place, *refs):
     if again:
         grads_before, batch_before = refs[:2]
         refs = refs[2:]
     sources = refs[: len(masks)]
     refs = refs[len(masks) :]
     states = refs[:4] if begun else ()
-    arranged, slot_rows, w_in, w_mid, w_out, grads, batch = refs[len(states) :]
-    feats = w_in.shape[0]
-    mid_rows = grads.shape[0] - feats - arranged.shape[2]
+    arranged, slot_rows, w_in, w_mid, w_out, grads, batch, *rest = refs[len(states) :]
+    mid_rows = grads.shape[0] - arranged.shape[2]
     dom, rep = place[0], place[1]
     width = batch.shape[1]
     replicas = sources[0].shape[0]
@@ -216,37 +215,40 @@
             jnp.concatenate([state[...], result], axis=0) for state, result in zip(states, results)
         ]
     own_hidden, hidden_two, slope_one, slope_two = results
-
-    def add(first_row, last_row, term):
-        cut = slice(first_row, last_row)
-        grads[cut, :] = grads_before[cut, :] + term if again else term
-
-    add(
-        feats + mid_rows,
-        grads.shape[0],
-        lax.dot_general(cot, hidden_two, LEADING, preferred_element_type=F32),
-    )
+    term = lax.dot_general(cot, hidden_two, LEADING, preferred_element_type=F32)
+    grads[mid_rows:, :] = grads_before[mid_rows:, :] + term if again else term
     back_two = jnp.dot(cot, w_out[...], preferred_element_type=F32)
     delta_two = (back_two * slope_two).astype(BF16)
-    add(
-        feats,
-        feats + mid_rows,
-        lax.dot_general(own_hidden, delta_two, LEADING, preferred_element_type=F32),
-    )
+    term = lax.dot_general(own_hidden, delta_two, LEADING, preferred_element_type=F32)
+    grads[:mid_rows, :] = grads_before[:mid_rows, :] + term if again else term
+    if finish:
+        rest[0][...] = input_gradient(inputs, delta_two, slope_one, w_mid)
+    else:
+        for out, value in zip(rest, (inputs, delta_two, slope_one)):
+            out[...] = value
+
+
+def input_gradient(inputs, delta_two, slope_one, w_mid):
     back_one = lax.dot_general(delta_two, w_mid[...], TRAILING, preferred_element_type=F32)
     delta_one = (back_one * slope_one).astype(BF16)
-    add(0, feats, jnp.dot(inputs, delta_one, preferred_element_type=F32))
-
-
-def add_kernel(mine, theirs, grad_in, grad_mid, grad_out):
+    return jnp.dot(inputs, delta_one, preferred_element_type=F32)
+
+
+def last_kernel(before, inputs, delta_two, slope_one, w_mid, grad_in):
+    grad_in[...] = before[...] + input_gradient(
+        inputs[...], delta_two[...], slope_one[...], w_mid
+    )
+
+
+def add_kernel(split, mine, theirs, *outs):
     start = 0
-    for out in (grad_in, grad_mid, grad_out):
-        rows = out.shape[0]
-        out[...] = mine[start : start + rows, :] + theirs[start : start + rows, :]
-        start += rows
-
-
-def call(kernel, outs, scalars, arrays, scratch=(), micros=1.5, space=pltpu.VMEM):
+    for out in outs:
+        cut = slice(start, start + out.shape[0]) if split else slice(None)
+        out[...] = mine[cut, :] + theirs[cut, :]
+        start += out.shape[0]
+
+
+def call(kernel, outs, scalars, arrays, scratch=(), micros=1.5, space=pltpu.VMEM, mib=16):
     cost = pl.CostEstimate(
         flops=int(micros * 1e9), bytes_accessed=int(micros * 3.6e6), transcendentals=0
     )
@@ -256,7 +258,7 @@
         in_specs=[SMEM] * len(scalars) + [pl.BlockSpec(memory_space=space)] * len(arrays),
         out_specs=jax.tree.map(lambda _: VMEM, outs),
         scratch_shapes=list(scratch),
-        compiler_params=pltpu.CompilerParams(vmem_limit_bytes=48 * 2**20),
+        compiler_params=pltpu.CompilerParams(vmem_limit_bytes=mib * 2**20),
         cost_estimate=cost,
     )(*scalars, *arrays)
 
@@ -305,7 +307,7 @@
             pltpu.VMEM((classes, width), BF16),
             pltpu.SemaphoreType.DMA((2,)),
         ],
-        space=pl.ANY,
+        space=pltpu.HBM,
     )
     field = pltpu.VMEM((3 * count, 3 * feature_count, size), BF16)
     first = call(
@@ -330,6 +332,20 @@
     own = jnp.stack([mine, send(other, 1), send(mine, 2), send(other, 3)])
     facing = send(own, 4)
     ring = [send(own, m) for m in (8, 16, 24)]
+    mid_rows = hidden // owners
+    begun = call(
+        functools.partial(forward_kernel, mid_rows),
+        (
+            jax.ShapeDtypeStruct((2 * half, mid_rows), BF16),
+            jax.ShapeDtypeStruct((2 * half, hidden), BF16),
+            jax.ShapeDtypeStruct((2 * half, hidden), F32),
+            jax.ShapeDtypeStruct((2 * half, hidden), F32),
+        ),
+        [place],
+        [own, facing, w_in, w_mid],
+        micros=2.5,
+        mib=16,
+    )
     orders = ((0, 4, 8, 12), (2, 6, 10, 14), (1, 5, 9, 13), (3, 7), (11, 15))
     arranged, slot_rows = call(
         functools.partial(cotangent_kernel, orders, classes, segment),
@@ -344,49 +360,50 @@
             pltpu.VMEM((devices // 2, rows, width), F32),
         ],
     )
-    mid_rows = hidden // owners
-    total_rows = feature_count * replicas + mid_rows + classes
-
-    begun = call(
-        functools.partial(forward_kernel, mid_rows),
-        (
-            jax.ShapeDtypeStruct((2 * half, mid_rows), BF16),
-            jax.ShapeDtypeStruct((2 * half, hidden), BF16),
-            jax.ShapeDtypeStruct((2 * half, hidden), F32),
-            jax.ShapeDtypeStruct((2 * half, hidden), F32),
-        ),
-        [place],
-        [own, facing, w_in, w_mid],
-        micros=2.5,
-    )
-    *ring, gate = lax.optimization_barrier((*ring, begun[0]))
+    *ring, gate, slot_rows = lax.optimization_barrier((*ring, begun[0], slot_rows))
     begun = (gate, *begun[1:])
     last = send(jnp.stack(ring), 4)
 
-    def train(before, sources, masks, states):
+    feats = feature_count * replicas
+    mid_shape = jax.ShapeDtypeStruct((mid_rows, hidden), F32)
+    out_shape = jax.ShapeDtypeStruct((classes, hidden), F32)
+    grads_shape = jax.ShapeDtypeStruct((mid_rows + classes, hidden), F32)
+    in_shape = jax.ShapeDtypeStruct((feats, hidden), F32)
+    batch_shape = jax.ShapeDtypeStruct((feats, width), F32)
+
+    def train(before, sources, masks, states, finish, mib):
         fresh = half * (len(masks) - 2 * bool(states))
+        rows = half * len(masks)
+        rest = (
+            (in_shape,)
+            if finish
+            else (
+                jax.ShapeDtypeStruct((feats, rows), BF16),
+                jax.ShapeDtypeStruct((rows, hidden), BF16),
+                jax.ShapeDtypeStruct((rows, hidden), F32),
+            )
+        )
         return call(
-            functools.partial(train_kernel, fresh, masks, bool(states), bool(before)),
-            (
-                jax.ShapeDtypeStruct((total_rows, hidden), F32),
-                jax.ShapeDtypeStruct((feature_count * replicas, width), F32),
-            ),
+            functools.partial(train_kernel, fresh, masks, bool(states), bool(before), finish),
+            (grads_shape, batch_shape, *rest),
             [place],
             [*before, *sources, *states, arranged, slot_rows, w_in, w_mid, w_out],
             micros=2.5 * len(masks),
+            mib=mib,
         )
 
-    state = train((), [own, facing, *ring], (0, 1, 2, 4, 6), begun)
-    grads, batch_features = train(state, [last[0], last[1], last[2]], (3, 5, 7), ())
-    grad_in, grad_mid, grad_out = call(
-        add_kernel,
-        tuple(
-            jax.ShapeDtypeStruct((n, hidden), F32)
-            for n in (feature_count * replicas, mid_rows, classes)
-        ),
-        [],
-        [grads, send(grads, 1)],
-    )
+    grads_before, batch_before, in_before = train((), [own, facing, *ring], (0, 1, 2, 4, 6), begun, True, 32)
+    grads, batch_features, *rest = train(
+        (grads_before, batch_before), [last[0], last[1], last[2]], (3, 5, 7), (), False, 20
+    )
+    theirs = send(grads, 1)
+    grad_in = call(last_kernel, in_shape, [], [in_before, *rest, w_mid], micros=2.5, mib=12)
+    their_in = send(grad_in, 1)
+    grad_mid, grad_out = call(
+        functools.partial(add_kernel, True), (mid_shape, out_shape), [], [grads, theirs]
+    )
+    their_in, grad_mid = lax.optimization_barrier((their_in, grad_mid))
+    grad_in = call(functools.partial(add_kernel, False), (in_shape,), [], [grad_in, their_in])[0]
     return batch_features, grad_in, grad_mid, grad_out
 
 

time: 71.4 us -> 65.1 us (0.912)
  Pallas kernels: 29.1 us -> 25.9 us
  waiting for transfers between devices: 11 us -> 8.71 us
  local copies, waits for them, and re-layouts: 2.9 us -> 1.55 us
    pallas_call x8 -> x10, Pallas kernels: 29.1 us -> 25.9 us  [call(): pl.pallas_call(kernel, out_shape=outs, in_specs=[SMEM] * len(scalars) + [...]
    ppermute x18 -> x19, waiting for transfers between devices: 9.67 us -> 7.4 us  [exchanged(): return lax.ppermute(value, AXES, [(i, i ^ mask) for i in range(devices)])]
    unnamed x20 -> x18, local copies, waits for them, and re-layouts: 2.85 us -> 1.5 us
    ppermute x18 -> x19, starting transfers between devices: 18.5 us -> 19.1 us  [exchanged(): return lax.ppermute(value, AXES, [(i, i ^ mask) for i in range(devices)])]
  transfers between devices with their start and end apart: 20 -> 21, of which waited for: 6 -> 8; matrix products, arithmetic and copies ran while one was open for 0% -> 0% of each run, Pallas kernels for 29% -> 31%
where the time goes in v3:
time: 65.1 us; the launch traced here: 64.9 us
  starting transfers between devices  27.1 us (42%)
  Pallas kernels  25.9 us (40%)
  waiting for transfers between devices  8.71 us (13%)
  local copies, waits for them, and re-layouts  1.55 us (2%)
  between operations  1.5 us (2%)
    pallas_call x10, Pallas kernels, call(): pl.pallas_call(kernel, out_shape=outs, in_specs=[SMEM] * len(scalars) + [...  25.9 us
    ppermute x19, starting transfers between devices, exchanged(): return lax.ppermute(value, AXES, [(i, i ^ mask) for i in range(devices)])  19.1 us
    ppermute x2, starting transfers between devices, far(): return lax.ppermute(value, AXES, far_pairs)  8.02 us
    ppermute x19, waiting for transfers between devices, exchanged(): return lax.ppermute(value, AXES, [(i, i ^ mask) for i in range(devices)])  7.4 us
    unnamed x18, local copies, waits for them, and re-layouts  1.5 us
    ppermute x2, waiting for transfers between devices, far(): return lax.ppermute(value, AXES, far_pairs)  1.31 us
  transfers between devices with their start and end apart: 21, of which 8 were waited for; matrix products, arithmetic and copies ran while one was open for 0% of the time, Pallas kernels for 31%

profile of v3, /device:TPU:0, one launch (start us, length us, event | category | flops | bytes accessed | tf_op | source)
XLA Modules:
  0.0 64.9 jit_solution(14420872348681630554)
XLA Ops:
  0.6 6.0 %collective-permute-start.1 = (f32[32,512]{1,0:T(8,128)}, f32[32,512]{1,0:T(8,128)S(1)}, u32[]{:S(2)}, u32[]{:S(2)}) collective-permute-start(f32[32,512]{1,0:T(8,128)} %features.1), channel_id=1, source_target_pairs={{0,28},{1,29},{2,30},{3,31},{4,8},{5,9},{6,10},{7,11},{8,4},{9,5},... | collective-permute-start | bytes 196616 | tf_op jit(solution)/shard_map/ppermute | solution.py:292
  8.2 1.2 %shard_map.130 = (f32[176,128]{1,0:T(8,128)S(1)}, s32[1,512]{1,0:T(1,128)S(1)}) custom-call(s32[2]{0:T(128)S(1)} %pad_add_fusion.place, s32[1,512]{1,0:T(1,128)S(1)} %bitcast.25, bf16[172,128]{1,0:T(8,128)(2,1)S(1)} %copy-done.5), custom_call_target="tpu_custom_call" | custom-call | flops 1500000000 | bytes 5400000 | tf_op jit(solution)/shard_map/pallas_call | solution.py:255
  10.1 0.9 %collective-permute-start.12 = (f32[176,128]{1,0:T(8,128)S(1)}, f32[176,128]{1,0:T(8,128)S(1)}, u32[]{:S(2)}, u32[]{:S(2)}) collective-permute-start(f32[176,128]{1,0:T(8,128)S(1)} %get-tuple-element.35), channel_id=1, source_target_pairs={{0,16},{1,17},{2,18},{3,19},{4,20},{5,21},{6,22},{7,23},{8,24},{9,... | collective-permute-start | bytes 270344 | tf_op jit(solution)/shard_map/ppermute | solution.py:267
  11.0 2.8 %collective-permute-start.11 = (f32[176,128]{1,0:T(8,128)S(1)}, f32[176,128]{1,0:T(8,128)S(1)}, u32[]{:S(2)}, u32[]{:S(2)}) collective-permute-start(f32[176,128]{1,0:T(8,128)S(1)} %get-tuple-element.35), channel_id=1, source_target_pairs={{0,8},{1,9},{2,10},{3,11},{4,12},{5,13},{6,14},{7,15},{8,0},{9,1},... | collective-permute-start | bytes 270344 | tf_op jit(solution)/shard_map/ppermute | solution.py:267
  14.6 1.5 %shard_map.129.own = f32[32,512]{1,0:T(8,128)S(1)} custom-call(s32[2]{0:T(128)S(1)} %pad_add_fusion.place, s32[1]{0:T(128)S(6)} %copy.14.live, s32[40]{0:T(128)S(1)} %copy-done.7, s32[40]{0:T(128)S(1)} %copy-done.8, f32[32,512]{1,0:T(8,128)S(1)} %copy-done.4, f32[32,512]{1,0:T(8,128)S(1)} %collective-permute-done.near, ...), custom_call_target="tpu_custom_call" | custom-call | flops 1500000000 | bytes 5400000 | tf_op jit(solution)/shard_map/pallas_call | solution.py:255
  16.1 2.0 %collective-permute-start.3 = (f32[32,512]{1,0:T(8,128)S(1)}, f32[32,512]{1,0:T(8,128)S(1)}, u32[]{:S(2)}, u32[]{:S(2)}) collective-permute-start(f32[32,512]{1,0:T(8,128)S(1)} %shard_map.129.own), channel_id=1, source_target_pairs={{0,28},{1,29},{2,30},{3,31},{4,8},{5,9},{6,10},{7,11},{8,4},{9,5},... | collective-permute-start | bytes 196616 | tf_op jit(solution)/shard_map/ppermute | solution.py:292
  18.3 1.7 %collective-permute-done.12 = f32[176,128]{1,0:T(8,128)S(1)} collective-permute-done((f32[176,128]{1,0:T(8,128)S(1)}, f32[176,128]{1,0:T(8,128)S(1)}, u32[]{:S(2)}, u32[]{:S(2)}) %collective-permute-start.12) | collective-permute-done | bytes 90144 | tf_op jit(solution)/shard_map/ppermute | solution.py:267
  20.0 1.6 %collective-permute-start.15 = (f32[4,176,128]{2,1,0:T(8,128)S(1)}, f32[4,176,128]{2,1,0:T(8,128)S(1)}, u32[]{:S(2)}, u32[]{:S(2)}) collective-permute-start(f32[4,176,128]{2,1,0:T(8,128)S(1)} %pad_maximum_fusion.1.refs_0_), channel_id=1, source_target_pairs={{0,2},{1,3},{2,0},{3,1},{4,6},{5,7},{6,4},{7,5},{8,10},{9,11},{10,... | collective-permute-start | bytes 1081352 | tf_op jit(solution)/shard_map/ppermute | solution.py:267
  21.9 1.3 %collective-permute-done.3.far = f32[32,512]{1,0:T(8,128)S(1)} collective-permute-done((f32[32,512]{1,0:T(8,128)S(1)}, f32[32,512]{1,0:T(8,128)S(1)}, u32[]{:S(2)}, u32[]{:S(2)}) %collective-permute-start.3) | collective-permute-done | bytes 65568 | tf_op jit(solution)/shard_map/ppermute | solution.py:292
  23.2 1.7 %shard_map.131 = (f32[32,256]{1,0:T(8,128)S(1)}, f32[32,256]{1,0:T(8,128)S(1)}) custom-call(s32[2]{0:T(128)S(1)} %pad_add_fusion.place, s32[1]{0:T(128)S(6)} %copy.14.live, s32[40]{0:T(128)S(1)} %copy-done.7, s32[40]{0:T(128)S(1)} %copy-done.8, f32[32,512]{1,0:T(8,128)S(1)} %shard_map.129.own, f32[32,512]{1,0:T(8,128)S(1)} %collective-permute-done.2.near, ...), custom_call_target="tpu_custom_call" | custom-call | flops 1500000000 | bytes 5400000 | tf_op jit(solution)/shard_map/pallas_call | solution.py:255
  24.9 2.1 %collective-permute-start.5 = (f32[32,256]{1,0:T(8,128)S(1)}, f32[32,256]{1,0:T(8,128)S(1)}, u32[]{:S(2)}, u32[]{:S(2)}) collective-permute-start(f32[32,256]{1,0:T(8,128)S(1)} %get-tuple-element.32), channel_id=1, source_target_pairs={{0,2},{1,3},{2,0},{3,1},{4,6},{5,7},{6,4},{7,5},{8,10},{9,11},{10,... | collective-permute-start | bytes 98312 | tf_op jit(solution)/shard_map/ppermute | solution.py:267
  27.2 2.7 %collective-permute-done.5 = f32[32,256]{1,0:T(8,128)S(1)} collective-permute-done((f32[32,256]{1,0:T(8,128)S(1)}, f32[32,256]{1,0:T(8,128)S(1)}, u32[]{:S(2)}, u32[]{:S(2)}) %collective-permute-start.5) | collective-permute-done | bytes 32800 | tf_op jit(solution)/shard_map/ppermute | solution.py:267
  30.7 3.1 %collective-permute-start.10 = (f32[4,32,256]{2,1,0:T(8,128)S(1)}, f32[4,32,256]{2,1,0:T(8,128)S(1)}, u32[]{:S(2)}, u32[]{:S(2)}) collective-permute-start(f32[4,32,256]{2,1,0:T(8,128)S(1)} %pad_maximum_fusion.2.refs_0_), channel_id=1, source_target_pairs={{0,24},{1,25},{2,26},{3,27},{4,28},{5,29},{6,30},{7,31},{8,16},{9,... | collective-permute-start | bytes 393224 | tf_op jit(solution)/shard_map/ppermute | solution.py:267
  33.8 1.4 %collective-permute-start.8 = (f32[4,32,256]{2,1,0:T(8,128)S(1)}, f32[4,32,256]{2,1,0:T(8,128)S(1)}, u32[]{:S(2)}, u32[]{:S(2)}) collective-permute-start(f32[4,32,256]{2,1,0:T(8,128)S(1)} %pad_maximum_fusion.2.refs_0_), channel_id=1, source_target_pairs={{0,8},{1,9},{2,10},{3,11},{4,12},{5,13},{6,14},{7,15},{8,0},{9,1},... | collective-permute-start | bytes 393224 | tf_op jit(solution)/shard_map/ppermute | solution.py:267
  35.2 2.0 %collective-permute-start.16 = (f32[2,176,128]{2,1,0:T(8,128)S(1)}, f32[2,176,128]{2,1,0:T(8,128)S(1)}, u32[]{:S(2)}, u32[]{:S(2)}) collective-permute-start(f32[2,176,128]{2,1,0:T(8,128)S(1)} %slice.20), channel_id=1, source_target_pairs={{0,4},{1,5},{2,6},{3,7},{4,0},{5,1},{6,2},{7,3},{8,12},{9,13},{10,... | collective-permute-start | bytes 540680 | tf_op jit(solution)/shard_map/ppermute | solution.py:267
  37.2 1.2 %collective-permute-start.17 = (f32[2,176,128]{2,1,0:T(8,128)S(1)}, f32[2,176,128]{2,1,0:T(8,128)S(1)}, u32[]{:S(2)}, u32[]{:S(2)}) collective-permute-start(f32[2,176,128]{2,1,0:T(8,128)S(1)} %slice.21), channel_id=1, source_target_pairs={{0,2},{1,3},{2,0},{3,1},{4,6},{5,7},{6,4},{7,5},{8,10},{9,11},{10,... | collective-permute-start | bytes 540680 | tf_op jit(solution)/shard_map/ppermute | solution.py:267
  38.5 2.7 %shard_map.132 = (bf16[512,128]{1,0:T(8,128)(2,1)S(1)}, bf16[512,1024]{1,0:T(8,128)(2,1)S(1)}, f32[512,1024]{1,0:T(8,128)S(1)}, f32[512,1024]{1,0:T(8,128)S(1)}) custom-call(s32[2]{0:T(128)S(1)} %pad_add_fusion.place, f32[4,32,256]{2,1,0:T(8,128)S(1)} %pad_maximum_fusion.2.refs_0_, f32[4,32,256]{2,1,0:T(8,128)S(1)} %collective-permute-done.7.refs_1_, ...), custom_call_target="tpu_custom_call" | custom-call | flops 2500000000 | bytes 9000000 | tf_op jit(solution)/shard_map/pallas_call | solution.py:255
  41.2 1.6 %collective-permute-done.17.refs_4_ = f32[2,176,128]{2,1,0:T(8,128)S(1)} collective-permute-done((f32[2,176,128]{2,1,0:T(8,128)S(1)}, f32[2,176,128]{2,1,0:T(8,128)S(1)}, u32[]{:S(2)}, u32[]{:S(2)}) %collective-permute-start.17) | collective-permute-done | bytes 180256 | tf_op jit(solution)/shard_map/ppermute | solution.py:267
  42.8 1.3 %shard_map.133 = (bf16[8,256,172]{2,1,0:T(8,128)(2,1)S(1)}, f32[8,1,256]{2,1,0:T(1,128)S(1)}) custom-call(s32[2]{0:T(128)S(1)} %pad_add_fusion.place, f32[4,176,128]{2,1,0:T(8,128)S(1)} %pad_maximum_fusion.1.refs_0_, f32[4,176,128]{2,1,0:T(8,128)S(1)} %collective-permute-done.14.refs_1_, f32[4,176,128]{2,1,0:T(8,128)S(1)} %collective-permute-done.15.refs_2_, ...), custom_call_target="tpu_custom_call" | custom-call | flops 1500000000 | bytes 5400000 | tf_op jit(solution)/shard_map/pallas_call | solution.py:255
  44.5 1.9 %collective-permute-start.18 = (f32[3,4,32,256]{3,2,1,0:T(8,128)S(1)}, f32[3,4,32,256]{3,2,1,0:T(8,128)S(1)}, u32[]{:S(2)}, u32[]{:S(2)}) collective-permute-start(f32[3,4,32,256]{3,2,1,0:T(8,128)S(1)} %pad_maximum_fusion), channel_id=1, source_target_pairs={{0,4},{1,5},{2,6},{3,7},{4,0},{5,1},{6,2},{7,3},{8,12},{9,13},{10,... | collective-permute-start | bytes 1179656 | tf_op jit(solution)/shard_map/ppermute | solution.py:267
  46.4 8.7 %shard_map.134 = (f32[300,1024]{1,0:T(8,128)S(1)}, f32[128,128]{1,0:T(8,128)S(1)}, f32[128,1024]{1,0:T(8,128)S(1)}) custom-call(s32[2]{0:T(128)S(1)} %pad_add_fusion.place, f32[4,32,256]{2,1,0:T(8,128)S(1)} %pad_maximum_fusion.2.refs_0_, f32[4,32,256]{2,1,0:T(8,128)S(1)} %collective-permute-done.7.refs_1_, f32[4,32,256]{2,1,0:T(8,128)S(1)} %collective-permute-done.8.refs_2_, ...), custom_call_target="tpu_custom_call" | custom-call | flops 12499999744 | bytes 45000000 | tf_op jit(solution)/shard_map/pallas_call | solution.py:255
  55.1 4.6 %shard_map.135 = (f32[300,1024]{1,0:T(8,128)S(1)}, f32[128,128]{1,0:T(8,128)}, bf16[128,768]{1,0:T(8,128)(2,1)S(1)}, bf16[768,1024]{1,0:T(8,128)(2,1)S(1)}, f32[768,1024]{1,0:T(8,128)S(1)}) custom-call(s32[2]{0:T(128)S(1)} %pad_add_fusion.place, f32[300,1024]{1,0:T(8,128)S(1)} %get-tuple-element.46.refs_0_, f32[128,128]{1,0:T(8,128)S(1)} %get-tuple-element.47.refs_1_, ...), custom_call_target="tpu_custom_call" | custom-call | flops 7500000256 | bytes 27000000 | tf_op jit(solution)/shard_map/pallas_call | solution.py:255
  59.9 2.1 %shard_map.136.mine = f32[128,1024]{1,0:T(8,128)S(1)} custom-call(f32[128,1024]{1,0:T(8,128)S(1)} %get-tuple-element.49.before, bf16[128,768]{1,0:T(8,128)(2,1)S(1)} %get-tuple-element.50.inputs, bf16[768,1024]{1,0:T(8,128)(2,1)S(1)} %get-tuple-element.51.delta_two, f32[768,1024]{1,0:T(8,128)S(1)} %get-tuple-element.52.slope_one, bf16[1024,1024]{1,0:T(8,128)(2,1)S(1)} %copy-done), custom_call_target="tpu_custom_call" | custom-call | flops 2500000000 | bytes 9000000 | tf_op jit(solution)/shard_map/pallas_call | solution.py:255
  62.8 1.2 %shard_map.137 = (f32[128,1024]{1,0:T(8,128)}, f32[172,1024]{1,0:T(8,128)}) custom-call(f32[300,1024]{1,0:T(8,128)S(1)} %get-tuple-element.53.mine, f32[300,1024]{1,0:T(8,128)S(1)} %collective-permute-done.20.theirs), custom_call_target="tpu_custom_call" | custom-call | flops 1500000000 | bytes 5400000 | tf_op jit(solution)/shard_map/pallas_call | solution.py:255
  (53 shorter events, 6.0 us)
Async XLA Ops:
  0.6 13.9 %collective-permute-start.1 = (f32[32,512]{1,0:T(8,128)}, f32[32,512]{1,0:T(8,128)S(1)}, u32[]{:S(2)}, u32[]{:S(2)}) collective-permute-start(f32[32,512]{1,0:T(8,128)} %features.1), channel_id=1, source_target_pairs={{0,28},{1,29},{2,30},{3,31},{4,8},{5,9},{6,10},{7,11},{8,4},{9,5},... | collective-permute-start | bytes 196616 | tf_op jit(solution)/shard_map/ppermute | solution.py:292
  6.7 7.9 %collective-permute-start = (f32[32,512]{1,0:T(8,128)}, f32[32,512]{1,0:T(8,128)S(1)}, u32[]{:S(2)}, u32[]{:S(2)}) collective-permute-start(f32[32,512]{1,0:T(8,128)} %features.1), channel_id=1, source_target_pairs={{0,4},{1,5},{2,6},{3,7},{4,0},{5,1},{6,2},{7,3},{8,12},{9,13},{10,... | collective-permute-start | bytes 196616 | tf_op jit(solution)/shard_map/ppermute | solution.py:267
  8.2 6.4 %copy-start.8 = (s32[40]{0:T(128)S(1)}, s32[40]{0:T(128)}, u32[]{:S(2)}) copy-start(s32[40]{0:T(128)} %col.3) | copy-start | bytes 484
  9.4 8.8 %collective-permute-start.13 = (f32[176,128]{1,0:T(8,128)S(1)}, f32[176,128]{1,0:T(8,128)S(1)}, u32[]{:S(2)}, u32[]{:S(2)}) collective-permute-start(f32[176,128]{1,0:T(8,128)S(1)} %get-tuple-element.35), channel_id=1, source_target_pairs={{0,24},{1,25},{2,26},{3,27},{4,28},{5,29},{6,30},{7,31},{8,16},{9,... | collective-permute-start | bytes 270344 | tf_op jit(solution)/shard_map/ppermute | solution.py:267
  10.1 9.8 %collective-permute-start.12 = (f32[176,128]{1,0:T(8,128)S(1)}, f32[176,128]{1,0:T(8,128)S(1)}, u32[]{:S(2)}, u32[]{:S(2)}) collective-permute-start(f32[176,128]{1,0:T(8,128)S(1)} %get-tuple-element.35), channel_id=1, source_target_pairs={{0,16},{1,17},{2,18},{3,19},{4,20},{5,21},{6,22},{7,23},{8,24},{9,... | collective-permute-start | bytes 270344 | tf_op jit(solution)/shard_map/ppermute | solution.py:267
  11.0 8.9 %collective-permute-start.11 = (f32[176,128]{1,0:T(8,128)S(1)}, f32[176,128]{1,0:T(8,128)S(1)}, u32[]{:S(2)}, u32[]{:S(2)}) collective-permute-start(f32[176,128]{1,0:T(8,128)S(1)} %get-tuple-element.35), channel_id=1, source_target_pairs={{0,8},{1,9},{2,10},{3,11},{4,12},{5,13},{6,14},{7,15},{8,0},{9,1},... | collective-permute-start | bytes 270344 | tf_op jit(solution)/shard_map/ppermute | solution.py:267
  16.1 7.1 %collective-permute-start.3 = (f32[32,512]{1,0:T(8,128)S(1)}, f32[32,512]{1,0:T(8,128)S(1)}, u32[]{:S(2)}, u32[]{:S(2)}) collective-permute-start(f32[32,512]{1,0:T(8,128)S(1)} %shard_map.129.own), channel_id=1, source_target_pairs={{0,28},{1,29},{2,30},{3,31},{4,8},{5,9},{6,10},{7,11},{8,4},{9,5},... | collective-permute-start | bytes 196616 | tf_op jit(solution)/shard_map/ppermute | solution.py:292
  18.1 5.1 %collective-permute-start.2 = (f32[32,512]{1,0:T(8,128)S(1)}, f32[32,512]{1,0:T(8,128)S(1)}, u32[]{:S(2)}, u32[]{:S(2)}) collective-permute-start(f32[32,512]{1,0:T(8,128)S(1)} %shard_map.129.own), channel_id=1, source_target_pairs={{0,4},{1,5},{2,6},{3,7},{4,0},{5,1},{6,2},{7,3},{8,12},{9,13},{10,... | collective-permute-start | bytes 196616 | tf_op jit(solution)/shard_map/ppermute | solution.py:267
  20.0 13.8 %collective-permute-start.15 = (f32[4,176,128]{2,1,0:T(8,128)S(1)}, f32[4,176,128]{2,1,0:T(8,128)S(1)}, u32[]{:S(2)}, u32[]{:S(2)}) collective-permute-start(f32[4,176,128]{2,1,0:T(8,128)S(1)} %pad_maximum_fusion.1.refs_0_), channel_id=1, source_target_pairs={{0,2},{1,3},{2,0},{3,1},{4,6},{5,7},{6,4},{7,5},{8,10},{9,11},{10,... | collective-permute-start | bytes 1081352 | tf_op jit(solution)/shard_map/ppermute | solution.py:267
  21.6 13.6 %collective-permute-start.14 = (f32[4,176,128]{2,1,0:T(8,128)S(1)}, f32[4,176,128]{2,1,0:T(8,128)S(1)}, u32[]{:S(2)}, u32[]{:S(2)}) collective-permute-start(f32[4,176,128]{2,1,0:T(8,128)S(1)} %pad_maximum_fusion.1.refs_0_), channel_id=1, source_target_pairs={{0,4},{1,5},{2,6},{3,7},{4,0},{5,1},{6,2},{7,3},{8,12},{9,13},{10,... | collective-permute-start | bytes 1081352 | tf_op jit(solution)/shard_map/ppermute | solution.py:267
  23.2 15.3 %copy-start = (bf16[1024,1024]{1,0:T(8,128)(2,1)S(1)}, bf16[1024,1024]{1,0:T(8,128)(2,1)}, u32[]{:S(2)}) copy-start(bf16[1024,1024]{1,0:T(8,128)(2,1)} %w_mid.1) | copy-start | bytes 6291460
  23.2 15.3 %copy-start.3 = (bf16[128,1024]{1,0:T(8,128)(2,1)S(1)}, bf16[128,1024]{1,0:T(8,128)(2,1)}, u32[]{:S(2)}) copy-start(bf16[128,1024]{1,0:T(8,128)(2,1)} %refs_7_.1) | copy-start | bytes 786436
  24.9 5.0 %collective-permute-start.5 = (f32[32,256]{1,0:T(8,128)S(1)}, f32[32,256]{1,0:T(8,128)S(1)}, u32[]{:S(2)}, u32[]{:S(2)}) collective-permute-start(f32[32,256]{1,0:T(8,128)S(1)} %get-tuple-element.32), channel_id=1, source_target_pairs={{0,2},{1,3},{2,0},{3,1},{4,6},{5,7},{6,4},{7,5},{8,10},{9,11},{10,... | collective-permute-start | bytes 98312 | tf_op jit(solution)/shard_map/ppermute | solution.py:267
  27.0 3.6 %collective-permute-start.6 = (f32[32,256]{1,0:T(8,128)S(1)}, f32[32,256]{1,0:T(8,128)S(1)}, u32[]{:S(2)}, u32[]{:S(2)}) collective-permute-start(f32[32,256]{1,0:T(8,128)S(1)} %get-tuple-element.33), channel_id=1, source_target_pairs={{0,3},{1,2},{2,1},{3,0},{4,7},{5,6},{6,5},{7,4},{8,11},{9,10},{10,... | collective-permute-start | bytes 98312 | tf_op jit(solution)/shard_map/ppermute | solution.py:267
  27.0 3.6 %collective-permute-start.4 = (f32[32,256]{1,0:T(8,128)S(1)}, f32[32,256]{1,0:T(8,128)S(1)}, u32[]{:S(2)}, u32[]{:S(2)}) collective-permute-start(f32[32,256]{1,0:T(8,128)S(1)} %get-tuple-element.33), channel_id=1, source_target_pairs={{0,1},{1,0},{2,3},{3,2},{4,5},{5,4},{6,7},{7,6},{8,9},{9,8},{10,11... | collective-permute-start | bytes 98312 | tf_op jit(solution)/shard_map/ppermute | solution.py:267
  30.6 6.6 %collective-permute-start.7 = (f32[4,32,256]{2,1,0:T(8,128)S(1)}, f32[4,32,256]{2,1,0:T(8,128)S(1)}, u32[]{:S(2)}, u32[]{:S(2)}) collective-permute-start(f32[4,32,256]{2,1,0:T(8,128)S(1)} %pad_maximum_fusion.2.refs_0_), channel_id=1, source_target_pairs={{0,4},{1,5},{2,6},{3,7},{4,0},{5,1},{6,2},{7,3},{8,12},{9,13},{10,... | collective-permute-start | bytes 393224 | tf_op jit(solution)/shard_map/ppermute | solution.py:267
  30.7 13.4 %collective-permute-start.10 = (f32[4,32,256]{2,1,0:T(8,128)S(1)}, f32[4,32,256]{2,1,0:T(8,128)S(1)}, u32[]{:S(2)}, u32[]{:S(2)}) collective-permute-start(f32[4,32,256]{2,1,0:T(8,128)S(1)} %pad_maximum_fusion.2.refs_0_), channel_id=1, source_target_pairs={{0,24},{1,25},{2,26},{3,27},{4,28},{5,29},{6,30},{7,31},{8,16},{9,... | collective-permute-start | bytes 393224 | tf_op jit(solution)/shard_map/ppermute | solution.py:267
  33.8 10.7 %collective-permute-start.9 = (f32[4,32,256]{2,1,0:T(8,128)S(1)}, f32[4,32,256]{2,1,0:T(8,128)S(1)}, u32[]{:S(2)}, u32[]{:S(2)}) collective-permute-start(f32[4,32,256]{2,1,0:T(8,128)S(1)} %pad_maximum_fusion.2.refs_0_), channel_id=1, source_target_pairs={{0,16},{1,17},{2,18},{3,19},{4,20},{5,21},{6,22},{7,23},{8,24},{9,... | collective-permute-start | bytes 393224 | tf_op jit(solution)/shard_map/ppermute | solution.py:267
  33.8 10.7 %collective-permute-start.8 = (f32[4,32,256]{2,1,0:T(8,128)S(1)}, f32[4,32,256]{2,1,0:T(8,128)S(1)}, u32[]{:S(2)}, u32[]{:S(2)}) collective-permute-start(f32[4,32,256]{2,1,0:T(8,128)S(1)} %pad_maximum_fusion.2.refs_0_), channel_id=1, source_target_pairs={{0,8},{1,9},{2,10},{3,11},{4,12},{5,13},{6,14},{7,15},{8,0},{9,1},... | collective-permute-start | bytes 393224 | tf_op jit(solution)/shard_map/ppermute | solution.py:267
  35.2 6.0 %collective-permute-start.16 = (f32[2,176,128]{2,1,0:T(8,128)S(1)}, f32[2,176,128]{2,1,0:T(8,128)S(1)}, u32[]{:S(2)}, u32[]{:S(2)}) collective-permute-start(f32[2,176,128]{2,1,0:T(8,128)S(1)} %slice.20), channel_id=1, source_target_pairs={{0,4},{1,5},{2,6},{3,7},{4,0},{5,1},{6,2},{7,3},{8,12},{9,13},{10,... | collective-permute-start | bytes 540680 | tf_op jit(solution)/shard_map/ppermute | solution.py:267
  37.2 5.6 %collective-permute-start.17 = (f32[2,176,128]{2,1,0:T(8,128)S(1)}, f32[2,176,128]{2,1,0:T(8,128)S(1)}, u32[]{:S(2)}, u32[]{:S(2)}) collective-permute-start(f32[2,176,128]{2,1,0:T(8,128)S(1)} %slice.21), channel_id=1, source_target_pairs={{0,2},{1,3},{2,0},{3,1},{4,6},{5,7},{6,4},{7,5},{8,10},{9,11},{10,... | collective-permute-start | bytes 540680 | tf_op jit(solution)/shard_map/ppermute | solution.py:267
  44.5 10.6 %collective-permute-start.18 = (f32[3,4,32,256]{3,2,1,0:T(8,128)S(1)}, f32[3,4,32,256]{3,2,1,0:T(8,128)S(1)}, u32[]{:S(2)}, u32[]{:S(2)}) collective-permute-start(f32[3,4,32,256]{3,2,1,0:T(8,128)S(1)} %pad_maximum_fusion), channel_id=1, source_target_pairs={{0,4},{1,5},{2,6},{3,7},{4,0},{5,1},{6,2},{7,3},{8,12},{9,13},{10,... | collective-permute-start | bytes 1179656 | tf_op jit(solution)/shard_map/ppermute | solution.py:267
  59.8 3.0 %collective-permute-start.20 = (f32[300,1024]{1,0:T(8,128)S(1)}, f32[300,1024]{1,0:T(8,128)S(1)}, u32[]{:S(2)}, u32[]{:S(2)}) collective-permute-start(f32[300,1024]{1,0:T(8,128)S(1)} %get-tuple-element.53.mine), channel_id=1, source_target_pairs={{0,1},{1,0},{2,3},{3,2},{4,5},{5,4},{6,7},{7,6},{8,9},{9,8},{10,11... | collective-permute-start | bytes 3686408 | tf_op jit(solution)/shard_map/ppermute | solution.py:267
  62.0 2.1 %collective-permute-start.19 = (f32[128,1024]{1,0:T(8,128)S(1)}, f32[128,1024]{1,0:T(8,128)S(1)}, u32[]{:S(2)}, u32[]{:S(2)}) collective-permute-start(f32[128,1024]{1,0:T(8,128)S(1)} %shard_map.136.mine), channel_id=1, source_target_pairs={{0,1},{1,0},{2,3},{3,2},{4,5},{5,4},{6,7},{7,6},{8,9},{9,8},{10,11... | collective-permute-start | bytes 1572872 | tf_op jit(solution)/shard_map/ppermute | solution.py:267
  (6 other events, 25.7 us)

commit v4 on v3

--- a/solution.py
+++ b/solution.py
@@ -331,20 +331,21 @@
     )
     own = jnp.stack([mine, send(other, 1), send(mine, 2), send(other, 3)])
     facing = send(own, 4)
-    ring = [send(own, m) for m in (8, 16, 24)]
+    ring = [send(own, m) for m in (24, 16)]
+    near_line = send(own, 8)
     mid_rows = hidden // owners
     begun = call(
         functools.partial(forward_kernel, mid_rows),
         (
-            jax.ShapeDtypeStruct((2 * half, mid_rows), BF16),
-            jax.ShapeDtypeStruct((2 * half, hidden), BF16),
-            jax.ShapeDtypeStruct((2 * half, hidden), F32),
-            jax.ShapeDtypeStruct((2 * half, hidden), F32),
+            jax.ShapeDtypeStruct((3 * half, mid_rows), BF16),
+            jax.ShapeDtypeStruct((3 * half, hidden), BF16),
+            jax.ShapeDtypeStruct((3 * half, hidden), F32),
+            jax.ShapeDtypeStruct((3 * half, hidden), F32),
         ),
         [place],
-        [own, facing, w_in, w_mid],
-        micros=2.5,
-        mib=16,
+        [own, facing, near_line, w_in, w_mid],
+        micros=3.7,
+        mib=20,
     )
     orders = ((0, 4, 8, 12), (2, 6, 10, 14), (1, 5, 9, 13), (3, 7), (11, 15))
     arranged, slot_rows = call(
@@ -360,6 +361,8 @@
             pltpu.VMEM((devices // 2, rows, width), F32),
         ],
     )
+    near_ready, *begun = lax.optimization_barrier((near_line, *begun))
+    near_across = send(near_ready, 4)
     *ring, gate, slot_rows = lax.optimization_barrier((*ring, begun[0], slot_rows))
     begun = (gate, *begun[1:])
     last = send(jnp.stack(ring), 4)
@@ -372,7 +375,7 @@
     batch_shape = jax.ShapeDtypeStruct((feats, width), F32)
 
     def train(before, sources, masks, states, finish, mib):
-        fresh = half * (len(masks) - 2 * bool(states))
+        fresh = half * (len(masks) - 3 * bool(states))
         rows = half * len(masks)
         rest = (
             (in_shape,)
@@ -392,9 +395,11 @@
             mib=mib,
         )
 
-    grads_before, batch_before, in_before = train((), [own, facing, *ring], (0, 1, 2, 4, 6), begun, True, 32)
+    grads_before, batch_before, in_before = train(
+        (), [own, facing, near_line, *ring], (0, 1, 2, 6, 4), begun, True, 32
+    )
     grads, batch_features, *rest = train(
-        (grads_before, batch_before), [last[0], last[1], last[2]], (3, 5, 7), (), False, 20
+        (grads_before, batch_before), [near_across, last[0], last[1]], (3, 7, 5), (), False, 20
     )
     theirs = send(grads, 1)
     grad_in = call(last_kernel, in_shape, [], [in_before, *rest, w_mid], micros=2.5, mib=12)

time: 65.1 us -> 64.2 us (0.986)
  waiting for transfers between devices: 8.71 us -> 7.68 us
    ppermute x19 -> x20, waiting for transfers between devices: 7.4 us -> 6.37 us  [exchanged(): return lax.ppermute(value, AXES, [(i, i ^ mask) for i in range(devices)])]
    ppermute x19 -> x20, starting transfers between devices: 19.1 us -> 19 us  [exchanged(): return lax.ppermute(value, AXES, [(i, i ^ mask) for i in range(devices)])]
  transfers between devices with their start and end apart: 21 -> 22, of which waited for: 8 -> 8; matrix products, arithmetic and copies ran while one was open for 0% -> 0% of each run, Pallas kernels for 31% -> 32%
where the time goes in v4:
time: 64.2 us; the launch traced here: 64 us
  starting transfers between devices  27 us (42%)
  Pallas kernels  26.1 us (41%)
  waiting for transfers between devices  7.68 us (12%)
  local copies, waits for them, and re-layouts  1.54 us (2%)
  between operations  1.52 us (2%)
    pallas_call x10, Pallas kernels, call(): pl.pallas_call(kernel, out_shape=outs, in_specs=[SMEM] * len(scalars) + [...  26.1 us
    ppermute x20, starting transfers between devices, exchanged(): return lax.ppermute(value, AXES, [(i, i ^ mask) for i in range(devices)])  19 us
    ppermute x2, starting transfers between devices, far(): return lax.ppermute(value, AXES, far_pairs)  8.01 us
    ppermute x20, waiting for transfers between devices, exchanged(): return lax.ppermute(value, AXES, [(i, i ^ mask) for i in range(devices)])  6.37 us
    unnamed x18, local copies, waits for them, and re-layouts  1.5 us
    ppermute x2, waiting for transfers between devices, far(): return lax.ppermute(value, AXES, far_pairs)  1.3 us
  transfers between devices with their start and end apart: 22, of which 8 were waited for; matrix products, arithmetic and copies ran while one was open for 0% of the time, Pallas kernels for 32%

profile of v4, /device:TPU:0, one launch (start us, length us, event | category | flops | bytes accessed | tf_op | source)
XLA Modules:
  0.0 64.0 jit_solution(14658895606566529981)
XLA Ops:
  0.6 6.0 %collective-permute-start.1 = (f32[32,512]{1,0:T(8,128)}, f32[32,512]{1,0:T(8,128)S(1)}, u32[]{:S(2)}, u32[]{:S(2)}) collective-permute-start(f32[32,512]{1,0:T(8,128)} %features.1), channel_id=1, source_target_pairs={{0,28},{1,29},{2,30},{3,31},{4,8},{5,9},{6,10},{7,11},{8,4},{9,5},... | collective-permute-start | bytes 196616 | tf_op jit(solution)/shard_map/ppermute | solution.py:292
  8.2 1.2 %shard_map.130 = (f32[176,128]{1,0:T(8,128)S(1)}, s32[1,512]{1,0:T(1,128)S(1)}) custom-call(s32[2]{0:T(128)S(1)} %pad_add_fusion.place, s32[1,512]{1,0:T(1,128)S(1)} %bitcast.21, bf16[172,128]{1,0:T(8,128)(2,1)S(1)} %copy-done.5), custom_call_target="tpu_custom_call" | custom-call | flops 1500000000 | bytes 5400000 | tf_op jit(solution)/shard_map/pallas_call | solution.py:255
  10.1 0.9 %collective-permute-start.12 = (f32[176,128]{1,0:T(8,128)S(1)}, f32[176,128]{1,0:T(8,128)S(1)}, u32[]{:S(2)}, u32[]{:S(2)}) collective-permute-start(f32[176,128]{1,0:T(8,128)S(1)} %get-tuple-element.43), channel_id=1, source_target_pairs={{0,16},{1,17},{2,18},{3,19},{4,20},{5,21},{6,22},{7,23},{8,24},{9,... | collective-permute-start | bytes 270344 | tf_op jit(solution)/shard_map/ppermute | solution.py:267
  11.0 2.8 %collective-permute-start.11 = (f32[176,128]{1,0:T(8,128)S(1)}, f32[176,128]{1,0:T(8,128)S(1)}, u32[]{:S(2)}, u32[]{:S(2)}) collective-permute-start(f32[176,128]{1,0:T(8,128)S(1)} %get-tuple-element.43), channel_id=1, source_target_pairs={{0,8},{1,9},{2,10},{3,11},{4,12},{5,13},{6,14},{7,15},{8,0},{9,1},... | collective-permute-start | bytes 270344 | tf_op jit(solution)/shard_map/ppermute | solution.py:267
  14.6 1.5 %shard_map.129.own = f32[32,512]{1,0:T(8,128)S(1)} custom-call(s32[2]{0:T(128)S(1)} %pad_add_fusion.place, s32[1]{0:T(128)S(6)} %copy.14.live, s32[40]{0:T(128)S(1)} %copy-done.7, s32[40]{0:T(128)S(1)} %copy-done.8, f32[32,512]{1,0:T(8,128)S(1)} %copy-done.4, f32[32,512]{1,0:T(8,128)S(1)} %collective-permute-done.near, ...), custom_call_target="tpu_custom_call" | custom-call | flops 1500000000 | bytes 5400000 | tf_op jit(solution)/shard_map/pallas_call | solution.py:255
  16.1 2.0 %collective-permute-start.3 = (f32[32,512]{1,0:T(8,128)S(1)}, f32[32,512]{1,0:T(8,128)S(1)}, u32[]{:S(2)}, u32[]{:S(2)}) collective-permute-start(f32[32,512]{1,0:T(8,128)S(1)} %shard_map.129.own), channel_id=1, source_target_pairs={{0,28},{1,29},{2,30},{3,31},{4,8},{5,9},{6,10},{7,11},{8,4},{9,5},... | collective-permute-start | bytes 196616 | tf_op jit(solution)/shard_map/ppermute | solution.py:292
  18.3 1.7 %collective-permute-done.12 = f32[176,128]{1,0:T(8,128)S(1)} collective-permute-done((f32[176,128]{1,0:T(8,128)S(1)}, f32[176,128]{1,0:T(8,128)S(1)}, u32[]{:S(2)}, u32[]{:S(2)}) %collective-permute-start.12) | collective-permute-done | bytes 90144 | tf_op jit(solution)/shard_map/ppermute | solution.py:267
  20.0 1.6 %collective-permute-start.15 = (f32[4,176,128]{2,1,0:T(8,128)S(1)}, f32[4,176,128]{2,1,0:T(8,128)S(1)}, u32[]{:S(2)}, u32[]{:S(2)}) collective-permute-start(f32[4,176,128]{2,1,0:T(8,128)S(1)} %pad_maximum_fusion.refs_0_), channel_id=1, source_target_pairs={{0,2},{1,3},{2,0},{3,1},{4,6},{5,7},{6,4},{7,5},{8,10},{9,11},{10,... | collective-permute-start | bytes 1081352 | tf_op jit(solution)/shard_map/ppermute | solution.py:267
  21.9 1.3 %collective-permute-done.3.far = f32[32,512]{1,0:T(8,128)S(1)} collective-permute-done((f32[32,512]{1,0:T(8,128)S(1)}, f32[32,512]{1,0:T(8,128)S(1)}, u32[]{:S(2)}, u32[]{:S(2)}) %collective-permute-start.3) | collective-permute-done | bytes 65568 | tf_op jit(solution)/shard_map/ppermute | solution.py:292
  23.2 1.7 %shard_map.131 = (f32[32,256]{1,0:T(8,128)S(1)}, f32[32,256]{1,0:T(8,128)S(1)}) custom-call(s32[2]{0:T(128)S(1)} %pad_add_fusion.place, s32[1]{0:T(128)S(6)} %copy.14.live, s32[40]{0:T(128)S(1)} %copy-done.7, s32[40]{0:T(128)S(1)} %copy-done.8, f32[32,512]{1,0:T(8,128)S(1)} %shard_map.129.own, f32[32,512]{1,0:T(8,128)S(1)} %collective-permute-done.2.near, ...), custom_call_target="tpu_custom_call" | custom-call | flops 1500000000 | bytes 5400000 | tf_op jit(solution)/shard_map/pallas_call | solution.py:255
  24.9 2.1 %collective-permute-start.5 = (f32[32,256]{1,0:T(8,128)S(1)}, f32[32,256]{1,0:T(8,128)S(1)}, u32[]{:S(2)}, u32[]{:S(2)}) collective-permute-start(f32[32,256]{1,0:T(8,128)S(1)} %get-tuple-element.36), channel_id=1, source_target_pairs={{0,2},{1,3},{2,0},{3,1},{4,6},{5,7},{6,4},{7,5},{8,10},{9,11},{10,... | collective-permute-start | bytes 98312 | tf_op jit(solution)/shard_map/ppermute | solution.py:267
  27.2 2.7 %collective-permute-done.5 = f32[32,256]{1,0:T(8,128)S(1)} collective-permute-done((f32[32,256]{1,0:T(8,128)S(1)}, f32[32,256]{1,0:T(8,128)S(1)}, u32[]{:S(2)}, u32[]{:S(2)}) %collective-permute-start.5) | collective-permute-done | bytes 32800 | tf_op jit(solution)/shard_map/ppermute | solution.py:267
  30.6 0.8 %collective-permute-start.8 = (f32[4,32,256]{2,1,0:T(8,128)S(1)}, f32[4,32,256]{2,1,0:T(8,128)S(1)}, u32[]{:S(2)}, u32[]{:S(2)}) collective-permute-start(f32[4,32,256]{2,1,0:T(8,128)S(1)} %pad_maximum_fusion.2.refs_0_), channel_id=1, source_target_pairs={{0,8},{1,9},{2,10},{3,11},{4,12},{5,13},{6,14},{7,15},{8,0},{9,1},... | collective-permute-start | bytes 393224 | tf_op jit(solution)/shard_map/ppermute | solution.py:267
  31.6 2.7 %collective-permute-start.10 = (f32[4,32,256]{2,1,0:T(8,128)S(1)}, f32[4,32,256]{2,1,0:T(8,128)S(1)}, u32[]{:S(2)}, u32[]{:S(2)}) collective-permute-start(f32[4,32,256]{2,1,0:T(8,128)S(1)} %pad_maximum_fusion.2.refs_0_), channel_id=1, source_target_pairs={{0,16},{1,17},{2,18},{3,19},{4,20},{5,21},{6,22},{7,23},{8,24},{9,... | collective-permute-start | bytes 393224 | tf_op jit(solution)/shard_map/ppermute | solution.py:267
  35.1 2.1 %collective-permute-start.16 = (f32[2,176,128]{2,1,0:T(8,128)S(1)}, f32[2,176,128]{2,1,0:T(8,128)S(1)}, u32[]{:S(2)}, u32[]{:S(2)}) collective-permute-start(f32[2,176,128]{2,1,0:T(8,128)S(1)} %slice.16), channel_id=1, source_target_pairs={{0,4},{1,5},{2,6},{3,7},{4,0},{5,1},{6,2},{7,3},{8,12},{9,13},{10,... | collective-permute-start | bytes 540680 | tf_op jit(solution)/shard_map/ppermute | solution.py:267
  37.6 1.4 %collective-permute-start.17 = (f32[2,176,128]{2,1,0:T(8,128)S(1)}, f32[2,176,128]{2,1,0:T(8,128)S(1)}, u32[]{:S(2)}, u32[]{:S(2)}) collective-permute-start(f32[2,176,128]{2,1,0:T(8,128)S(1)} %slice.17), channel_id=1, source_target_pairs={{0,2},{1,3},{2,0},{3,1},{4,6},{5,7},{6,4},{7,5},{8,10},{9,11},{10,... | collective-permute-start | bytes 540680 | tf_op jit(solution)/shard_map/ppermute | solution.py:267
  39.0 3.7 %shard_map.132 = (bf16[768,128]{1,0:T(8,128)(2,1)S(1)}, bf16[768,1024]{1,0:T(8,128)(2,1)S(1)}, f32[768,1024]{1,0:T(8,128)S(1)}, f32[768,1024]{1,0:T(8,128)S(1)}) custom-call(s32[2]{0:T(128)S(1)} %pad_add_fusion.place, f32[4,32,256]{2,1,0:T(8,128)S(1)} %pad_maximum_fusion.2.refs_0_, f32[4,32,256]{2,1,0:T(8,128)S(1)} %collective-permute-done.7.refs_1_, ...), custom_call_target="tpu_custom_call" | custom-call | flops 3700000000 | bytes 13320000 | tf_op jit(solution)/shard_map/pallas_call | solution.py:255
  43.4 1.3 %shard_map.133 = (bf16[8,256,172]{2,1,0:T(8,128)(2,1)S(1)}, f32[8,1,256]{2,1,0:T(1,128)S(1)}) custom-call(s32[2]{0:T(128)S(1)} %pad_add_fusion.place, f32[4,176,128]{2,1,0:T(8,128)S(1)} %pad_maximum_fusion.refs_0_, f32[4,176,128]{2,1,0:T(8,128)S(1)} %collective-permute-done.14.refs_1_, f32[4,176,128]{2,1,0:T(8,128)S(1)} %collective-permute-done.15.refs_2_, ...), custom_call_target="tpu_custom_call" | custom-call | flops 1500000000 | bytes 5400000 | tf_op jit(solution)/shard_map/pallas_call | solution.py:255
  44.7 1.5 %collective-permute-start.19 = (f32[2,4,32,256]{3,2,1,0:T(8,128)S(1)}, f32[2,4,32,256]{3,2,1,0:T(8,128)S(1)}, u32[]{:S(2)}, u32[]{:S(2)}) collective-permute-start(f32[2,4,32,256]{3,2,1,0:T(8,128)S(1)} %pad_maximum_fusion.1), channel_id=1, source_target_pairs={{0,4},{1,5},{2,6},{3,7},{4,0},{5,1},{6,2},{7,3},{8,12},{9,13},{10,... | collective-permute-start | bytes 786440 | tf_op jit(solution)/shard_map/ppermute | solution.py:267
  46.2 7.9 %shard_map.134 = (f32[300,1024]{1,0:T(8,128)S(1)}, f32[128,128]{1,0:T(8,128)S(1)}, f32[128,1024]{1,0:T(8,128)S(1)}) custom-call(s32[2]{0:T(128)S(1)} %pad_add_fusion.place, f32[4,32,256]{2,1,0:T(8,128)S(1)} %pad_maximum_fusion.2.refs_0_, f32[4,32,256]{2,1,0:T(8,128)S(1)} %collective-permute-done.7.refs_1_, f32[4,32,256]{2,1,0:T(8,128)S(1)} %collective-permute-done.8.refs_2_, ...), custom_call_target="tpu_custom_call" | custom-call | flops 12499999744 | bytes 45000000 | tf_op jit(solution)/shard_map/pallas_call | solution.py:255
  54.2 4.6 %shard_map.135 = (f32[300,1024]{1,0:T(8,128)S(1)}, f32[128,128]{1,0:T(8,128)}, bf16[128,768]{1,0:T(8,128)(2,1)S(1)}, bf16[768,1024]{1,0:T(8,128)(2,1)S(1)}, f32[768,1024]{1,0:T(8,128)S(1)}) custom-call(s32[2]{0:T(128)S(1)} %pad_add_fusion.place, f32[300,1024]{1,0:T(8,128)S(1)} %get-tuple-element.53.refs_0_, f32[128,128]{1,0:T(8,128)S(1)} %get-tuple-element.54.refs_1_, ...), custom_call_target="tpu_custom_call" | custom-call | flops 7500000256 | bytes 27000000 | tf_op jit(solution)/shard_map/pallas_call | solution.py:255
  58.9 2.1 %shard_map.136.mine = f32[128,1024]{1,0:T(8,128)S(1)} custom-call(f32[128,1024]{1,0:T(8,128)S(1)} %get-tuple-element.57.before, bf16[128,768]{1,0:T(8,128)(2,1)S(1)} %get-tuple-element.58.inputs, bf16[768,1024]{1,0:T(8,128)(2,1)S(1)} %get-tuple-element.59.delta_two, f32[768,1024]{1,0:T(8,128)S(1)} %get-tuple-element.60.slope_one, bf16[1024,1024]{1,0:T(8,128)(2,1)S(1)} %copy-done), custom_call_target="tpu_custom_call" | custom-call | flops 2500000000 | bytes 9000000 | tf_op jit(solution)/shard_map/pallas_call | solution.py:255
  61.9 1.2 %shard_map.137 = (f32[128,1024]{1,0:T(8,128)}, f32[172,1024]{1,0:T(8,128)}) custom-call(f32[300,1024]{1,0:T(8,128)S(1)} %get-tuple-element.61.mine, f32[300,1024]{1,0:T(8,128)S(1)} %collective-permute-done.21.theirs), custom_call_target="tpu_custom_call" | custom-call | flops 1500000000 | bytes 5400000 | tf_op jit(solution)/shard_map/pallas_call | solution.py:255
  63.1 0.8 %shard_map.138 = f32[128,1024]{1,0:T(8,128)} custom-call(f32[128,1024]{1,0:T(8,128)S(1)} %shard_map.136.mine, f32[128,1024]{1,0:T(8,128)S(1)} %collective-permute-done.20.theirs), custom_call_target="tpu_custom_call" | custom-call | flops 1500000000 | bytes 5400000 | tf_op jit(solution)/shard_map/pallas_call | solution.py:255
  (55 shorter events, 6.6 us)
Async XLA Ops:
  0.6 13.9 %collective-permute-start.1 = (f32[32,512]{1,0:T(8,128)}, f32[32,512]{1,0:T(8,128)S(1)}, u32[]{:S(2)}, u32[]{:S(2)}) collective-permute-start(f32[32,512]{1,0:T(8,128)} %features.1), channel_id=1, source_target_pairs={{0,28},{1,29},{2,30},{3,31},{4,8},{5,9},{6,10},{7,11},{8,4},{9,5},... | collective-permute-start | bytes 196616 | tf_op jit(solution)/shard_map/ppermute | solution.py:292
  6.7 7.9 %collective-permute-start = (f32[32,512]{1,0:T(8,128)}, f32[32,512]{1,0:T(8,128)S(1)}, u32[]{:S(2)}, u32[]{:S(2)}) collective-permute-start(f32[32,512]{1,0:T(8,128)} %features.1), channel_id=1, source_target_pairs={{0,4},{1,5},{2,6},{3,7},{4,0},{5,1},{6,2},{7,3},{8,12},{9,13},{10,... | collective-permute-start | bytes 196616 | tf_op jit(solution)/shard_map/ppermute | solution.py:267
  9.4 8.9 %collective-permute-start.13 = (f32[176,128]{1,0:T(8,128)S(1)}, f32[176,128]{1,0:T(8,128)S(1)}, u32[]{:S(2)}, u32[]{:S(2)}) collective-permute-start(f32[176,128]{1,0:T(8,128)S(1)} %get-tuple-element.43), channel_id=1, source_target_pairs={{0,24},{1,25},{2,26},{3,27},{4,28},{5,29},{6,30},{7,31},{8,16},{9,... | collective-permute-start | bytes 270344 | tf_op jit(solution)/shard_map/ppermute | solution.py:267
  10.1 9.8 %collective-permute-start.12 = (f32[176,128]{1,0:T(8,128)S(1)}, f32[176,128]{1,0:T(8,128)S(1)}, u32[]{:S(2)}, u32[]{:S(2)}) collective-permute-start(f32[176,128]{1,0:T(8,128)S(1)} %get-tuple-element.43), channel_id=1, source_target_pairs={{0,16},{1,17},{2,18},{3,19},{4,20},{5,21},{6,22},{7,23},{8,24},{9,... | collective-permute-start | bytes 270344 | tf_op jit(solution)/shard_map/ppermute | solution.py:267
  11.0 8.9 %collective-permute-start.11 = (f32[176,128]{1,0:T(8,128)S(1)}, f32[176,128]{1,0:T(8,128)S(1)}, u32[]{:S(2)}, u32[]{:S(2)}) collective-permute-start(f32[176,128]{1,0:T(8,128)S(1)} %get-tuple-element.43), channel_id=1, source_target_pairs={{0,8},{1,9},{2,10},{3,11},{4,12},{5,13},{6,14},{7,15},{8,0},{9,1},... | collective-permute-start | bytes 270344 | tf_op jit(solution)/shard_map/ppermute | solution.py:267
  16.1 7.1 %collective-permute-start.3 = (f32[32,512]{1,0:T(8,128)S(1)}, f32[32,512]{1,0:T(8,128)S(1)}, u32[]{:S(2)}, u32[]{:S(2)}) collective-permute-start(f32[32,512]{1,0:T(8,128)S(1)} %shard_map.129.own), channel_id=1, source_target_pairs={{0,28},{1,29},{2,30},{3,31},{4,8},{5,9},{6,10},{7,11},{8,4},{9,5},... | collective-permute-start | bytes 196616 | tf_op jit(solution)/shard_map/ppermute | solution.py:292
  18.1 5.1 %collective-permute-start.2 = (f32[32,512]{1,0:T(8,128)S(1)}, f32[32,512]{1,0:T(8,128)S(1)}, u32[]{:S(2)}, u32[]{:S(2)}) collective-permute-start(f32[32,512]{1,0:T(8,128)S(1)} %shard_map.129.own), channel_id=1, source_target_pairs={{0,4},{1,5},{2,6},{3,7},{4,0},{5,1},{6,2},{7,3},{8,12},{9,13},{10,... | collective-permute-start | bytes 196616 | tf_op jit(solution)/shard_map/ppermute | solution.py:267
  20.0 14.4 %collective-permute-start.15 = (f32[4,176,128]{2,1,0:T(8,128)S(1)}, f32[4,176,128]{2,1,0:T(8,128)S(1)}, u32[]{:S(2)}, u32[]{:S(2)}) collective-permute-start(f32[4,176,128]{2,1,0:T(8,128)S(1)} %pad_maximum_fusion.refs_0_), channel_id=1, source_target_pairs={{0,2},{1,3},{2,0},{3,1},{4,6},{5,7},{6,4},{7,5},{8,10},{9,11},{10,... | collective-permute-start | bytes 1081352 | tf_op jit(solution)/shard_map/ppermute | solution.py:267
  21.6 13.5 %collective-permute-start.14 = (f32[4,176,128]{2,1,0:T(8,128)S(1)}, f32[4,176,128]{2,1,0:T(8,128)S(1)}, u32[]{:S(2)}, u32[]{:S(2)}) collective-permute-start(f32[4,176,128]{2,1,0:T(8,128)S(1)} %pad_maximum_fusion.refs_0_), channel_id=1, source_target_pairs={{0,4},{1,5},{2,6},{3,7},{4,0},{5,1},{6,2},{7,3},{8,12},{9,13},{10,... | collective-permute-start | bytes 1081352 | tf_op jit(solution)/shard_map/ppermute | solution.py:267
  23.2 15.8 %copy-start = (bf16[1024,1024]{1,0:T(8,128)(2,1)S(1)}, bf16[1024,1024]{1,0:T(8,128)(2,1)}, u32[]{:S(2)}) copy-start(bf16[1024,1024]{1,0:T(8,128)(2,1)} %w_mid.1) | copy-start | bytes 6291460
  23.2 15.8 %copy-start.3 = (bf16[128,1024]{1,0:T(8,128)(2,1)S(1)}, bf16[128,1024]{1,0:T(8,128)(2,1)}, u32[]{:S(2)}) copy-start(bf16[128,1024]{1,0:T(8,128)(2,1)} %refs_7_.1) | copy-start | bytes 786436
  24.9 5.0 %collective-permute-start.5 = (f32[32,256]{1,0:T(8,128)S(1)}, f32[32,256]{1,0:T(8,128)S(1)}, u32[]{:S(2)}, u32[]{:S(2)}) collective-permute-start(f32[32,256]{1,0:T(8,128)S(1)} %get-tuple-element.36), channel_id=1, source_target_pairs={{0,2},{1,3},{2,0},{3,1},{4,6},{5,7},{6,4},{7,5},{8,10},{9,11},{10,... | collective-permute-start | bytes 98312 | tf_op jit(solution)/shard_map/ppermute | solution.py:267
  27.0 3.6 %collective-permute-start.6 = (f32[32,256]{1,0:T(8,128)S(1)}, f32[32,256]{1,0:T(8,128)S(1)}, u32[]{:S(2)}, u32[]{:S(2)}) collective-permute-start(f32[32,256]{1,0:T(8,128)S(1)} %get-tuple-element.37), channel_id=1, source_target_pairs={{0,3},{1,2},{2,1},{3,0},{4,7},{5,6},{6,5},{7,4},{8,11},{9,10},{10,... | collective-permute-start | bytes 98312 | tf_op jit(solution)/shard_map/ppermute | solution.py:267
  27.0 3.6 %collective-permute-start.4 = (f32[32,256]{1,0:T(8,128)S(1)}, f32[32,256]{1,0:T(8,128)S(1)}, u32[]{:S(2)}, u32[]{:S(2)}) collective-permute-start(f32[32,256]{1,0:T(8,128)S(1)} %get-tuple-element.37), channel_id=1, source_target_pairs={{0,1},{1,0},{2,3},{3,2},{4,5},{5,4},{6,7},{7,6},{8,9},{9,8},{10,11... | collective-permute-start | bytes 98312 | tf_op jit(solution)/shard_map/ppermute | solution.py:267
  30.6 6.9 %collective-permute-start.8 = (f32[4,32,256]{2,1,0:T(8,128)S(1)}, f32[4,32,256]{2,1,0:T(8,128)S(1)}, u32[]{:S(2)}, u32[]{:S(2)}) collective-permute-start(f32[4,32,256]{2,1,0:T(8,128)S(1)} %pad_maximum_fusion.2.refs_0_), channel_id=1, source_target_pairs={{0,8},{1,9},{2,10},{3,11},{4,12},{5,13},{6,14},{7,15},{8,0},{9,1},... | collective-permute-start | bytes 393224 | tf_op jit(solution)/shard_map/ppermute | solution.py:267
  31.5 7.5 %collective-permute-start.7 = (f32[4,32,256]{2,1,0:T(8,128)S(1)}, f32[4,32,256]{2,1,0:T(8,128)S(1)}, u32[]{:S(2)}, u32[]{:S(2)}) collective-permute-start(f32[4,32,256]{2,1,0:T(8,128)S(1)} %pad_maximum_fusion.2.refs_0_), channel_id=1, source_target_pairs={{0,4},{1,5},{2,6},{3,7},{4,0},{5,1},{6,2},{7,3},{8,12},{9,13},{10,... | collective-permute-start | bytes 393224 | tf_op jit(solution)/shard_map/ppermute | solution.py:267
  31.6 13.0 %collective-permute-start.10 = (f32[4,32,256]{2,1,0:T(8,128)S(1)}, f32[4,32,256]{2,1,0:T(8,128)S(1)}, u32[]{:S(2)}, u32[]{:S(2)}) collective-permute-start(f32[4,32,256]{2,1,0:T(8,128)S(1)} %pad_maximum_fusion.2.refs_0_), channel_id=1, source_target_pairs={{0,16},{1,17},{2,18},{3,19},{4,20},{5,21},{6,22},{7,23},{8,24},{9,... | collective-permute-start | bytes 393224 | tf_op jit(solution)/shard_map/ppermute | solution.py:267
  34.4 10.3 %collective-permute-start.9 = (f32[4,32,256]{2,1,0:T(8,128)S(1)}, f32[4,32,256]{2,1,0:T(8,128)S(1)}, u32[]{:S(2)}, u32[]{:S(2)}) collective-permute-start(f32[4,32,256]{2,1,0:T(8,128)S(1)} %pad_maximum_fusion.2.refs_0_), channel_id=1, source_target_pairs={{0,24},{1,25},{2,26},{3,27},{4,28},{5,29},{6,30},{7,31},{8,16},{9,... | collective-permute-start | bytes 393224 | tf_op jit(solution)/shard_map/ppermute | solution.py:267
  35.1 7.7 %collective-permute-start.16 = (f32[2,176,128]{2,1,0:T(8,128)S(1)}, f32[2,176,128]{2,1,0:T(8,128)S(1)}, u32[]{:S(2)}, u32[]{:S(2)}) collective-permute-start(f32[2,176,128]{2,1,0:T(8,128)S(1)} %slice.16), channel_id=1, source_target_pairs={{0,4},{1,5},{2,6},{3,7},{4,0},{5,1},{6,2},{7,3},{8,12},{9,13},{10,... | collective-permute-start | bytes 540680 | tf_op jit(solution)/shard_map/ppermute | solution.py:267
  37.6 5.8 %collective-permute-start.17 = (f32[2,176,128]{2,1,0:T(8,128)S(1)}, f32[2,176,128]{2,1,0:T(8,128)S(1)}, u32[]{:S(2)}, u32[]{:S(2)}) collective-permute-start(f32[2,176,128]{2,1,0:T(8,128)S(1)} %slice.17), channel_id=1, source_target_pairs={{0,2},{1,3},{2,0},{3,1},{4,6},{5,7},{6,4},{7,5},{8,10},{9,11},{10,... | collective-permute-start | bytes 540680 | tf_op jit(solution)/shard_map/ppermute | solution.py:267
  42.7 11.5 %collective-permute-start.18 = (f32[4,32,256]{2,1,0:T(8,128)S(1)}, f32[4,32,256]{2,1,0:T(8,128)S(1)}, u32[]{:S(2)}, u32[]{:S(2)}) collective-permute-start(f32[4,32,256]{2,1,0:T(8,128)S(1)} %collective-permute-done.8.refs_2_), channel_id=1, source_target_pairs={{0,4},{1,5},{2,6},{3,7},{4,0},{5,1},{6,2},{7,3},{8,12},{9,13},{10,... | collective-permute-start | bytes 393224 | tf_op jit(solution)/shard_map/ppermute | solution.py:267
  44.7 9.5 %collective-permute-start.19 = (f32[2,4,32,256]{3,2,1,0:T(8,128)S(1)}, f32[2,4,32,256]{3,2,1,0:T(8,128)S(1)}, u32[]{:S(2)}, u32[]{:S(2)}) collective-permute-start(f32[2,4,32,256]{3,2,1,0:T(8,128)S(1)} %pad_maximum_fusion.1), channel_id=1, source_target_pairs={{0,4},{1,5},{2,6},{3,7},{4,0},{5,1},{6,2},{7,3},{8,12},{9,13},{10,... | collective-permute-start | bytes 786440 | tf_op jit(solution)/shard_map/ppermute | solution.py:267
  58.9 3.0 %collective-permute-start.21 = (f32[300,1024]{1,0:T(8,128)S(1)}, f32[300,1024]{1,0:T(8,128)S(1)}, u32[]{:S(2)}, u32[]{:S(2)}) collective-permute-start(f32[300,1024]{1,0:T(8,128)S(1)} %get-tuple-element.61.mine), channel_id=1, source_target_pairs={{0,1},{1,0},{2,3},{3,2},{4,5},{5,4},{6,7},{7,6},{8,9},{9,8},{10,11... | collective-permute-start | bytes 3686408 | tf_op jit(solution)/shard_map/ppermute | solution.py:267
  61.0 2.1 %collective-permute-start.20 = (f32[128,1024]{1,0:T(8,128)S(1)}, f32[128,1024]{1,0:T(8,128)S(1)}, u32[]{:S(2)}, u32[]{:S(2)}) collective-permute-start(f32[128,1024]{1,0:T(8,128)S(1)} %shard_map.136.mine), channel_id=1, source_target_pairs={{0,1},{1,0},{2,3},{3,2},{4,5},{5,4},{6,7},{7,6},{8,9},{9,8},{10,11... | collective-permute-start | bytes 1572872 | tf_op jit(solution)/shard_map/ppermute | solution.py:267
  (7 other events, 30.4 us)

commit v5 on v4

--- a/solution.py
+++ b/solution.py
@@ -32,7 +32,11 @@
     return parts[:rows] + parts[rows : 2 * rows] + parts[2 * rows :]
 
 
-def prepare_kernel(segment, block, place, slots_hbm, cot_hbm, packed, rank_row, slots, cot, sems):
+def open_kernel(place, out):
+    out[...] = jnp.full(out.shape, place[0], F32)
+
+
+def prepare_kernel(segment, block, place, slots_hbm, cot_hbm, opened, packed, rank_row, slots, cot, sems):
     fetch_slots = pltpu.make_async_copy(slots_hbm, slots, sems.at[0])
     fetch_cot = pltpu.make_async_copy(cot_hbm, cot, sems.at[1])
     fetch_slots.start()
@@ -293,7 +297,9 @@
 
     rows = half // width
     padded = classes + rows + (-(classes + rows)) % 8
-    near_one, far_one = send(features, replicas), far(features)
+    opened = call(open_kernel, jax.ShapeDtypeStruct((8, 128), F32), [place], [], micros=4.0)
+    opened, ready = lax.optimization_barrier((opened, features))
+    near_one, far_one = send(ready, replicas), far(ready)
     packed, rank_row = call(
         functools.partial(prepare_kernel, segment, width),
         (
@@ -301,7 +307,7 @@
             jax.ShapeDtypeStruct((1, node_count), jnp.int32),
         ),
         [place],
-        [dest_slot.reshape(1, -1), cotangent],
+        [dest_slot.reshape(1, -1), cotangent, opened],
         [
             pltpu.VMEM((1, node_count), jnp.int32),
             pltpu.VMEM((classes, width), BF16),
@@ -320,8 +326,9 @@
     line = [packed] + [send(packed, m) for m in (8, 16, 24)]
     column = jnp.stack(line)
     near_two, far_two = send(first, replicas), far(first)
-    across_x, across_y = send(column, 4), send(column, 2)
-    corner_one, corner_two = send(across_y[0:2], 4), send(across_x[2:4], 2)
+    across_x, across_y = send(column, 4), send(column[0:3], 2)
+    corner_one = send(across_y, 4)
+    corner_two = send(jnp.concatenate([column[3:4], across_x[3:4]]), 2)
     mine, other = call(
         functools.partial(second_kernel, owners),
         tuple(jax.ShapeDtypeStruct((feature_count, half), F32) for _ in range(2)),
@@ -347,7 +354,7 @@
         micros=3.7,
         mib=20,
     )
-    orders = ((0, 4, 8, 12), (2, 6, 10, 14), (1, 5, 9, 13), (3, 7), (11, 15))
+    orders = ((0, 4, 8, 12), (2, 6, 10, 14), (1, 5, 9), (3, 7, 11), (13, 15))
     arranged, slot_rows = call(
         functools.partial(cotangent_kernel, orders, classes, segment),
         (

time: 64.2 us -> 62.9 us (0.980)
  local copies, waits for them, and re-layouts: 1.54 us -> 0.35 us
  waiting for transfers between devices: 7.68 us -> 6.8 us
    unnamed x18, local copies, waits for them, and re-layouts: 1.5 us -> 0.32 us
    ppermute x20, waiting for transfers between devices: 6.37 us -> 5.5 us  [exchanged(): return lax.ppermute(value, AXES, [(i, i ^ mask) for i in range(devices)])]
    pallas_call x10 -> x11, Pallas kernels: 26.1 us -> 26.7 us  [call(): pl.pallas_call(kernel, out_shape=outs, in_specs=[SMEM] * len(scalars) + [...]
  transfers between devices with their start and end apart: 22 -> 22, of which waited for: 8 -> 8; matrix products, arithmetic and copies ran while one was open for 0% -> 0% of each run, Pallas kernels for 32% -> 33%
where the time goes in v5:
time: 62.9 us; the launch traced here: 62.7 us
  starting transfers between devices  27.2 us (43%)
  Pallas kernels  26.7 us (42%)
  waiting for transfers between devices  6.8 us (11%)
  between operations  1.51 us (2%)
    pallas_call x11, Pallas kernels, call(): pl.pallas_call(kernel, out_shape=outs, in_specs=[SMEM] * len(scalars) + [...  26.7 us
    ppermute x20, starting transfers between devices, exchanged(): return lax.ppermute(value, AXES, [(i, i ^ mask) for i in range(devices)])  19.3 us
    ppermute x2, starting transfers between devices, far(): return lax.ppermute(value, AXES, far_pairs)  7.93 us
    ppermute x20, waiting for transfers between devices, exchanged(): return lax.ppermute(value, AXES, [(i, i ^ mask) for i in range(devices)])  5.5 us
    ppermute x2, waiting for transfers between devices, far(): return lax.ppermute(value, AXES, far_pairs)  1.3 us
  transfers between devices with their start and end apart: 22, of which 8 were waited for; matrix products, arithmetic and copies ran while one was open for 0% of the time, Pallas kernels for 33%

profile of v5, /device:TPU:0, one launch (start us, length us, event | category | flops | bytes accessed | tf_op | source)
XLA Modules:
  0.0 62.7 jit_solution(7122127244096097370)
XLA Ops:
  1.6 6.0 %collective-permute-start.1 = (f32[32,512]{1,0:T(8,128)S(1)}, f32[32,512]{1,0:T(8,128)S(1)}, u32[]{:S(2)}, u32[]{:S(2)}) collective-permute-start(f32[32,512]{1,0:T(8,128)S(1)} %copy-done.4), channel_id=1, source_target_pairs={{0,28},{1,29},{2,30},{3,31},{4,8},{5,9},{6,10},{7,11},{8,4},{9,5},... | collective-permute-start | bytes 196616 | tf_op jit(solution)/shard_map/ppermute | solution.py:296
  7.6 1.2 %shard_map.131 = (f32[176,128]{1,0:T(8,128)S(1)}, s32[1,512]{1,0:T(1,128)S(1)}) custom-call(s32[2]{0:T(128)S(1)} %pad_add_fusion.place, s32[1,512]{1,0:T(1,128)S(1)} %bitcast.22, bf16[172,128]{1,0:T(8,128)(2,1)S(1)} %copy-done.5, f32[8,128]{1,0:T(8,128)S(1)} %shard_map.129.opened), custom_call_target="tpu_custom_call" | custom-call | flops 1500000000 | bytes 5400000 | tf_op jit(solution)/shard_map/pallas_call | solution.py:259
  9.4 1.0 %collective-permute-start.12 = (f32[176,128]{1,0:T(8,128)S(1)}, f32[176,128]{1,0:T(8,128)S(1)}, u32[]{:S(2)}, u32[]{:S(2)}) collective-permute-start(f32[176,128]{1,0:T(8,128)S(1)} %get-tuple-element.47), channel_id=1, source_target_pairs={{0,16},{1,17},{2,18},{3,19},{4,20},{5,21},{6,22},{7,23},{8,24},{9,... | collective-permute-start | bytes 270344 | tf_op jit(solution)/shard_map/ppermute | solution.py:271
  10.4 2.9 %collective-permute-start.11 = (f32[176,128]{1,0:T(8,128)S(1)}, f32[176,128]{1,0:T(8,128)S(1)}, u32[]{:S(2)}, u32[]{:S(2)}) collective-permute-start(f32[176,128]{1,0:T(8,128)S(1)} %get-tuple-element.47), channel_id=1, source_target_pairs={{0,8},{1,9},{2,10},{3,11},{4,12},{5,13},{6,14},{7,15},{8,0},{9,1},... | collective-permute-start | bytes 270344 | tf_op jit(solution)/shard_map/ppermute | solution.py:271
  13.9 1.5 %shard_map.130.own = f32[32,512]{1,0:T(8,128)S(1)} custom-call(s32[2]{0:T(128)S(1)} %pad_add_fusion.place, s32[1]{0:T(128)S(6)} %copy.14.live, s32[40]{0:T(128)S(1)} %copy-done.7, s32[40]{0:T(128)S(1)} %copy-done.8, f32[32,512]{1,0:T(8,128)S(1)} %copy-done.4, f32[32,512]{1,0:T(8,128)S(1)} %collective-permute-done.near, ...), custom_call_target="tpu_custom_call" | custom-call | flops 1500000000 | bytes 5400000 | tf_op jit(solution)/shard_map/pallas_call | solution.py:259
  15.4 2.0 %collective-permute-start.3 = (f32[32,512]{1,0:T(8,128)S(1)}, f32[32,512]{1,0:T(8,128)S(1)}, u32[]{:S(2)}, u32[]{:S(2)}) collective-permute-start(f32[32,512]{1,0:T(8,128)S(1)} %shard_map.130.own), channel_id=1, source_target_pairs={{0,28},{1,29},{2,30},{3,31},{4,8},{5,9},{6,10},{7,11},{8,4},{9,5},... | collective-permute-start | bytes 196616 | tf_op jit(solution)/shard_map/ppermute | solution.py:296
  17.6 1.8 %collective-permute-done.12 = f32[176,128]{1,0:T(8,128)S(1)} collective-permute-done((f32[176,128]{1,0:T(8,128)S(1)}, f32[176,128]{1,0:T(8,128)S(1)}, u32[]{:S(2)}, u32[]{:S(2)}) %collective-permute-start.12) | collective-permute-done | bytes 90144 | tf_op jit(solution)/shard_map/ppermute | solution.py:271
  19.7 1.6 %collective-permute-start.15 = (f32[3,176,128]{2,1,0:T(8,128)S(1)}, f32[3,176,128]{2,1,0:T(8,128)S(1)}, u32[]{:S(2)}, u32[]{:S(2)}) collective-permute-start(f32[3,176,128]{2,1,0:T(8,128)S(1)} %pad_maximum_fusion.1), channel_id=1, source_target_pairs={{0,2},{1,3},{2,0},{3,1},{4,6},{5,7},{6,4},{7,5},{8,10},{9,11},{10,... | collective-permute-start | bytes 811016 | tf_op jit(solution)/shard_map/ppermute | solution.py:271
  21.3 1.3 %collective-permute-done.3.far = f32[32,512]{1,0:T(8,128)S(1)} collective-permute-done((f32[32,512]{1,0:T(8,128)S(1)}, f32[32,512]{1,0:T(8,128)S(1)}, u32[]{:S(2)}, u32[]{:S(2)}) %collective-permute-start.3) | collective-permute-done | bytes 65568 | tf_op jit(solution)/shard_map/ppermute | solution.py:296
  23.1 1.8 %shard_map.132 = (f32[32,256]{1,0:T(8,128)S(1)}, f32[32,256]{1,0:T(8,128)S(1)}) custom-call(s32[2]{0:T(128)S(1)} %pad_add_fusion.place, s32[1]{0:T(128)S(6)} %copy.14.live, s32[40]{0:T(128)S(1)} %copy-done.7, s32[40]{0:T(128)S(1)} %copy-done.8, f32[32,512]{1,0:T(8,128)S(1)} %shard_map.130.own, f32[32,512]{1,0:T(8,128)S(1)} %collective-permute-done.2.near, ...), custom_call_target="tpu_custom_call" | custom-call | flops 1500000000 | bytes 5400000 | tf_op jit(solution)/shard_map/pallas_call | solution.py:259
  24.8 1.6 %collective-permute-start.5 = (f32[32,256]{1,0:T(8,128)S(1)}, f32[32,256]{1,0:T(8,128)S(1)}, u32[]{:S(2)}, u32[]{:S(2)}) collective-permute-start(f32[32,256]{1,0:T(8,128)S(1)} %get-tuple-element.40), channel_id=1, source_target_pairs={{0,2},{1,3},{2,0},{3,1},{4,6},{5,7},{6,4},{7,5},{8,10},{9,11},{10,... | collective-permute-start | bytes 98312 | tf_op jit(solution)/shard_map/ppermute | solution.py:271
  27.0 1.8 %collective-permute-done.5 = f32[32,256]{1,0:T(8,128)S(1)} collective-permute-done((f32[32,256]{1,0:T(8,128)S(1)}, f32[32,256]{1,0:T(8,128)S(1)}, u32[]{:S(2)}, u32[]{:S(2)}) %collective-permute-start.5) | collective-permute-done | bytes 32800 | tf_op jit(solution)/shard_map/ppermute | solution.py:271
  28.8 0.9 %collective-permute-done.6 = f32[32,256]{1,0:T(8,128)S(1)} collective-permute-done((f32[32,256]{1,0:T(8,128)S(1)}, f32[32,256]{1,0:T(8,128)S(1)}, u32[]{:S(2)}, u32[]{:S(2)}) %collective-permute-start.6) | collective-permute-done | bytes 32800 | tf_op jit(solution)/shard_map/ppermute | solution.py:271
  29.8 1.0 %collective-permute-start.8 = (f32[4,32,256]{2,1,0:T(8,128)S(1)}, f32[4,32,256]{2,1,0:T(8,128)S(1)}, u32[]{:S(2)}, u32[]{:S(2)}) collective-permute-start(f32[4,32,256]{2,1,0:T(8,128)S(1)} %pad_maximum_fusion.4.refs_0_), channel_id=1, source_target_pairs={{0,8},{1,9},{2,10},{3,11},{4,12},{5,13},{6,14},{7,15},{8,0},{9,1},... | collective-permute-start | bytes 393224 | tf_op jit(solution)/shard_map/ppermute | solution.py:271
  30.9 3.1 %collective-permute-start.10 = (f32[4,32,256]{2,1,0:T(8,128)S(1)}, f32[4,32,256]{2,1,0:T(8,128)S(1)}, u32[]{:S(2)}, u32[]{:S(2)}) collective-permute-start(f32[4,32,256]{2,1,0:T(8,128)S(1)} %pad_maximum_fusion.4.refs_0_), channel_id=1, source_target_pairs={{0,16},{1,17},{2,18},{3,19},{4,20},{5,21},{6,22},{7,23},{8,24},{9,... | collective-permute-start | bytes 393224 | tf_op jit(solution)/shard_map/ppermute | solution.py:271
  34.4 1.8 %collective-permute-start.16 = (f32[3,176,128]{2,1,0:T(8,128)S(1)}, f32[3,176,128]{2,1,0:T(8,128)S(1)}, u32[]{:S(2)}, u32[]{:S(2)}) collective-permute-start(f32[3,176,128]{2,1,0:T(8,128)S(1)} %collective-permute-done.15.refs_2_), channel_id=1, source_target_pairs={{0,4},{1,5},{2,6},{3,7},{4,0},{5,1},{6,2},{7,3},{8,12},{9,13},{10,... | collective-permute-start | bytes 811016 | tf_op jit(solution)/shard_map/ppermute | solution.py:271
  36.3 1.5 %collective-permute-start.17 = (f32[2,176,128]{2,1,0:T(8,128)S(1)}, f32[2,176,128]{2,1,0:T(8,128)S(1)}, u32[]{:S(2)}, u32[]{:S(2)}) collective-permute-start(f32[2,176,128]{2,1,0:T(8,128)S(1)} %pad_maximum_fusion.3), channel_id=1, source_target_pairs={{0,2},{1,3},{2,0},{3,1},{4,6},{5,7},{6,4},{7,5},{8,10},{9,11},{10,... | collective-permute-start | bytes 540680 | tf_op jit(solution)/shard_map/ppermute | solution.py:271
  37.7 3.7 %shard_map.133 = (bf16[768,128]{1,0:T(8,128)(2,1)S(1)}, bf16[768,1024]{1,0:T(8,128)(2,1)S(1)}, f32[768,1024]{1,0:T(8,128)S(1)}, f32[768,1024]{1,0:T(8,128)S(1)}) custom-call(s32[2]{0:T(128)S(1)} %pad_add_fusion.place, f32[4,32,256]{2,1,0:T(8,128)S(1)} %pad_maximum_fusion.4.refs_0_, f32[4,32,256]{2,1,0:T(8,128)S(1)} %collective-permute-done.7.refs_1_, ...), custom_call_target="tpu_custom_call" | custom-call | flops 3700000000 | bytes 13320000 | tf_op jit(solution)/shard_map/pallas_call | solution.py:259
  42.3 1.3 %shard_map.134 = (bf16[8,256,172]{2,1,0:T(8,128)(2,1)S(1)}, f32[8,1,256]{2,1,0:T(1,128)S(1)}) custom-call(s32[2]{0:T(128)S(1)} %pad_add_fusion.place, f32[4,176,128]{2,1,0:T(8,128)S(1)} %pad_maximum_fusion.refs_0_, f32[4,176,128]{2,1,0:T(8,128)S(1)} %collective-permute-done.14.refs_1_, f32[3,176,128]{2,1,0:T(8,128)S(1)} %collective-permute-done.15.refs_2_, ...), custom_call_target="tpu_custom_call" | custom-call | flops 1500000000 | bytes 5400000 | tf_op jit(solution)/shard_map/pallas_call | solution.py:259
  43.8 1.2 %collective-permute-start.19 = (f32[2,4,32,256]{3,2,1,0:T(8,128)S(1)}, f32[2,4,32,256]{3,2,1,0:T(8,128)S(1)}, u32[]{:S(2)}, u32[]{:S(2)}) collective-permute-start(f32[2,4,32,256]{3,2,1,0:T(8,128)S(1)} %pad_maximum_fusion.2), channel_id=1, source_target_pairs={{0,4},{1,5},{2,6},{3,7},{4,0},{5,1},{6,2},{7,3},{8,12},{9,13},{10,... | collective-permute-start | bytes 786440 | tf_op jit(solution)/shard_map/ppermute | solution.py:271
  45.0 7.9 %shard_map.135 = (f32[300,1024]{1,0:T(8,128)S(1)}, f32[128,128]{1,0:T(8,128)S(1)}, f32[128,1024]{1,0:T(8,128)S(1)}) custom-call(s32[2]{0:T(128)S(1)} %pad_add_fusion.place, f32[4,32,256]{2,1,0:T(8,128)S(1)} %pad_maximum_fusion.4.refs_0_, f32[4,32,256]{2,1,0:T(8,128)S(1)} %collective-permute-done.7.refs_1_, f32[4,32,256]{2,1,0:T(8,128)S(1)} %collective-permute-done.8.refs_2_, ...), custom_call_target="tpu_custom_call" | custom-call | flops 12499999744 | bytes 45000000 | tf_op jit(solution)/shard_map/pallas_call | solution.py:259
  53.0 4.6 %shard_map.136 = (f32[300,1024]{1,0:T(8,128)S(1)}, f32[128,128]{1,0:T(8,128)}, bf16[128,768]{1,0:T(8,128)(2,1)S(1)}, bf16[768,1024]{1,0:T(8,128)(2,1)S(1)}, f32[768,1024]{1,0:T(8,128)S(1)}) custom-call(s32[2]{0:T(128)S(1)} %pad_add_fusion.place, f32[300,1024]{1,0:T(8,128)S(1)} %get-tuple-element.57.refs_0_, f32[128,128]{1,0:T(8,128)S(1)} %get-tuple-element.58.refs_1_, ...), custom_call_target="tpu_custom_call" | custom-call | flops 7500000256 | bytes 27000000 | tf_op jit(solution)/shard_map/pallas_call | solution.py:259
  57.7 2.1 %shard_map.137.mine = f32[128,1024]{1,0:T(8,128)S(1)} custom-call(f32[128,1024]{1,0:T(8,128)S(1)} %get-tuple-element.61.before, bf16[128,768]{1,0:T(8,128)(2,1)S(1)} %get-tuple-element.62.inputs, bf16[768,1024]{1,0:T(8,128)(2,1)S(1)} %get-tuple-element.63.delta_two, f32[768,1024]{1,0:T(8,128)S(1)} %get-tuple-element.64.slope_one, bf16[1024,1024]{1,0:T(8,128)(2,1)S(1)} %copy-done), custom_call_target="tpu_custom_call" | custom-call | flops 2500000000 | bytes 9000000 | tf_op jit(solution)/shard_map/pallas_call | solution.py:259
  60.6 1.2 %shard_map.138 = (f32[128,1024]{1,0:T(8,128)}, f32[172,1024]{1,0:T(8,128)}) custom-call(f32[300,1024]{1,0:T(8,128)S(1)} %get-tuple-element.65.mine, f32[300,1024]{1,0:T(8,128)S(1)} %collective-permute-done.21.theirs), custom_call_target="tpu_custom_call" | custom-call | flops 1500000000 | bytes 5400000 | tf_op jit(solution)/shard_map/pallas_call | solution.py:259
  (57 shorter events, 6.6 us)
Async XLA Ops:
  1.6 12.3 %collective-permute-start.1 = (f32[32,512]{1,0:T(8,128)S(1)}, f32[32,512]{1,0:T(8,128)S(1)}, u32[]{:S(2)}, u32[]{:S(2)}) collective-permute-start(f32[32,512]{1,0:T(8,128)S(1)} %copy-done.4), channel_id=1, source_target_pairs={{0,28},{1,29},{2,30},{3,31},{4,8},{5,9},{6,10},{7,11},{8,4},{9,5},... | collective-permute-start | bytes 196616 | tf_op jit(solution)/shard_map/ppermute | solution.py:296
  7.5 6.4 %collective-permute-start = (f32[32,512]{1,0:T(8,128)S(1)}, f32[32,512]{1,0:T(8,128)S(1)}, u32[]{:S(2)}, u32[]{:S(2)}) collective-permute-start(f32[32,512]{1,0:T(8,128)S(1)} %copy-done.4), channel_id=1, source_target_pairs={{0,4},{1,5},{2,6},{3,7},{4,0},{5,1},{6,2},{7,3},{8,12},{9,13},{10,... | collective-permute-start | bytes 196616 | tf_op jit(solution)/shard_map/ppermute | solution.py:271
  8.8 8.8 %collective-permute-start.13 = (f32[176,128]{1,0:T(8,128)S(1)}, f32[176,128]{1,0:T(8,128)S(1)}, u32[]{:S(2)}, u32[]{:S(2)}) collective-permute-start(f32[176,128]{1,0:T(8,128)S(1)} %get-tuple-element.47), channel_id=1, source_target_pairs={{0,24},{1,25},{2,26},{3,27},{4,28},{5,29},{6,30},{7,31},{8,16},{9,... | collective-permute-start | bytes 270344 | tf_op jit(solution)/shard_map/ppermute | solution.py:271
  9.4 10.0 %collective-permute-start.12 = (f32[176,128]{1,0:T(8,128)S(1)}, f32[176,128]{1,0:T(8,128)S(1)}, u32[]{:S(2)}, u32[]{:S(2)}) collective-permute-start(f32[176,128]{1,0:T(8,128)S(1)} %get-tuple-element.47), channel_id=1, source_target_pairs={{0,16},{1,17},{2,18},{3,19},{4,20},{5,21},{6,22},{7,23},{8,24},{9,... | collective-permute-start | bytes 270344 | tf_op jit(solution)/shard_map/ppermute | solution.py:271
  10.4 9.0 %collective-permute-start.11 = (f32[176,128]{1,0:T(8,128)S(1)}, f32[176,128]{1,0:T(8,128)S(1)}, u32[]{:S(2)}, u32[]{:S(2)}) collective-permute-start(f32[176,128]{1,0:T(8,128)S(1)} %get-tuple-element.47), channel_id=1, source_target_pairs={{0,8},{1,9},{2,10},{3,11},{4,12},{5,13},{6,14},{7,15},{8,0},{9,1},... | collective-permute-start | bytes 270344 | tf_op jit(solution)/shard_map/ppermute | solution.py:271
  15.4 7.1 %collective-permute-start.3 = (f32[32,512]{1,0:T(8,128)S(1)}, f32[32,512]{1,0:T(8,128)S(1)}, u32[]{:S(2)}, u32[]{:S(2)}) collective-permute-start(f32[32,512]{1,0:T(8,128)S(1)} %shard_map.130.own), channel_id=1, source_target_pairs={{0,28},{1,29},{2,30},{3,31},{4,8},{5,9},{6,10},{7,11},{8,4},{9,5},... | collective-permute-start | bytes 196616 | tf_op jit(solution)/shard_map/ppermute | solution.py:296
  17.4 5.7 %collective-permute-start.2 = (f32[32,512]{1,0:T(8,128)S(1)}, f32[32,512]{1,0:T(8,128)S(1)}, u32[]{:S(2)}, u32[]{:S(2)}) collective-permute-start(f32[32,512]{1,0:T(8,128)S(1)} %shard_map.130.own), channel_id=1, source_target_pairs={{0,4},{1,5},{2,6},{3,7},{4,0},{5,1},{6,2},{7,3},{8,12},{9,13},{10,... | collective-permute-start | bytes 196616 | tf_op jit(solution)/shard_map/ppermute | solution.py:271
  19.4 15.0 %collective-permute-start.14 = (f32[4,176,128]{2,1,0:T(8,128)S(1)}, f32[4,176,128]{2,1,0:T(8,128)S(1)}, u32[]{:S(2)}, u32[]{:S(2)}) collective-permute-start(f32[4,176,128]{2,1,0:T(8,128)S(1)} %pad_maximum_fusion.refs_0_), channel_id=1, source_target_pairs={{0,4},{1,5},{2,6},{3,7},{4,0},{5,1},{6,2},{7,3},{8,12},{9,13},{10,... | collective-permute-start | bytes 1081352 | tf_op jit(solution)/shard_map/ppermute | solution.py:271
  19.7 14.3 %collective-permute-start.15 = (f32[3,176,128]{2,1,0:T(8,128)S(1)}, f32[3,176,128]{2,1,0:T(8,128)S(1)}, u32[]{:S(2)}, u32[]{:S(2)}) collective-permute-start(f32[3,176,128]{2,1,0:T(8,128)S(1)} %pad_maximum_fusion.1), channel_id=1, source_target_pairs={{0,2},{1,3},{2,0},{3,1},{4,6},{5,7},{6,4},{7,5},{8,10},{9,11},{10,... | collective-permute-start | bytes 811016 | tf_op jit(solution)/shard_map/ppermute | solution.py:271
  23.1 14.7 %copy-start = (bf16[1024,1024]{1,0:T(8,128)(2,1)S(1)}, bf16[1024,1024]{1,0:T(8,128)(2,1)}, u32[]{:S(2)}) copy-start(bf16[1024,1024]{1,0:T(8,128)(2,1)} %w_mid.1) | copy-start | bytes 6291460
  23.1 14.7 %copy-start.3 = (bf16[128,1024]{1,0:T(8,128)(2,1)S(1)}, bf16[128,1024]{1,0:T(8,128)(2,1)}, u32[]{:S(2)}) copy-start(bf16[128,1024]{1,0:T(8,128)(2,1)} %refs_7_.1) | copy-start | bytes 786436
  24.8 4.0 %collective-permute-start.5 = (f32[32,256]{1,0:T(8,128)S(1)}, f32[32,256]{1,0:T(8,128)S(1)}, u32[]{:S(2)}, u32[]{:S(2)}) collective-permute-start(f32[32,256]{1,0:T(8,128)S(1)} %get-tuple-element.40), channel_id=1, source_target_pairs={{0,2},{1,3},{2,0},{3,1},{4,6},{5,7},{6,4},{7,5},{8,10},{9,11},{10,... | collective-permute-start | bytes 98312 | tf_op jit(solution)/shard_map/ppermute | solution.py:271
  26.4 3.3 %collective-permute-start.6 = (f32[32,256]{1,0:T(8,128)S(1)}, f32[32,256]{1,0:T(8,128)S(1)}, u32[]{:S(2)}, u32[]{:S(2)}) collective-permute-start(f32[32,256]{1,0:T(8,128)S(1)} %get-tuple-element.41), channel_id=1, source_target_pairs={{0,3},{1,2},{2,1},{3,0},{4,7},{5,6},{6,5},{7,4},{8,11},{9,10},{10,... | collective-permute-start | bytes 98312 | tf_op jit(solution)/shard_map/ppermute | solution.py:271
  26.4 3.3 %collective-permute-start.4 = (f32[32,256]{1,0:T(8,128)S(1)}, f32[32,256]{1,0:T(8,128)S(1)}, u32[]{:S(2)}, u32[]{:S(2)}) collective-permute-start(f32[32,256]{1,0:T(8,128)S(1)} %get-tuple-element.41), channel_id=1, source_target_pairs={{0,1},{1,0},{2,3},{3,2},{4,5},{5,4},{6,7},{7,6},{8,9},{9,8},{10,11... | collective-permute-start | bytes 98312 | tf_op jit(solution)/shard_map/ppermute | solution.py:271
  29.8 6.5 %collective-permute-start.8 = (f32[4,32,256]{2,1,0:T(8,128)S(1)}, f32[4,32,256]{2,1,0:T(8,128)S(1)}, u32[]{:S(2)}, u32[]{:S(2)}) collective-permute-start(f32[4,32,256]{2,1,0:T(8,128)S(1)} %pad_maximum_fusion.4.refs_0_), channel_id=1, source_target_pairs={{0,8},{1,9},{2,10},{3,11},{4,12},{5,13},{6,14},{7,15},{8,0},{9,1},... | collective-permute-start | bytes 393224 | tf_op jit(solution)/shard_map/ppermute | solution.py:271
  30.7 7.0 %collective-permute-start.7 = (f32[4,32,256]{2,1,0:T(8,128)S(1)}, f32[4,32,256]{2,1,0:T(8,128)S(1)}, u32[]{:S(2)}, u32[]{:S(2)}) collective-permute-start(f32[4,32,256]{2,1,0:T(8,128)S(1)} %pad_maximum_fusion.4.refs_0_), channel_id=1, source_target_pairs={{0,4},{1,5},{2,6},{3,7},{4,0},{5,1},{6,2},{7,3},{8,12},{9,13},{10,... | collective-permute-start | bytes 393224 | tf_op jit(solution)/shard_map/ppermute | solution.py:271
  30.9 12.8 %collective-permute-start.10 = (f32[4,32,256]{2,1,0:T(8,128)S(1)}, f32[4,32,256]{2,1,0:T(8,128)S(1)}, u32[]{:S(2)}, u32[]{:S(2)}) collective-permute-start(f32[4,32,256]{2,1,0:T(8,128)S(1)} %pad_maximum_fusion.4.refs_0_), channel_id=1, source_target_pairs={{0,16},{1,17},{2,18},{3,19},{4,20},{5,21},{6,22},{7,23},{8,24},{9,... | collective-permute-start | bytes 393224 | tf_op jit(solution)/shard_map/ppermute | solution.py:271
  34.0 9.7 %collective-permute-start.9 = (f32[4,32,256]{2,1,0:T(8,128)S(1)}, f32[4,32,256]{2,1,0:T(8,128)S(1)}, u32[]{:S(2)}, u32[]{:S(2)}) collective-permute-start(f32[4,32,256]{2,1,0:T(8,128)S(1)} %pad_maximum_fusion.4.refs_0_), channel_id=1, source_target_pairs={{0,24},{1,25},{2,26},{3,27},{4,28},{5,29},{6,30},{7,31},{8,16},{9,... | collective-permute-start | bytes 393224 | tf_op jit(solution)/shard_map/ppermute | solution.py:271
  34.4 7.9 %collective-permute-start.16 = (f32[3,176,128]{2,1,0:T(8,128)S(1)}, f32[3,176,128]{2,1,0:T(8,128)S(1)}, u32[]{:S(2)}, u32[]{:S(2)}) collective-permute-start(f32[3,176,128]{2,1,0:T(8,128)S(1)} %collective-permute-done.15.refs_2_), channel_id=1, source_target_pairs={{0,4},{1,5},{2,6},{3,7},{4,0},{5,1},{6,2},{7,3},{8,12},{9,13},{10,... | collective-permute-start | bytes 811016 | tf_op jit(solution)/shard_map/ppermute | solution.py:271
  36.3 6.0 %collective-permute-start.17 = (f32[2,176,128]{2,1,0:T(8,128)S(1)}, f32[2,176,128]{2,1,0:T(8,128)S(1)}, u32[]{:S(2)}, u32[]{:S(2)}) collective-permute-start(f32[2,176,128]{2,1,0:T(8,128)S(1)} %pad_maximum_fusion.3), channel_id=1, source_target_pairs={{0,2},{1,3},{2,0},{3,1},{4,6},{5,7},{6,4},{7,5},{8,10},{9,11},{10,... | collective-permute-start | bytes 540680 | tf_op jit(solution)/shard_map/ppermute | solution.py:271
  41.5 11.5 %collective-permute-start.18 = (f32[4,32,256]{2,1,0:T(8,128)S(1)}, f32[4,32,256]{2,1,0:T(8,128)S(1)}, u32[]{:S(2)}, u32[]{:S(2)}) collective-permute-start(f32[4,32,256]{2,1,0:T(8,128)S(1)} %collective-permute-done.8.refs_2_), channel_id=1, source_target_pairs={{0,4},{1,5},{2,6},{3,7},{4,0},{5,1},{6,2},{7,3},{8,12},{9,13},{10,... | collective-permute-start | bytes 393224 | tf_op jit(solution)/shard_map/ppermute | solution.py:271
  43.8 9.2 %collective-permute-start.19 = (f32[2,4,32,256]{3,2,1,0:T(8,128)S(1)}, f32[2,4,32,256]{3,2,1,0:T(8,128)S(1)}, u32[]{:S(2)}, u32[]{:S(2)}) collective-permute-start(f32[2,4,32,256]{3,2,1,0:T(8,128)S(1)} %pad_maximum_fusion.2), channel_id=1, source_target_pairs={{0,4},{1,5},{2,6},{3,7},{4,0},{5,1},{6,2},{7,3},{8,12},{9,13},{10,... | collective-permute-start | bytes 786440 | tf_op jit(solution)/shard_map/ppermute | solution.py:271
  57.6 3.0 %collective-permute-start.21 = (f32[300,1024]{1,0:T(8,128)S(1)}, f32[300,1024]{1,0:T(8,128)S(1)}, u32[]{:S(2)}, u32[]{:S(2)}) collective-permute-start(f32[300,1024]{1,0:T(8,128)S(1)} %get-tuple-element.65.mine), channel_id=1, source_target_pairs={{0,1},{1,0},{2,3},{3,2},{4,5},{5,4},{6,7},{7,6},{8,9},{9,8},{10,11... | collective-permute-start | bytes 3686408 | tf_op jit(solution)/shard_map/ppermute | solution.py:271
  59.8 2.1 %collective-permute-start.20 = (f32[128,1024]{1,0:T(8,128)S(1)}, f32[128,1024]{1,0:T(8,128)S(1)}, u32[]{:S(2)}, u32[]{:S(2)}) collective-permute-start(f32[128,1024]{1,0:T(8,128)S(1)} %shard_map.137.mine), channel_id=1, source_target_pairs={{0,1},{1,0},{2,3},{3,2},{4,5},{5,4},{6,7},{7,6},{8,9},{9,8},{10,11... | collective-permute-start | bytes 1572872 | tf_op jit(solution)/shard_map/ppermute | solution.py:271
  (7 other events, 37.1 us)

commit v6 on v5

--- a/solution.py
+++ b/solution.py
@@ -36,12 +36,7 @@
     out[...] = jnp.full(out.shape, place[0], F32)
 
 
-def prepare_kernel(segment, block, place, slots_hbm, cot_hbm, opened, packed, rank_row, slots, cot, sems):
-    fetch_slots = pltpu.make_async_copy(slots_hbm, slots, sems.at[0])
-    fetch_cot = pltpu.make_async_copy(cot_hbm, cot, sems.at[1])
-    fetch_slots.start()
-    fetch_cot.start()
-    fetch_slots.wait()
+def prepare_kernel(segment, block, place, slots, cot, opened, packed, rank_row):
     nodes = slots.shape[1]
     half = nodes // 2
     row = slots[...].astype(F32)
@@ -56,7 +51,6 @@
     ordered = jnp.sum(jnp.where(rank_column == lane, column, 0.0), axis=0, keepdims=True)
     mine = jnp.where(place[1] % 2 == 0, ordered[:, :half], ordered[:, half:])
     classes, width = cot.shape
-    fetch_cot.wait()
     packed[0:classes, :] = cot[...].astype(F32)
     extra = packed.shape[0] - classes
     rows = half // width
@@ -252,14 +246,14 @@
         start += out.shape[0]
 
 
-def call(kernel, outs, scalars, arrays, scratch=(), micros=1.5, space=pltpu.VMEM, mib=16):
+def call(kernel, outs, scalars, arrays, scratch=(), micros=1.5, mib=16):
     cost = pl.CostEstimate(
         flops=int(micros * 1e9), bytes_accessed=int(micros * 3.6e6), transcendentals=0
     )
     return pl.pallas_call(
         kernel,
         out_shape=outs,
-        in_specs=[SMEM] * len(scalars) + [pl.BlockSpec(memory_space=space)] * len(arrays),
+        in_specs=[SMEM] * len(scalars) + [VMEM] * len(arrays),
         out_specs=jax.tree.map(lambda _: VMEM, outs),
         scratch_shapes=list(scratch),
         compiler_params=pltpu.CompilerParams(vmem_limit_bytes=mib * 2**20),
@@ -298,8 +292,7 @@
     rows = half // width
     padded = classes + rows + (-(classes + rows)) % 8
     opened = call(open_kernel, jax.ShapeDtypeStruct((8, 128), F32), [place], [], micros=4.0)
-    opened, ready = lax.optimization_barrier((opened, features))
-    near_one, far_one = send(ready, replicas), far(ready)
+    near_one, far_one = send(features, replicas), far(features)
     packed, rank_row = call(
         functools.partial(prepare_kernel, segment, width),
         (
@@ -308,12 +301,6 @@
         ),
         [place],
         [dest_slot.reshape(1, -1), cotangent, opened],
-        [
-            pltpu.VMEM((1, node_count), jnp.int32),
-            pltpu.VMEM((classes, width), BF16),
-            pltpu.SemaphoreType.DMA((2,)),
-        ],
-        space=pltpu.HBM,
     )
     field = pltpu.VMEM((3 * count, 3 * feature_count, size), BF16)
     first = call(
@@ -326,7 +313,7 @@
     line = [packed] + [send(packed, m) for m in (8, 16, 24)]
     column = jnp.stack(line)
     near_two, far_two = send(first, replicas), far(first)
-    across_x, across_y = send(column, 4), send(column[0:3], 2)
+    across_y, across_x = send(jnp.stack(line[0:3]), 2), send(column, 4)
     corner_one = send(across_y, 4)
     corner_two = send(jnp.concatenate([column[3:4], across_x[3:4]]), 2)
     mine, other = call(
@@ -354,7 +341,7 @@
         micros=3.7,
         mib=20,
     )
-    orders = ((0, 4, 8, 12), (2, 6, 10, 14), (1, 5, 9), (3, 7, 11), (13, 15))
+    orders = ((0, 4, 8, 12), (1, 5, 9), (2, 6, 10, 14), (3, 7, 11), (13, 15))
     arranged, slot_rows = call(
         functools.partial(cotangent_kernel, orders, classes, segment),
         (
@@ -362,7 +349,7 @@
             jax.ShapeDtypeStruct((owners, 1, half), F32),
         ),
         [place],
-        [column, across_x, across_y, corner_one, corner_two],
+        [column, across_y, across_x, corner_one, corner_two],
         [
             pltpu.VMEM((devices // 2, classes, width), BF16),
             pltpu.VMEM((devices // 2, rows, width), F32),

time: 62.9 us -> 62.8 us (level)
  transfers between devices with their start and end apart: 22 -> 22, of which waited for: 8 -> 8; matrix products, arithmetic and copies ran while one was open for 0% -> 0% of each run, Pallas kernels for 33% -> 34%
where the time goes in v6:
time: 62.8 us; the launch traced here: 62.6 us
  starting transfers between devices  27.4 us (44%)
  Pallas kernels  26.6 us (42%)
  waiting for transfers between devices  6.63 us (11%)
  between operations  1.51 us (2%)
    pallas_call x11, Pallas kernels, call(): pl.pallas_call(kernel, out_shape=outs, in_specs=[SMEM] * len(scalars) + [...  26.6 us
    ppermute x20, starting transfers between devices, exchanged(): return lax.ppermute(value, AXES, [(i, i ^ mask) for i in range(devices)])  19.4 us
    ppermute x2, starting transfers between devices, far(): return lax.ppermute(value, AXES, far_pairs)  8.01 us
    ppermute x20, waiting for transfers between devices, exchanged(): return lax.ppermute(value, AXES, [(i, i ^ mask) for i in range(devices)])  5.33 us
    ppermute x2, waiting for transfers between devices, far(): return lax.ppermute(value, AXES, far_pairs)  1.3 us
  transfers between devices with their start and end apart: 22, of which 8 were waited for; matrix products, arithmetic and copies ran while one was open for 0% of the time, Pallas kernels for 34%

profile of v6, /device:TPU:0, one launch (start us, length us, event | category | flops | bytes accessed | tf_op | source)
XLA Modules:
  0.0 62.6 jit_solution(8392768078092157103)
XLA Ops:
  0.6 6.0 %collective-permute-start.1 = (f32[32,512]{1,0:T(8,128)}, f32[32,512]{1,0:T(8,128)S(1)}, u32[]{:S(2)}, u32[]{:S(2)}) collective-permute-start(f32[32,512]{1,0:T(8,128)} %features.1), channel_id=1, source_target_pairs={{0,28},{1,29},{2,30},{3,31},{4,8},{5,9},{6,10},{7,11},{8,4},{9,5},... | collective-permute-start | bytes 196616 | tf_op jit(solution)/shard_map/ppermute | solution.py:290
  7.6 1.1 %shard_map.131 = (f32[176,128]{1,0:T(8,128)S(1)}, s32[1,512]{1,0:T(1,128)S(1)}) custom-call(s32[2]{0:T(128)S(1)} %pad_add_fusion.place, s32[1,512]{1,0:T(1,128)S(1)} %bitcast.22, bf16[172,128]{1,0:T(8,128)(2,1)S(1)} %copy-done.5, f32[8,128]{1,0:T(8,128)S(1)} %shard_map.130.opened), custom_call_target="tpu_custom_call" | custom-call | flops 1500000000 | bytes 5400000 | tf_op jit(solution)/shard_map/pallas_call | solution.py:253
  9.4 0.9 %collective-permute-start.12 = (f32[176,128]{1,0:T(8,128)S(1)}, f32[176,128]{1,0:T(8,128)S(1)}, u32[]{:S(2)}, u32[]{:S(2)}) collective-permute-start(f32[176,128]{1,0:T(8,128)S(1)} %get-tuple-element.43), channel_id=1, source_target_pairs={{0,16},{1,17},{2,18},{3,19},{4,20},{5,21},{6,22},{7,23},{8,24},{9,... | collective-permute-start | bytes 270344 | tf_op jit(solution)/shard_map/ppermute | solution.py:265
  10.3 2.8 %collective-permute-start.11 = (f32[176,128]{1,0:T(8,128)S(1)}, f32[176,128]{1,0:T(8,128)S(1)}, u32[]{:S(2)}, u32[]{:S(2)}) collective-permute-start(f32[176,128]{1,0:T(8,128)S(1)} %get-tuple-element.43), channel_id=1, source_target_pairs={{0,8},{1,9},{2,10},{3,11},{4,12},{5,13},{6,14},{7,15},{8,0},{9,1},... | collective-permute-start | bytes 270344 | tf_op jit(solution)/shard_map/ppermute | solution.py:265
  13.8 1.5 %shard_map.129.own = f32[32,512]{1,0:T(8,128)S(1)} custom-call(s32[2]{0:T(128)S(1)} %pad_add_fusion.place, s32[1]{0:T(128)S(6)} %copy.14.live, s32[40]{0:T(128)S(1)} %copy-done.7, s32[40]{0:T(128)S(1)} %copy-done.8, f32[32,512]{1,0:T(8,128)S(1)} %copy-done.4, f32[32,512]{1,0:T(8,128)S(1)} %collective-permute-done.near, ...), custom_call_target="tpu_custom_call" | custom-call | flops 1500000000 | bytes 5400000 | tf_op jit(solution)/shard_map/pallas_call | solution.py:253
  15.3 2.0 %collective-permute-start.3 = (f32[32,512]{1,0:T(8,128)S(1)}, f32[32,512]{1,0:T(8,128)S(1)}, u32[]{:S(2)}, u32[]{:S(2)}) collective-permute-start(f32[32,512]{1,0:T(8,128)S(1)} %shard_map.129.own), channel_id=1, source_target_pairs={{0,28},{1,29},{2,30},{3,31},{4,8},{5,9},{6,10},{7,11},{8,4},{9,5},... | collective-permute-start | bytes 196616 | tf_op jit(solution)/shard_map/ppermute | solution.py:290
  17.5 1.7 %collective-permute-done.12 = f32[176,128]{1,0:T(8,128)S(1)} collective-permute-done((f32[176,128]{1,0:T(8,128)S(1)}, f32[176,128]{1,0:T(8,128)S(1)}, u32[]{:S(2)}, u32[]{:S(2)}) %collective-permute-start.12) | collective-permute-done | bytes 90144 | tf_op jit(solution)/shard_map/ppermute | solution.py:265
  19.6 1.6 %collective-permute-start.14 = (f32[3,176,128]{2,1,0:T(8,128)S(1)}, f32[3,176,128]{2,1,0:T(8,128)S(1)}, u32[]{:S(2)}, u32[]{:S(2)}) collective-permute-start(f32[3,176,128]{2,1,0:T(8,128)S(1)} %pad_maximum_fusion.1), channel_id=1, source_target_pairs={{0,2},{1,3},{2,0},{3,1},{4,6},{5,7},{6,4},{7,5},{8,10},{9,11},{10,... | collective-permute-start | bytes 811016 | tf_op jit(solution)/shard_map/ppermute | solution.py:265
  21.2 1.3 %collective-permute-done.3.far = f32[32,512]{1,0:T(8,128)S(1)} collective-permute-done((f32[32,512]{1,0:T(8,128)S(1)}, f32[32,512]{1,0:T(8,128)S(1)}, u32[]{:S(2)}, u32[]{:S(2)}) %collective-permute-start.3) | collective-permute-done | bytes 65568 | tf_op jit(solution)/shard_map/ppermute | solution.py:290
  23.0 1.7 %shard_map.132 = (f32[32,256]{1,0:T(8,128)S(1)}, f32[32,256]{1,0:T(8,128)S(1)}) custom-call(s32[2]{0:T(128)S(1)} %pad_add_fusion.place, s32[1]{0:T(128)S(6)} %copy.14.live, s32[40]{0:T(128)S(1)} %copy-done.7, s32[40]{0:T(128)S(1)} %copy-done.8, f32[32,512]{1,0:T(8,128)S(1)} %shard_map.129.own, f32[32,512]{1,0:T(8,128)S(1)} %collective-permute-done.2.near, ...), custom_call_target="tpu_custom_call" | custom-call | flops 1500000000 | bytes 5400000 | tf_op jit(solution)/shard_map/pallas_call | solution.py:253
  24.7 1.6 %collective-permute-start.5 = (f32[32,256]{1,0:T(8,128)S(1)}, f32[32,256]{1,0:T(8,128)S(1)}, u32[]{:S(2)}, u32[]{:S(2)}) collective-permute-start(f32[32,256]{1,0:T(8,128)S(1)} %get-tuple-element.36), channel_id=1, source_target_pairs={{0,2},{1,3},{2,0},{3,1},{4,6},{5,7},{6,4},{7,5},{8,10},{9,11},{10,... | collective-permute-start | bytes 98312 | tf_op jit(solution)/shard_map/ppermute | solution.py:265
  26.9 1.8 %collective-permute-done.5 = f32[32,256]{1,0:T(8,128)S(1)} collective-permute-done((f32[32,256]{1,0:T(8,128)S(1)}, f32[32,256]{1,0:T(8,128)S(1)}, u32[]{:S(2)}, u32[]{:S(2)}) %collective-permute-start.5) | collective-permute-done | bytes 32800 | tf_op jit(solution)/shard_map/ppermute | solution.py:265
  28.7 1.0 %collective-permute-done.6 = f32[32,256]{1,0:T(8,128)S(1)} collective-permute-done((f32[32,256]{1,0:T(8,128)S(1)}, f32[32,256]{1,0:T(8,128)S(1)}, u32[]{:S(2)}, u32[]{:S(2)}) %collective-permute-start.6) | collective-permute-done | bytes 32800 | tf_op jit(solution)/shard_map/ppermute | solution.py:265
  29.7 1.0 %collective-permute-start.8 = (f32[4,32,256]{2,1,0:T(8,128)S(1)}, f32[4,32,256]{2,1,0:T(8,128)S(1)}, u32[]{:S(2)}, u32[]{:S(2)}) collective-permute-start(f32[4,32,256]{2,1,0:T(8,128)S(1)} %pad_maximum_fusion.4.refs_0_), channel_id=1, source_target_pairs={{0,8},{1,9},{2,10},{3,11},{4,12},{5,13},{6,14},{7,15},{8,0},{9,1},... | collective-permute-start | bytes 393224 | tf_op jit(solution)/shard_map/ppermute | solution.py:265
  30.9 2.8 %collective-permute-start.10 = (f32[4,32,256]{2,1,0:T(8,128)S(1)}, f32[4,32,256]{2,1,0:T(8,128)S(1)}, u32[]{:S(2)}, u32[]{:S(2)}) collective-permute-start(f32[4,32,256]{2,1,0:T(8,128)S(1)} %pad_maximum_fusion.4.refs_0_), channel_id=1, source_target_pairs={{0,16},{1,17},{2,18},{3,19},{4,20},{5,21},{6,22},{7,23},{8,24},{9,... | collective-permute-start | bytes 393224 | tf_op jit(solution)/shard_map/ppermute | solution.py:265
  34.4 1.8 %collective-permute-start.16 = (f32[3,176,128]{2,1,0:T(8,128)S(1)}, f32[3,176,128]{2,1,0:T(8,128)S(1)}, u32[]{:S(2)}, u32[]{:S(2)}) collective-permute-start(f32[3,176,128]{2,1,0:T(8,128)S(1)} %collective-permute-done.14.refs_1_), channel_id=1, source_target_pairs={{0,4},{1,5},{2,6},{3,7},{4,0},{5,1},{6,2},{7,3},{8,12},{9,13},{10,... | collective-permute-start | bytes 811016 | tf_op jit(solution)/shard_map/ppermute | solution.py:265
  36.2 1.4 %collective-permute-start.17 = (f32[2,176,128]{2,1,0:T(8,128)S(1)}, f32[2,176,128]{2,1,0:T(8,128)S(1)}, u32[]{:S(2)}, u32[]{:S(2)}) collective-permute-start(f32[2,176,128]{2,1,0:T(8,128)S(1)} %pad_maximum_fusion.3), channel_id=1, source_target_pairs={{0,2},{1,3},{2,0},{3,1},{4,6},{5,7},{6,4},{7,5},{8,10},{9,11},{10,... | collective-permute-start | bytes 540680 | tf_op jit(solution)/shard_map/ppermute | solution.py:265
  37.6 3.7 %shard_map.133 = (bf16[768,128]{1,0:T(8,128)(2,1)S(1)}, bf16[768,1024]{1,0:T(8,128)(2,1)S(1)}, f32[768,1024]{1,0:T(8,128)S(1)}, f32[768,1024]{1,0:T(8,128)S(1)}) custom-call(s32[2]{0:T(128)S(1)} %pad_add_fusion.place, f32[4,32,256]{2,1,0:T(8,128)S(1)} %pad_maximum_fusion.4.refs_0_, f32[4,32,256]{2,1,0:T(8,128)S(1)} %collective-permute-done.7.refs_1_, ...), custom_call_target="tpu_custom_call" | custom-call | flops 3700000000 | bytes 13320000 | tf_op jit(solution)/shard_map/pallas_call | solution.py:253
  42.0 1.3 %shard_map.134 = (bf16[8,256,172]{2,1,0:T(8,128)(2,1)S(1)}, f32[8,1,256]{2,1,0:T(1,128)S(1)}) custom-call(s32[2]{0:T(128)S(1)} %pad_add_fusion.place, f32[4,176,128]{2,1,0:T(8,128)S(1)} %pad_maximum_fusion.refs_0_, f32[3,176,128]{2,1,0:T(8,128)S(1)} %collective-permute-done.14.refs_1_, f32[4,176,128]{2,1,0:T(8,128)S(1)} %collective-permute-done.15.refs_2_, ...), custom_call_target="tpu_custom_call" | custom-call | flops 1500000000 | bytes 5400000 | tf_op jit(solution)/shard_map/pallas_call | solution.py:253
  43.4 1.5 %collective-permute-start.19 = (f32[2,4,32,256]{3,2,1,0:T(8,128)S(1)}, f32[2,4,32,256]{3,2,1,0:T(8,128)S(1)}, u32[]{:S(2)}, u32[]{:S(2)}) collective-permute-start(f32[2,4,32,256]{3,2,1,0:T(8,128)S(1)} %pad_maximum_fusion.2), channel_id=1, source_target_pairs={{0,4},{1,5},{2,6},{3,7},{4,0},{5,1},{6,2},{7,3},{8,12},{9,13},{10,... | collective-permute-start | bytes 786440 | tf_op jit(solution)/shard_map/ppermute | solution.py:265
  44.9 7.9 %shard_map.135 = (f32[300,1024]{1,0:T(8,128)S(1)}, f32[128,128]{1,0:T(8,128)S(1)}, f32[128,1024]{1,0:T(8,128)S(1)}) custom-call(s32[2]{0:T(128)S(1)} %pad_add_fusion.place, f32[4,32,256]{2,1,0:T(8,128)S(1)} %pad_maximum_fusion.4.refs_0_, f32[4,32,256]{2,1,0:T(8,128)S(1)} %collective-permute-done.7.refs_1_, f32[4,32,256]{2,1,0:T(8,128)S(1)} %collective-permute-done.8.refs_2_, ...), custom_call_target="tpu_custom_call" | custom-call | flops 12499999744 | bytes 45000000 | tf_op jit(solution)/shard_map/pallas_call | solution.py:253
  52.8 4.6 %shard_map.136 = (f32[300,1024]{1,0:T(8,128)S(1)}, f32[128,128]{1,0:T(8,128)}, bf16[128,768]{1,0:T(8,128)(2,1)S(1)}, bf16[768,1024]{1,0:T(8,128)(2,1)S(1)}, f32[768,1024]{1,0:T(8,128)S(1)}) custom-call(s32[2]{0:T(128)S(1)} %pad_add_fusion.place, f32[300,1024]{1,0:T(8,128)S(1)} %get-tuple-element.53.refs_0_, f32[128,128]{1,0:T(8,128)S(1)} %get-tuple-element.54.refs_1_, ...), custom_call_target="tpu_custom_call" | custom-call | flops 7500000256 | bytes 27000000 | tf_op jit(solution)/shard_map/pallas_call | solution.py:253
  57.6 2.1 %shard_map.137.mine = f32[128,1024]{1,0:T(8,128)S(1)} custom-call(f32[128,1024]{1,0:T(8,128)S(1)} %get-tuple-element.57.before, bf16[128,768]{1,0:T(8,128)(2,1)S(1)} %get-tuple-element.58.inputs, bf16[768,1024]{1,0:T(8,128)(2,1)S(1)} %get-tuple-element.59.delta_two, f32[768,1024]{1,0:T(8,128)S(1)} %get-tuple-element.60.slope_one, bf16[1024,1024]{1,0:T(8,128)(2,1)S(1)} %copy-done), custom_call_target="tpu_custom_call" | custom-call | flops 2500000000 | bytes 9000000 | tf_op jit(solution)/shard_map/pallas_call | solution.py:253
  60.5 1.2 %shard_map.138 = (f32[128,1024]{1,0:T(8,128)}, f32[172,1024]{1,0:T(8,128)}) custom-call(f32[300,1024]{1,0:T(8,128)S(1)} %get-tuple-element.61.mine, f32[300,1024]{1,0:T(8,128)S(1)} %collective-permute-done.21.theirs), custom_call_target="tpu_custom_call" | custom-call | flops 1500000000 | bytes 5400000 | tf_op jit(solution)/shard_map/pallas_call | solution.py:253
  (57 shorter events, 6.7 us)
Async XLA Ops:
  0.6 13.1 %collective-permute-start.1 = (f32[32,512]{1,0:T(8,128)}, f32[32,512]{1,0:T(8,128)S(1)}, u32[]{:S(2)}, u32[]{:S(2)}) collective-permute-start(f32[32,512]{1,0:T(8,128)} %features.1), channel_id=1, source_target_pairs={{0,28},{1,29},{2,30},{3,31},{4,8},{5,9},{6,10},{7,11},{8,4},{9,5},... | collective-permute-start | bytes 196616 | tf_op jit(solution)/shard_map/ppermute | solution.py:290
  6.7 7.1 %collective-permute-start = (f32[32,512]{1,0:T(8,128)}, f32[32,512]{1,0:T(8,128)S(1)}, u32[]{:S(2)}, u32[]{:S(2)}) collective-permute-start(f32[32,512]{1,0:T(8,128)} %features.1), channel_id=1, source_target_pairs={{0,4},{1,5},{2,6},{3,7},{4,0},{5,1},{6,2},{7,3},{8,12},{9,13},{10,... | collective-permute-start | bytes 196616 | tf_op jit(solution)/shard_map/ppermute | solution.py:265
  8.7 8.8 %collective-permute-start.13 = (f32[176,128]{1,0:T(8,128)S(1)}, f32[176,128]{1,0:T(8,128)S(1)}, u32[]{:S(2)}, u32[]{:S(2)}) collective-permute-start(f32[176,128]{1,0:T(8,128)S(1)} %get-tuple-element.43), channel_id=1, source_target_pairs={{0,24},{1,25},{2,26},{3,27},{4,28},{5,29},{6,30},{7,31},{8,16},{9,... | collective-permute-start | bytes 270344 | tf_op jit(solution)/shard_map/ppermute | solution.py:265
  9.4 9.8 %collective-permute-start.12 = (f32[176,128]{1,0:T(8,128)S(1)}, f32[176,128]{1,0:T(8,128)S(1)}, u32[]{:S(2)}, u32[]{:S(2)}) collective-permute-start(f32[176,128]{1,0:T(8,128)S(1)} %get-tuple-element.43), channel_id=1, source_target_pairs={{0,16},{1,17},{2,18},{3,19},{4,20},{5,21},{6,22},{7,23},{8,24},{9,... | collective-permute-start | bytes 270344 | tf_op jit(solution)/shard_map/ppermute | solution.py:265
  10.3 8.9 %collective-permute-start.11 = (f32[176,128]{1,0:T(8,128)S(1)}, f32[176,128]{1,0:T(8,128)S(1)}, u32[]{:S(2)}, u32[]{:S(2)}) collective-permute-start(f32[176,128]{1,0:T(8,128)S(1)} %get-tuple-element.43), channel_id=1, source_target_pairs={{0,8},{1,9},{2,10},{3,11},{4,12},{5,13},{6,14},{7,15},{8,0},{9,1},... | collective-permute-start | bytes 270344 | tf_op jit(solution)/shard_map/ppermute | solution.py:265
  15.3 7.1 %collective-permute-start.3 = (f32[32,512]{1,0:T(8,128)S(1)}, f32[32,512]{1,0:T(8,128)S(1)}, u32[]{:S(2)}, u32[]{:S(2)}) collective-permute-start(f32[32,512]{1,0:T(8,128)S(1)} %shard_map.129.own), channel_id=1, source_target_pairs={{0,28},{1,29},{2,30},{3,31},{4,8},{5,9},{6,10},{7,11},{8,4},{9,5},... | collective-permute-start | bytes 196616 | tf_op jit(solution)/shard_map/ppermute | solution.py:290
  17.3 5.7 %collective-permute-start.2 = (f32[32,512]{1,0:T(8,128)S(1)}, f32[32,512]{1,0:T(8,128)S(1)}, u32[]{:S(2)}, u32[]{:S(2)}) collective-permute-start(f32[32,512]{1,0:T(8,128)S(1)} %shard_map.129.own), channel_id=1, source_target_pairs={{0,4},{1,5},{2,6},{3,7},{4,0},{5,1},{6,2},{7,3},{8,12},{9,13},{10,... | collective-permute-start | bytes 196616 | tf_op jit(solution)/shard_map/ppermute | solution.py:265
  19.2 15.1 %collective-permute-start.15 = (f32[4,176,128]{2,1,0:T(8,128)S(1)}, f32[4,176,128]{2,1,0:T(8,128)S(1)}, u32[]{:S(2)}, u32[]{:S(2)}) collective-permute-start(f32[4,176,128]{2,1,0:T(8,128)S(1)} %pad_maximum_fusion.refs_0_), channel_id=1, source_target_pairs={{0,4},{1,5},{2,6},{3,7},{4,0},{5,1},{6,2},{7,3},{8,12},{9,13},{10,... | collective-permute-start | bytes 1081352 | tf_op jit(solution)/shard_map/ppermute | solution.py:265
  19.6 14.0 %collective-permute-start.14 = (f32[3,176,128]{2,1,0:T(8,128)S(1)}, f32[3,176,128]{2,1,0:T(8,128)S(1)}, u32[]{:S(2)}, u32[]{:S(2)}) collective-permute-start(f32[3,176,128]{2,1,0:T(8,128)S(1)} %pad_maximum_fusion.1), channel_id=1, source_target_pairs={{0,2},{1,3},{2,0},{3,1},{4,6},{5,7},{6,4},{7,5},{8,10},{9,11},{10,... | collective-permute-start | bytes 811016 | tf_op jit(solution)/shard_map/ppermute | solution.py:265
  23.0 14.7 %copy-start = (bf16[1024,1024]{1,0:T(8,128)(2,1)S(1)}, bf16[1024,1024]{1,0:T(8,128)(2,1)}, u32[]{:S(2)}) copy-start(bf16[1024,1024]{1,0:T(8,128)(2,1)} %w_mid.1) | copy-start | bytes 6291460
  23.0 14.7 %copy-start.3 = (bf16[128,1024]{1,0:T(8,128)(2,1)S(1)}, bf16[128,1024]{1,0:T(8,128)(2,1)}, u32[]{:S(2)}) copy-start(bf16[128,1024]{1,0:T(8,128)(2,1)} %refs_7_.1) | copy-start | bytes 786436
  24.7 4.0 %collective-permute-start.5 = (f32[32,256]{1,0:T(8,128)S(1)}, f32[32,256]{1,0:T(8,128)S(1)}, u32[]{:S(2)}, u32[]{:S(2)}) collective-permute-start(f32[32,256]{1,0:T(8,128)S(1)} %get-tuple-element.36), channel_id=1, source_target_pairs={{0,2},{1,3},{2,0},{3,1},{4,6},{5,7},{6,4},{7,5},{8,10},{9,11},{10,... | collective-permute-start | bytes 98312 | tf_op jit(solution)/shard_map/ppermute | solution.py:265
  26.3 3.3 %collective-permute-start.6 = (f32[32,256]{1,0:T(8,128)S(1)}, f32[32,256]{1,0:T(8,128)S(1)}, u32[]{:S(2)}, u32[]{:S(2)}) collective-permute-start(f32[32,256]{1,0:T(8,128)S(1)} %get-tuple-element.37), channel_id=1, source_target_pairs={{0,3},{1,2},{2,1},{3,0},{4,7},{5,6},{6,5},{7,4},{8,11},{9,10},{10,... | collective-permute-start | bytes 98312 | tf_op jit(solution)/shard_map/ppermute | solution.py:265
  26.3 3.3 %collective-permute-start.4 = (f32[32,256]{1,0:T(8,128)S(1)}, f32[32,256]{1,0:T(8,128)S(1)}, u32[]{:S(2)}, u32[]{:S(2)}) collective-permute-start(f32[32,256]{1,0:T(8,128)S(1)} %get-tuple-element.37), channel_id=1, source_target_pairs={{0,1},{1,0},{2,3},{3,2},{4,5},{5,4},{6,7},{7,6},{8,9},{9,8},{10,11... | collective-permute-start | bytes 98312 | tf_op jit(solution)/shard_map/ppermute | solution.py:265
  29.7 6.5 %collective-permute-start.8 = (f32[4,32,256]{2,1,0:T(8,128)S(1)}, f32[4,32,256]{2,1,0:T(8,128)S(1)}, u32[]{:S(2)}, u32[]{:S(2)}) collective-permute-start(f32[4,32,256]{2,1,0:T(8,128)S(1)} %pad_maximum_fusion.4.refs_0_), channel_id=1, source_target_pairs={{0,8},{1,9},{2,10},{3,11},{4,12},{5,13},{6,14},{7,15},{8,0},{9,1},... | collective-permute-start | bytes 393224 | tf_op jit(solution)/shard_map/ppermute | solution.py:265
  30.7 6.9 %collective-permute-start.7 = (f32[4,32,256]{2,1,0:T(8,128)S(1)}, f32[4,32,256]{2,1,0:T(8,128)S(1)}, u32[]{:S(2)}, u32[]{:S(2)}) collective-permute-start(f32[4,32,256]{2,1,0:T(8,128)S(1)} %pad_maximum_fusion.4.refs_0_), channel_id=1, source_target_pairs={{0,4},{1,5},{2,6},{3,7},{4,0},{5,1},{6,2},{7,3},{8,12},{9,13},{10,... | collective-permute-start | bytes 393224 | tf_op jit(solution)/shard_map/ppermute | solution.py:265
  30.9 12.4 %collective-permute-start.10 = (f32[4,32,256]{2,1,0:T(8,128)S(1)}, f32[4,32,256]{2,1,0:T(8,128)S(1)}, u32[]{:S(2)}, u32[]{:S(2)}) collective-permute-start(f32[4,32,256]{2,1,0:T(8,128)S(1)} %pad_maximum_fusion.4.refs_0_), channel_id=1, source_target_pairs={{0,16},{1,17},{2,18},{3,19},{4,20},{5,21},{6,22},{7,23},{8,24},{9,... | collective-permute-start | bytes 393224 | tf_op jit(solution)/shard_map/ppermute | solution.py:265
  33.6 9.7 %collective-permute-start.9 = (f32[4,32,256]{2,1,0:T(8,128)S(1)}, f32[4,32,256]{2,1,0:T(8,128)S(1)}, u32[]{:S(2)}, u32[]{:S(2)}) collective-permute-start(f32[4,32,256]{2,1,0:T(8,128)S(1)} %pad_maximum_fusion.4.refs_0_), channel_id=1, source_target_pairs={{0,24},{1,25},{2,26},{3,27},{4,28},{5,29},{6,30},{7,31},{8,16},{9,... | collective-permute-start | bytes 393224 | tf_op jit(solution)/shard_map/ppermute | solution.py:265
  34.4 7.6 %collective-permute-start.16 = (f32[3,176,128]{2,1,0:T(8,128)S(1)}, f32[3,176,128]{2,1,0:T(8,128)S(1)}, u32[]{:S(2)}, u32[]{:S(2)}) collective-permute-start(f32[3,176,128]{2,1,0:T(8,128)S(1)} %collective-permute-done.14.refs_1_), channel_id=1, source_target_pairs={{0,4},{1,5},{2,6},{3,7},{4,0},{5,1},{6,2},{7,3},{8,12},{9,13},{10,... | collective-permute-start | bytes 811016 | tf_op jit(solution)/shard_map/ppermute | solution.py:265
  36.2 5.8 %collective-permute-start.17 = (f32[2,176,128]{2,1,0:T(8,128)S(1)}, f32[2,176,128]{2,1,0:T(8,128)S(1)}, u32[]{:S(2)}, u32[]{:S(2)}) collective-permute-start(f32[2,176,128]{2,1,0:T(8,128)S(1)} %pad_maximum_fusion.3), channel_id=1, source_target_pairs={{0,2},{1,3},{2,0},{3,1},{4,6},{5,7},{6,4},{7,5},{8,10},{9,11},{10,... | collective-permute-start | bytes 540680 | tf_op jit(solution)/shard_map/ppermute | solution.py:265
  41.4 11.5 %collective-permute-start.18 = (f32[4,32,256]{2,1,0:T(8,128)S(1)}, f32[4,32,256]{2,1,0:T(8,128)S(1)}, u32[]{:S(2)}, u32[]{:S(2)}) collective-permute-start(f32[4,32,256]{2,1,0:T(8,128)S(1)} %collective-permute-done.8.refs_2_), channel_id=1, source_target_pairs={{0,4},{1,5},{2,6},{3,7},{4,0},{5,1},{6,2},{7,3},{8,12},{9,13},{10,... | collective-permute-start | bytes 393224 | tf_op jit(solution)/shard_map/ppermute | solution.py:265
  43.4 9.4 %collective-permute-start.19 = (f32[2,4,32,256]{3,2,1,0:T(8,128)S(1)}, f32[2,4,32,256]{3,2,1,0:T(8,128)S(1)}, u32[]{:S(2)}, u32[]{:S(2)}) collective-permute-start(f32[2,4,32,256]{3,2,1,0:T(8,128)S(1)} %pad_maximum_fusion.2), channel_id=1, source_target_pairs={{0,4},{1,5},{2,6},{3,7},{4,0},{5,1},{6,2},{7,3},{8,12},{9,13},{10,... | collective-permute-start | bytes 786440 | tf_op jit(solution)/shard_map/ppermute | solution.py:265
  57.5 3.0 %collective-permute-start.21 = (f32[300,1024]{1,0:T(8,128)S(1)}, f32[300,1024]{1,0:T(8,128)S(1)}, u32[]{:S(2)}, u32[]{:S(2)}) collective-permute-start(f32[300,1024]{1,0:T(8,128)S(1)} %get-tuple-element.61.mine), channel_id=1, source_target_pairs={{0,1},{1,0},{2,3},{3,2},{4,5},{5,4},{6,7},{7,6},{8,9},{9,8},{10,11... | collective-permute-start | bytes 3686408 | tf_op jit(solution)/shard_map/ppermute | solution.py:265
  59.7 2.1 %collective-permute-start.20 = (f32[128,1024]{1,0:T(8,128)S(1)}, f32[128,1024]{1,0:T(8,128)S(1)}, u32[]{:S(2)}, u32[]{:S(2)}) collective-permute-start(f32[128,1024]{1,0:T(8,128)S(1)} %shard_map.137.mine), channel_id=1, source_target_pairs={{0,1},{1,0},{2,3},{3,2},{4,5},{5,4},{6,7},{7,6},{8,9},{9,8},{10,11... | collective-permute-start | bytes 1572872 | tf_op jit(solution)/shard_map/ppermute | solution.py:265
  (7 other events, 30.1 us)

commit v7 on v6

--- a/solution.py
+++ b/solution.py
@@ -60,7 +60,7 @@
         packed[classes + rows :, :] = jnp.zeros((extra - rows, width), F32)
 
 
-def operate(place, live, row, col, own, near, far, tiles, field, owners):
+def operate(place, live, row, col, own, near, far, tiles, field, sums, owners):
     capacity, size, _ = tiles.shape
     count = own.shape[1] // size
     dom = place[0]
@@ -73,26 +73,24 @@
         field[near_base + index] = pieces(near[:, cut])
         field[far_base + index] = pieces(far[:, cut])
     total = count * owners
-    sums = [jnp.zeros((own.shape[0], size), F32) for _ in range(count)]
+    sums[...] = jnp.zeros_like(sums)
     for slot in range(capacity):
         relative = lax.rem(col[slot] - dom * count + count + total, total)
-        target = jnp.where(slot < live[0], row[slot], -1)
         product = whole(
             lax.dot_general(field[relative], tiles[slot], TRAILING, preferred_element_type=F32)
         )
-        for index in range(count):
-            sums[index] = sums[index] + jnp.where(target == index, product, 0.0)
-    return jnp.concatenate(sums, axis=1)
-
-
-def first_kernel(owners, place, live, row, col, own, near, far, tiles, first, field):
-    first[...] = operate(place, live, row, col, own, near, far, tiles, field, owners)
+        sums[row[slot]] += jnp.where(slot < live[0], product, 0.0)
+    return jnp.concatenate([sums[index] for index in range(count)], axis=1)
+
+
+def first_kernel(owners, place, live, row, col, own, near, far, tiles, first, field, sums):
+    first[...] = operate(place, live, row, col, own, near, far, tiles, field, sums, owners)
 
 
 def second_kernel(
-    owners, place, live, row, col, own, near, far, tiles, features, rank_row, mine, other, field
+    owners, place, live, row, col, own, near, far, tiles, features, rank_row, mine, other, field, sums
 ):
-    applied = operate(place, live, row, col, own, near, far, tiles, field, owners)
+    applied = operate(place, live, row, col, own, near, far, tiles, field, sums, owners)
     base = features[...]
     second = 2.0 * applied - base
     diffused = series_zero * base + series_one * own[...] + series_two * second
@@ -303,12 +301,13 @@
         [dest_slot.reshape(1, -1), cotangent, opened],
     )
     field = pltpu.VMEM((3 * count, 3 * feature_count, size), BF16)
+    sums = pltpu.VMEM((count, feature_count, size), F32)
     first = call(
         functools.partial(first_kernel, owners),
         jax.ShapeDtypeStruct(features.shape, F32),
         scalars,
         [features, near_one, far_one, tiles],
-        [field],
+        [field, sums],
     )
     line = [packed] + [send(packed, m) for m in (8, 16, 24)]
     column = jnp.stack(line)
@@ -321,7 +320,7 @@
         tuple(jax.ShapeDtypeStruct((feature_count, half), F32) for _ in range(2)),
         scalars,
         [first, near_two, far_two, tiles, features, rank_row],
-        [field],
+        [field, sums],
     )
     own = jnp.stack([mine, send(other, 1), send(mine, 2), send(other, 3)])
     facing = send(own, 4)

time: 62.8 us -> 62.7 us (level)
  transfers between devices with their start and end apart: 22 -> 22, of which waited for: 8 -> 7; matrix products, arithmetic and copies ran while one was open for 0% -> 0% of each run, Pallas kernels for 34% -> 34%
where the time goes in v7:
time: 62.7 us; the launch traced here: 62.5 us
  starting transfers between devices  27.4 us (44%)
  Pallas kernels  26.5 us (42%)
  waiting for transfers between devices  6.57 us (10%)
  between operations  1.51 us (2%)
    pallas_call x11, Pallas kernels, call(): pl.pallas_call(kernel, out_shape=outs, in_specs=[SMEM] * len(scalars) + [...  26.5 us
    ppermute x20, starting transfers between devices, exchanged(): return lax.ppermute(value, AXES, [(i, i ^ mask) for i in range(devices)])  19.4 us
    ppermute x2, starting transfers between devices, far(): return lax.ppermute(value, AXES, far_pairs)  8 us
    ppermute x20, waiting for transfers between devices, exchanged(): return lax.ppermute(value, AXES, [(i, i ^ mask) for i in range(devices)])  5.29 us
    ppermute x2, waiting for transfers between devices, far(): return lax.ppermute(value, AXES, far_pairs)  1.28 us
  transfers between devices with their start and end apart: 22, of which 7 were waited for; matrix products, arithmetic and copies ran while one was open for 0% of the time, Pallas kernels for 34%

profile of v7, /device:TPU:0, one launch (start us, length us, event | category | flops | bytes accessed | tf_op | source)
XLA Modules:
  0.0 62.5 jit_solution(7263864196971667291)
XLA Ops:
  0.6 6.0 %collective-permute-start.1 = (f32[32,512]{1,0:T(8,128)}, f32[32,512]{1,0:T(8,128)S(1)}, u32[]{:S(2)}, u32[]{:S(2)}) collective-permute-start(f32[32,512]{1,0:T(8,128)} %features.1), channel_id=1, source_target_pairs={{0,28},{1,29},{2,30},{3,31},{4,8},{5,9},{6,10},{7,11},{8,4},{9,5},... | collective-permute-start | bytes 196616 | tf_op jit(solution)/shard_map/ppermute | solution.py:288
  7.6 1.1 %shard_map.131 = (f32[176,128]{1,0:T(8,128)S(1)}, s32[1,512]{1,0:T(1,128)S(1)}) custom-call(s32[2]{0:T(128)S(1)} %pad_add_fusion.place, s32[1,512]{1,0:T(1,128)S(1)} %bitcast.22, bf16[172,128]{1,0:T(8,128)(2,1)S(1)} %copy-done.5, f32[8,128]{1,0:T(8,128)S(1)} %shard_map.130.opened), custom_call_target="tpu_custom_call" | custom-call | flops 1500000000 | bytes 5400000 | tf_op jit(solution)/shard_map/pallas_call | solution.py:251
  9.4 0.9 %collective-permute-start.12 = (f32[176,128]{1,0:T(8,128)S(1)}, f32[176,128]{1,0:T(8,128)S(1)}, u32[]{:S(2)}, u32[]{:S(2)}) collective-permute-start(f32[176,128]{1,0:T(8,128)S(1)} %get-tuple-element.43), channel_id=1, source_target_pairs={{0,16},{1,17},{2,18},{3,19},{4,20},{5,21},{6,22},{7,23},{8,24},{9,... | collective-permute-start | bytes 270344 | tf_op jit(solution)/shard_map/ppermute | solution.py:263
  10.3 2.8 %collective-permute-start.11 = (f32[176,128]{1,0:T(8,128)S(1)}, f32[176,128]{1,0:T(8,128)S(1)}, u32[]{:S(2)}, u32[]{:S(2)}) collective-permute-start(f32[176,128]{1,0:T(8,128)S(1)} %get-tuple-element.43), channel_id=1, source_target_pairs={{0,8},{1,9},{2,10},{3,11},{4,12},{5,13},{6,14},{7,15},{8,0},{9,1},... | collective-permute-start | bytes 270344 | tf_op jit(solution)/shard_map/ppermute | solution.py:263
  13.8 1.5 %shard_map.129.own = f32[32,512]{1,0:T(8,128)S(1)} custom-call(s32[2]{0:T(128)S(1)} %pad_add_fusion.place, s32[1]{0:T(128)S(6)} %copy.14.live, s32[40]{0:T(128)S(1)} %copy-done.7, s32[40]{0:T(128)S(1)} %copy-done.8, f32[32,512]{1,0:T(8,128)S(1)} %copy-done.4, f32[32,512]{1,0:T(8,128)S(1)} %collective-permute-done.near, ...), custom_call_target="tpu_custom_call" | custom-call | flops 1500000000 | bytes 5400000 | tf_op jit(solution)/shard_map/pallas_call | solution.py:251
  15.3 2.0 %collective-permute-start.3 = (f32[32,512]{1,0:T(8,128)S(1)}, f32[32,512]{1,0:T(8,128)S(1)}, u32[]{:S(2)}, u32[]{:S(2)}) collective-permute-start(f32[32,512]{1,0:T(8,128)S(1)} %shard_map.129.own), channel_id=1, source_target_pairs={{0,28},{1,29},{2,30},{3,31},{4,8},{5,9},{6,10},{7,11},{8,4},{9,5},... | collective-permute-start | bytes 196616 | tf_op jit(solution)/shard_map/ppermute | solution.py:288
  17.5 1.7 %collective-permute-done.12 = f32[176,128]{1,0:T(8,128)S(1)} collective-permute-done((f32[176,128]{1,0:T(8,128)S(1)}, f32[176,128]{1,0:T(8,128)S(1)}, u32[]{:S(2)}, u32[]{:S(2)}) %collective-permute-start.12) | collective-permute-done | bytes 90144 | tf_op jit(solution)/shard_map/ppermute | solution.py:263
  19.6 1.6 %collective-permute-start.14 = (f32[3,176,128]{2,1,0:T(8,128)S(1)}, f32[3,176,128]{2,1,0:T(8,128)S(1)}, u32[]{:S(2)}, u32[]{:S(2)}) collective-permute-start(f32[3,176,128]{2,1,0:T(8,128)S(1)} %pad_maximum_fusion.1), channel_id=1, source_target_pairs={{0,2},{1,3},{2,0},{3,1},{4,6},{5,7},{6,4},{7,5},{8,10},{9,11},{10,... | collective-permute-start | bytes 811016 | tf_op jit(solution)/shard_map/ppermute | solution.py:263
  21.2 1.3 %collective-permute-done.3.far = f32[32,512]{1,0:T(8,128)S(1)} collective-permute-done((f32[32,512]{1,0:T(8,128)S(1)}, f32[32,512]{1,0:T(8,128)S(1)}, u32[]{:S(2)}, u32[]{:S(2)}) %collective-permute-start.3) | collective-permute-done | bytes 65568 | tf_op jit(solution)/shard_map/ppermute | solution.py:288
  23.0 1.7 %shard_map.132 = (f32[32,256]{1,0:T(8,128)S(1)}, f32[32,256]{1,0:T(8,128)S(1)}) custom-call(s32[2]{0:T(128)S(1)} %pad_add_fusion.place, s32[1]{0:T(128)S(6)} %copy.14.live, s32[40]{0:T(128)S(1)} %copy-done.7, s32[40]{0:T(128)S(1)} %copy-done.8, f32[32,512]{1,0:T(8,128)S(1)} %shard_map.129.own, f32[32,512]{1,0:T(8,128)S(1)} %collective-permute-done.2.near, ...), custom_call_target="tpu_custom_call" | custom-call | flops 1500000000 | bytes 5400000 | tf_op jit(solution)/shard_map/pallas_call | solution.py:251
  24.7 1.6 %collective-permute-start.5 = (f32[32,256]{1,0:T(8,128)S(1)}, f32[32,256]{1,0:T(8,128)S(1)}, u32[]{:S(2)}, u32[]{:S(2)}) collective-permute-start(f32[32,256]{1,0:T(8,128)S(1)} %get-tuple-element.36), channel_id=1, source_target_pairs={{0,2},{1,3},{2,0},{3,1},{4,6},{5,7},{6,4},{7,5},{8,10},{9,11},{10,... | collective-permute-start | bytes 98312 | tf_op jit(solution)/shard_map/ppermute | solution.py:263
  26.8 1.8 %collective-permute-done.5 = f32[32,256]{1,0:T(8,128)S(1)} collective-permute-done((f32[32,256]{1,0:T(8,128)S(1)}, f32[32,256]{1,0:T(8,128)S(1)}, u32[]{:S(2)}, u32[]{:S(2)}) %collective-permute-start.5) | collective-permute-done | bytes 32800 | tf_op jit(solution)/shard_map/ppermute | solution.py:263
  28.6 1.0 %collective-permute-done.6 = f32[32,256]{1,0:T(8,128)S(1)} collective-permute-done((f32[32,256]{1,0:T(8,128)S(1)}, f32[32,256]{1,0:T(8,128)S(1)}, u32[]{:S(2)}, u32[]{:S(2)}) %collective-permute-start.6) | collective-permute-done | bytes 32800 | tf_op jit(solution)/shard_map/ppermute | solution.py:263
  29.6 1.0 %collective-permute-start.8 = (f32[4,32,256]{2,1,0:T(8,128)S(1)}, f32[4,32,256]{2,1,0:T(8,128)S(1)}, u32[]{:S(2)}, u32[]{:S(2)}) collective-permute-start(f32[4,32,256]{2,1,0:T(8,128)S(1)} %pad_maximum_fusion.4.refs_0_), channel_id=1, source_target_pairs={{0,8},{1,9},{2,10},{3,11},{4,12},{5,13},{6,14},{7,15},{8,0},{9,1},... | collective-permute-start | bytes 393224 | tf_op jit(solution)/shard_map/ppermute | solution.py:263
  30.7 2.8 %collective-permute-start.10 = (f32[4,32,256]{2,1,0:T(8,128)S(1)}, f32[4,32,256]{2,1,0:T(8,128)S(1)}, u32[]{:S(2)}, u32[]{:S(2)}) collective-permute-start(f32[4,32,256]{2,1,0:T(8,128)S(1)} %pad_maximum_fusion.4.refs_0_), channel_id=1, source_target_pairs={{0,16},{1,17},{2,18},{3,19},{4,20},{5,21},{6,22},{7,23},{8,24},{9,... | collective-permute-start | bytes 393224 | tf_op jit(solution)/shard_map/ppermute | solution.py:263
  34.2 1.8 %collective-permute-start.16 = (f32[3,176,128]{2,1,0:T(8,128)S(1)}, f32[3,176,128]{2,1,0:T(8,128)S(1)}, u32[]{:S(2)}, u32[]{:S(2)}) collective-permute-start(f32[3,176,128]{2,1,0:T(8,128)S(1)} %collective-permute-done.14.refs_1_), channel_id=1, source_target_pairs={{0,4},{1,5},{2,6},{3,7},{4,0},{5,1},{6,2},{7,3},{8,12},{9,13},{10,... | collective-permute-start | bytes 811016 | tf_op jit(solution)/shard_map/ppermute | solution.py:263
  36.1 1.4 %collective-permute-start.17 = (f32[2,176,128]{2,1,0:T(8,128)S(1)}, f32[2,176,128]{2,1,0:T(8,128)S(1)}, u32[]{:S(2)}, u32[]{:S(2)}) collective-permute-start(f32[2,176,128]{2,1,0:T(8,128)S(1)} %pad_maximum_fusion.3), channel_id=1, source_target_pairs={{0,2},{1,3},{2,0},{3,1},{4,6},{5,7},{6,4},{7,5},{8,10},{9,11},{10,... | collective-permute-start | bytes 540680 | tf_op jit(solution)/shard_map/ppermute | solution.py:263
  37.5 3.7 %shard_map.133 = (bf16[768,128]{1,0:T(8,128)(2,1)S(1)}, bf16[768,1024]{1,0:T(8,128)(2,1)S(1)}, f32[768,1024]{1,0:T(8,128)S(1)}, f32[768,1024]{1,0:T(8,128)S(1)}) custom-call(s32[2]{0:T(128)S(1)} %pad_add_fusion.place, f32[4,32,256]{2,1,0:T(8,128)S(1)} %pad_maximum_fusion.4.refs_0_, f32[4,32,256]{2,1,0:T(8,128)S(1)} %collective-permute-done.7.refs_1_, ...), custom_call_target="tpu_custom_call" | custom-call | flops 3700000000 | bytes 13320000 | tf_op jit(solution)/shard_map/pallas_call | solution.py:251
  42.1 1.3 %shard_map.134 = (bf16[8,256,172]{2,1,0:T(8,128)(2,1)S(1)}, f32[8,1,256]{2,1,0:T(1,128)S(1)}) custom-call(s32[2]{0:T(128)S(1)} %pad_add_fusion.place, f32[4,176,128]{2,1,0:T(8,128)S(1)} %pad_maximum_fusion.refs_0_, f32[3,176,128]{2,1,0:T(8,128)S(1)} %collective-permute-done.14.refs_1_, f32[4,176,128]{2,1,0:T(8,128)S(1)} %collective-permute-done.15.refs_2_, ...), custom_call_target="tpu_custom_call" | custom-call | flops 1500000000 | bytes 5400000 | tf_op jit(solution)/shard_map/pallas_call | solution.py:251
  43.5 1.3 %collective-permute-start.19 = (f32[2,4,32,256]{3,2,1,0:T(8,128)S(1)}, f32[2,4,32,256]{3,2,1,0:T(8,128)S(1)}, u32[]{:S(2)}, u32[]{:S(2)}) collective-permute-start(f32[2,4,32,256]{3,2,1,0:T(8,128)S(1)} %pad_maximum_fusion.2), channel_id=1, source_target_pairs={{0,4},{1,5},{2,6},{3,7},{4,0},{5,1},{6,2},{7,3},{8,12},{9,13},{10,... | collective-permute-start | bytes 786440 | tf_op jit(solution)/shard_map/ppermute | solution.py:263
  44.8 7.9 %shard_map.135 = (f32[300,1024]{1,0:T(8,128)S(1)}, f32[128,128]{1,0:T(8,128)S(1)}, f32[128,1024]{1,0:T(8,128)S(1)}) custom-call(s32[2]{0:T(128)S(1)} %pad_add_fusion.place, f32[4,32,256]{2,1,0:T(8,128)S(1)} %pad_maximum_fusion.4.refs_0_, f32[4,32,256]{2,1,0:T(8,128)S(1)} %collective-permute-done.7.refs_1_, f32[4,32,256]{2,1,0:T(8,128)S(1)} %collective-permute-done.8.refs_2_, ...), custom_call_target="tpu_custom_call" | custom-call | flops 12499999744 | bytes 45000000 | tf_op jit(solution)/shard_map/pallas_call | solution.py:251
  52.7 4.6 %shard_map.136 = (f32[300,1024]{1,0:T(8,128)S(1)}, f32[128,128]{1,0:T(8,128)}, bf16[128,768]{1,0:T(8,128)(2,1)S(1)}, bf16[768,1024]{1,0:T(8,128)(2,1)S(1)}, f32[768,1024]{1,0:T(8,128)S(1)}) custom-call(s32[2]{0:T(128)S(1)} %pad_add_fusion.place, f32[300,1024]{1,0:T(8,128)S(1)} %get-tuple-element.53.refs_0_, f32[128,128]{1,0:T(8,128)S(1)} %get-tuple-element.54.refs_1_, ...), custom_call_target="tpu_custom_call" | custom-call | flops 7500000256 | bytes 27000000 | tf_op jit(solution)/shard_map/pallas_call | solution.py:251
  57.5 2.1 %shard_map.137.mine = f32[128,1024]{1,0:T(8,128)S(1)} custom-call(f32[128,1024]{1,0:T(8,128)S(1)} %get-tuple-element.57.before, bf16[128,768]{1,0:T(8,128)(2,1)S(1)} %get-tuple-element.58.inputs, bf16[768,1024]{1,0:T(8,128)(2,1)S(1)} %get-tuple-element.59.delta_two, f32[768,1024]{1,0:T(8,128)S(1)} %get-tuple-element.60.slope_one, bf16[1024,1024]{1,0:T(8,128)(2,1)S(1)} %copy-done), custom_call_target="tpu_custom_call" | custom-call | flops 2500000000 | bytes 9000000 | tf_op jit(solution)/shard_map/pallas_call | solution.py:251
  60.4 1.2 %shard_map.138 = (f32[128,1024]{1,0:T(8,128)}, f32[172,1024]{1,0:T(8,128)}) custom-call(f32[300,1024]{1,0:T(8,128)S(1)} %get-tuple-element.61.mine, f32[300,1024]{1,0:T(8,128)S(1)} %collective-permute-done.21.theirs), custom_call_target="tpu_custom_call" | custom-call | flops 1500000000 | bytes 5400000 | tf_op jit(solution)/shard_map/pallas_call | solution.py:251
  (57 shorter events, 7.0 us)
Async XLA Ops:
  0.6 13.1 %collective-permute-start.1 = (f32[32,512]{1,0:T(8,128)}, f32[32,512]{1,0:T(8,128)S(1)}, u32[]{:S(2)}, u32[]{:S(2)}) collective-permute-start(f32[32,512]{1,0:T(8,128)} %features.1), channel_id=1, source_target_pairs={{0,28},{1,29},{2,30},{3,31},{4,8},{5,9},{6,10},{7,11},{8,4},{9,5},... | collective-permute-start | bytes 196616 | tf_op jit(solution)/shard_map/ppermute | solution.py:288
  6.7 7.1 %collective-permute-start = (f32[32,512]{1,0:T(8,128)}, f32[32,512]{1,0:T(8,128)S(1)}, u32[]{:S(2)}, u32[]{:S(2)}) collective-permute-start(f32[32,512]{1,0:T(8,128)} %features.1), channel_id=1, source_target_pairs={{0,4},{1,5},{2,6},{3,7},{4,0},{5,1},{6,2},{7,3},{8,12},{9,13},{10,... | collective-permute-start | bytes 196616 | tf_op jit(solution)/shard_map/ppermute | solution.py:263
  8.7 8.8 %collective-permute-start.13 = (f32[176,128]{1,0:T(8,128)S(1)}, f32[176,128]{1,0:T(8,128)S(1)}, u32[]{:S(2)}, u32[]{:S(2)}) collective-permute-start(f32[176,128]{1,0:T(8,128)S(1)} %get-tuple-element.43), channel_id=1, source_target_pairs={{0,24},{1,25},{2,26},{3,27},{4,28},{5,29},{6,30},{7,31},{8,16},{9,... | collective-permute-start | bytes 270344 | tf_op jit(solution)/shard_map/ppermute | solution.py:263
  9.4 9.8 %collective-permute-start.12 = (f32[176,128]{1,0:T(8,128)S(1)}, f32[176,128]{1,0:T(8,128)S(1)}, u32[]{:S(2)}, u32[]{:S(2)}) collective-permute-start(f32[176,128]{1,0:T(8,128)S(1)} %get-tuple-element.43), channel_id=1, source_target_pairs={{0,16},{1,17},{2,18},{3,19},{4,20},{5,21},{6,22},{7,23},{8,24},{9,... | collective-permute-start | bytes 270344 | tf_op jit(solution)/shard_map/ppermute | solution.py:263
  10.3 8.9 %collective-permute-start.11 = (f32[176,128]{1,0:T(8,128)S(1)}, f32[176,128]{1,0:T(8,128)S(1)}, u32[]{:S(2)}, u32[]{:S(2)}) collective-permute-start(f32[176,128]{1,0:T(8,128)S(1)} %get-tuple-element.43), channel_id=1, source_target_pairs={{0,8},{1,9},{2,10},{3,11},{4,12},{5,13},{6,14},{7,15},{8,0},{9,1},... | collective-permute-start | bytes 270344 | tf_op jit(solution)/shard_map/ppermute | solution.py:263
  15.3 7.1 %collective-permute-start.3 = (f32[32,512]{1,0:T(8,128)S(1)}, f32[32,512]{1,0:T(8,128)S(1)}, u32[]{:S(2)}, u32[]{:S(2)}) collective-permute-start(f32[32,512]{1,0:T(8,128)S(1)} %shard_map.129.own), channel_id=1, source_target_pairs={{0,28},{1,29},{2,30},{3,31},{4,8},{5,9},{6,10},{7,11},{8,4},{9,5},... | collective-permute-start | bytes 196616 | tf_op jit(solution)/shard_map/ppermute | solution.py:288
  17.3 5.7 %collective-permute-start.2 = (f32[32,512]{1,0:T(8,128)S(1)}, f32[32,512]{1,0:T(8,128)S(1)}, u32[]{:S(2)}, u32[]{:S(2)}) collective-permute-start(f32[32,512]{1,0:T(8,128)S(1)} %shard_map.129.own), channel_id=1, source_target_pairs={{0,4},{1,5},{2,6},{3,7},{4,0},{5,1},{6,2},{7,3},{8,12},{9,13},{10,... | collective-permute-start | bytes 196616 | tf_op jit(solution)/shard_map/ppermute | solution.py:263
  19.2 15.0 %collective-permute-start.15 = (f32[4,176,128]{2,1,0:T(8,128)S(1)}, f32[4,176,128]{2,1,0:T(8,128)S(1)}, u32[]{:S(2)}, u32[]{:S(2)}) collective-permute-start(f32[4,176,128]{2,1,0:T(8,128)S(1)} %pad_maximum_fusion.refs_0_), channel_id=1, source_target_pairs={{0,4},{1,5},{2,6},{3,7},{4,0},{5,1},{6,2},{7,3},{8,12},{9,13},{10,... | collective-permute-start | bytes 1081352 | tf_op jit(solution)/shard_map/ppermute | solution.py:263
  19.6 13.9 %collective-permute-start.14 = (f32[3,176,128]{2,1,0:T(8,128)S(1)}, f32[3,176,128]{2,1,0:T(8,128)S(1)}, u32[]{:S(2)}, u32[]{:S(2)}) collective-permute-start(f32[3,176,128]{2,1,0:T(8,128)S(1)} %pad_maximum_fusion.1), channel_id=1, source_target_pairs={{0,2},{1,3},{2,0},{3,1},{4,6},{5,7},{6,4},{7,5},{8,10},{9,11},{10,... | collective-permute-start | bytes 811016 | tf_op jit(solution)/shard_map/ppermute | solution.py:263
  23.0 14.6 %copy-start = (bf16[1024,1024]{1,0:T(8,128)(2,1)S(1)}, bf16[1024,1024]{1,0:T(8,128)(2,1)}, u32[]{:S(2)}) copy-start(bf16[1024,1024]{1,0:T(8,128)(2,1)} %w_mid.1) | copy-start | bytes 6291460
  23.0 14.6 %copy-start.3 = (bf16[128,1024]{1,0:T(8,128)(2,1)S(1)}, bf16[128,1024]{1,0:T(8,128)(2,1)}, u32[]{:S(2)}) copy-start(bf16[128,1024]{1,0:T(8,128)(2,1)} %refs_7_.1) | copy-start | bytes 786436
  24.7 3.9 %collective-permute-start.5 = (f32[32,256]{1,0:T(8,128)S(1)}, f32[32,256]{1,0:T(8,128)S(1)}, u32[]{:S(2)}, u32[]{:S(2)}) collective-permute-start(f32[32,256]{1,0:T(8,128)S(1)} %get-tuple-element.36), channel_id=1, source_target_pairs={{0,2},{1,3},{2,0},{3,1},{4,6},{5,7},{6,4},{7,5},{8,10},{9,11},{10,... | collective-permute-start | bytes 98312 | tf_op jit(solution)/shard_map/ppermute | solution.py:263
  26.2 3.3 %collective-permute-start.6 = (f32[32,256]{1,0:T(8,128)S(1)}, f32[32,256]{1,0:T(8,128)S(1)}, u32[]{:S(2)}, u32[]{:S(2)}) collective-permute-start(f32[32,256]{1,0:T(8,128)S(1)} %get-tuple-element.37), channel_id=1, source_target_pairs={{0,3},{1,2},{2,1},{3,0},{4,7},{5,6},{6,5},{7,4},{8,11},{9,10},{10,... | collective-permute-start | bytes 98312 | tf_op jit(solution)/shard_map/ppermute | solution.py:263
  26.2 3.3 %collective-permute-start.4 = (f32[32,256]{1,0:T(8,128)S(1)}, f32[32,256]{1,0:T(8,128)S(1)}, u32[]{:S(2)}, u32[]{:S(2)}) collective-permute-start(f32[32,256]{1,0:T(8,128)S(1)} %get-tuple-element.37), channel_id=1, source_target_pairs={{0,1},{1,0},{2,3},{3,2},{4,5},{5,4},{6,7},{7,6},{8,9},{9,8},{10,11... | collective-permute-start | bytes 98312 | tf_op jit(solution)/shard_map/ppermute | solution.py:263
  29.6 6.5 %collective-permute-start.8 = (f32[4,32,256]{2,1,0:T(8,128)S(1)}, f32[4,32,256]{2,1,0:T(8,128)S(1)}, u32[]{:S(2)}, u32[]{:S(2)}) collective-permute-start(f32[4,32,256]{2,1,0:T(8,128)S(1)} %pad_maximum_fusion.4.refs_0_), channel_id=1, source_target_pairs={{0,8},{1,9},{2,10},{3,11},{4,12},{5,13},{6,14},{7,15},{8,0},{9,1},... | collective-permute-start | bytes 393224 | tf_op jit(solution)/shard_map/ppermute | solution.py:263
  30.6 6.9 %collective-permute-start.7 = (f32[4,32,256]{2,1,0:T(8,128)S(1)}, f32[4,32,256]{2,1,0:T(8,128)S(1)}, u32[]{:S(2)}, u32[]{:S(2)}) collective-permute-start(f32[4,32,256]{2,1,0:T(8,128)S(1)} %pad_maximum_fusion.4.refs_0_), channel_id=1, source_target_pairs={{0,4},{1,5},{2,6},{3,7},{4,0},{5,1},{6,2},{7,3},{8,12},{9,13},{10,... | collective-permute-start | bytes 393224 | tf_op jit(solution)/shard_map/ppermute | solution.py:263
  30.7 12.7 %collective-permute-start.10 = (f32[4,32,256]{2,1,0:T(8,128)S(1)}, f32[4,32,256]{2,1,0:T(8,128)S(1)}, u32[]{:S(2)}, u32[]{:S(2)}) collective-permute-start(f32[4,32,256]{2,1,0:T(8,128)S(1)} %pad_maximum_fusion.4.refs_0_), channel_id=1, source_target_pairs={{0,16},{1,17},{2,18},{3,19},{4,20},{5,21},{6,22},{7,23},{8,24},{9,... | collective-permute-start | bytes 393224 | tf_op jit(solution)/shard_map/ppermute | solution.py:263
  33.5 9.9 %collective-permute-start.9 = (f32[4,32,256]{2,1,0:T(8,128)S(1)}, f32[4,32,256]{2,1,0:T(8,128)S(1)}, u32[]{:S(2)}, u32[]{:S(2)}) collective-permute-start(f32[4,32,256]{2,1,0:T(8,128)S(1)} %pad_maximum_fusion.4.refs_0_), channel_id=1, source_target_pairs={{0,24},{1,25},{2,26},{3,27},{4,28},{5,29},{6,30},{7,31},{8,16},{9,... | collective-permute-start | bytes 393224 | tf_op jit(solution)/shard_map/ppermute | solution.py:263
  34.2 7.9 %collective-permute-start.16 = (f32[3,176,128]{2,1,0:T(8,128)S(1)}, f32[3,176,128]{2,1,0:T(8,128)S(1)}, u32[]{:S(2)}, u32[]{:S(2)}) collective-permute-start(f32[3,176,128]{2,1,0:T(8,128)S(1)} %collective-permute-done.14.refs_1_), channel_id=1, source_target_pairs={{0,4},{1,5},{2,6},{3,7},{4,0},{5,1},{6,2},{7,3},{8,12},{9,13},{10,... | collective-permute-start | bytes 811016 | tf_op jit(solution)/shard_map/ppermute | solution.py:263
  36.1 6.0 %collective-permute-start.17 = (f32[2,176,128]{2,1,0:T(8,128)S(1)}, f32[2,176,128]{2,1,0:T(8,128)S(1)}, u32[]{:S(2)}, u32[]{:S(2)}) collective-permute-start(f32[2,176,128]{2,1,0:T(8,128)S(1)} %pad_maximum_fusion.3), channel_id=1, source_target_pairs={{0,2},{1,3},{2,0},{3,1},{4,6},{5,7},{6,4},{7,5},{8,10},{9,11},{10,... | collective-permute-start | bytes 540680 | tf_op jit(solution)/shard_map/ppermute | solution.py:263
  41.3 11.5 %collective-permute-start.18 = (f32[4,32,256]{2,1,0:T(8,128)S(1)}, f32[4,32,256]{2,1,0:T(8,128)S(1)}, u32[]{:S(2)}, u32[]{:S(2)}) collective-permute-start(f32[4,32,256]{2,1,0:T(8,128)S(1)} %collective-permute-done.8.refs_2_), channel_id=1, source_target_pairs={{0,4},{1,5},{2,6},{3,7},{4,0},{5,1},{6,2},{7,3},{8,12},{9,13},{10,... | collective-permute-start | bytes 393224 | tf_op jit(solution)/shard_map/ppermute | solution.py:263
  43.5 9.2 %collective-permute-start.19 = (f32[2,4,32,256]{3,2,1,0:T(8,128)S(1)}, f32[2,4,32,256]{3,2,1,0:T(8,128)S(1)}, u32[]{:S(2)}, u32[]{:S(2)}) collective-permute-start(f32[2,4,32,256]{3,2,1,0:T(8,128)S(1)} %pad_maximum_fusion.2), channel_id=1, source_target_pairs={{0,4},{1,5},{2,6},{3,7},{4,0},{5,1},{6,2},{7,3},{8,12},{9,13},{10,... | collective-permute-start | bytes 786440 | tf_op jit(solution)/shard_map/ppermute | solution.py:263
  57.4 3.0 %collective-permute-start.21 = (f32[300,1024]{1,0:T(8,128)S(1)}, f32[300,1024]{1,0:T(8,128)S(1)}, u32[]{:S(2)}, u32[]{:S(2)}) collective-permute-start(f32[300,1024]{1,0:T(8,128)S(1)} %get-tuple-element.61.mine), channel_id=1, source_target_pairs={{0,1},{1,0},{2,3},{3,2},{4,5},{5,4},{6,7},{7,6},{8,9},{9,8},{10,11... | collective-permute-start | bytes 3686408 | tf_op jit(solution)/shard_map/ppermute | solution.py:263
  59.6 2.1 %collective-permute-start.20 = (f32[128,1024]{1,0:T(8,128)S(1)}, f32[128,1024]{1,0:T(8,128)S(1)}, u32[]{:S(2)}, u32[]{:S(2)}) collective-permute-start(f32[128,1024]{1,0:T(8,128)S(1)} %shard_map.137.mine), channel_id=1, source_target_pairs={{0,1},{1,0},{2,3},{3,2},{4,5},{5,4},{6,7},{7,6},{8,9},{9,8},{10,11... | collective-permute-start | bytes 1572872 | tf_op jit(solution)/shard_map/ppermute | solution.py:263
  (7 other events, 30.1 us)

commit v8 on v7

--- a/solution.py
+++ b/solution.py
@@ -142,9 +142,10 @@
 
 
 def activated(pre):
-    gate = 0.5 * jnp.tanh(0.5 * pre) + 0.5
-    value = pre * gate
-    return value.astype(BF16), gate + value * (1.0 - gate)
+    half = 0.5 * pre
+    lift = jnp.tanh(half) + 1.0
+    value = half * lift
+    return value.astype(BF16), lift + value * (2.0 - lift)
 
 
 def feature_rows(source, rep):
@@ -236,11 +237,11 @@
     )
 
 
-def add_kernel(split, mine, theirs, *outs):
+def add_kernel(scales, mine, theirs, *outs):
     start = 0
-    for out in outs:
-        cut = slice(start, start + out.shape[0]) if split else slice(None)
-        out[...] = mine[cut, :] + theirs[cut, :]
+    for out, scale in zip(outs, scales):
+        cut = slice(start, start + out.shape[0])
+        out[...] = (mine[cut, :] + theirs[cut, :]) * scale
         start += out.shape[0]
 
 
@@ -398,10 +399,10 @@
     grad_in = call(last_kernel, in_shape, [], [in_before, *rest, w_mid], micros=2.5, mib=12)
     their_in = send(grad_in, 1)
     grad_mid, grad_out = call(
-        functools.partial(add_kernel, True), (mid_shape, out_shape), [], [grads, theirs]
+        functools.partial(add_kernel, (0.5, 1.0)), (mid_shape, out_shape), [], [grads, theirs]
     )
     their_in, grad_mid = lax.optimization_barrier((their_in, grad_mid))
-    grad_in = call(functools.partial(add_kernel, False), (in_shape,), [], [grad_in, their_in])[0]
+    grad_in = call(functools.partial(add_kernel, (0.25,)), (in_shape,), [], [grad_in, their_in])[0]
     return batch_features, grad_in, grad_mid, grad_out
 
 

time: 62.7 us -> 62.9 us (level)
  no operation moved by 1% of the time
where the time goes in v8:
time: 62.9 us; the launch traced here: 62.7 us
  starting transfers between devices  27.5 us (44%)
  Pallas kernels  26.7 us (42%)
  waiting for transfers between devices  6.55 us (10%)
  between operations  1.5 us (2%)
    pallas_call x11, Pallas kernels, call(): pl.pallas_call(kernel, out_shape=outs, in_specs=[SMEM] * len(scalars) + [...  26.7 us
    ppermute x20, starting transfers between devices, exchanged(): return lax.ppermute(value, AXES, [(i, i ^ mask) for i in range(devices)])  19.5 us
    ppermute x2, starting transfers between devices, far(): return lax.ppermute(value, AXES, far_pairs)  8.01 us
    ppermute x20, waiting for transfers between devices, exchanged(): return lax.ppermute(value, AXES, [(i, i ^ mask) for i in range(devices)])  5.27 us
    ppermute x2, waiting for transfers between devices, far(): return lax.ppermute(value, AXES, far_pairs)  1.27 us
  transfers between devices with their start and end apart: 22, of which 7 were waited for; matrix products, arithmetic and copies ran while one was open for 0% of the time, Pallas kernels for 34%

profile of v8, /device:TPU:0, one launch (start us, length us, event | category | flops | bytes accessed | tf_op | source)
XLA Modules:
  0.0 62.7 jit_solution(4987645584135011689)
XLA Ops:
  0.6 6.0 %collective-permute-start.1 = (f32[32,512]{1,0:T(8,128)}, f32[32,512]{1,0:T(8,128)S(1)}, u32[]{:S(2)}, u32[]{:S(2)}) collective-permute-start(f32[32,512]{1,0:T(8,128)} %features.1), channel_id=1, source_target_pairs={{0,28},{1,29},{2,30},{3,31},{4,8},{5,9},{6,10},{7,11},{8,4},{9,5},... | collective-permute-start | bytes 196616 | tf_op jit(solution)/shard_map/ppermute | solution.py:289
  7.6 1.1 %shard_map.131 = (f32[176,128]{1,0:T(8,128)S(1)}, s32[1,512]{1,0:T(1,128)S(1)}) custom-call(s32[2]{0:T(128)S(1)} %pad_add_fusion.place, s32[1,512]{1,0:T(1,128)S(1)} %bitcast.22, bf16[172,128]{1,0:T(8,128)(2,1)S(1)} %copy-done.5, f32[8,128]{1,0:T(8,128)S(1)} %shard_map.130.opened), custom_call_target="tpu_custom_call" | custom-call | flops 1500000000 | bytes 5400000 | tf_op jit(solution)/shard_map/pallas_call | solution.py:252
  9.4 0.9 %collective-permute-start.12 = (f32[176,128]{1,0:T(8,128)S(1)}, f32[176,128]{1,0:T(8,128)S(1)}, u32[]{:S(2)}, u32[]{:S(2)}) collective-permute-start(f32[176,128]{1,0:T(8,128)S(1)} %get-tuple-element.43), channel_id=1, source_target_pairs={{0,16},{1,17},{2,18},{3,19},{4,20},{5,21},{6,22},{7,23},{8,24},{9,... | collective-permute-start | bytes 270344 | tf_op jit(solution)/shard_map/ppermute | solution.py:264
  10.3 2.8 %collective-permute-start.11 = (f32[176,128]{1,0:T(8,128)S(1)}, f32[176,128]{1,0:T(8,128)S(1)}, u32[]{:S(2)}, u32[]{:S(2)}) collective-permute-start(f32[176,128]{1,0:T(8,128)S(1)} %get-tuple-element.43), channel_id=1, source_target_pairs={{0,8},{1,9},{2,10},{3,11},{4,12},{5,13},{6,14},{7,15},{8,0},{9,1},... | collective-permute-start | bytes 270344 | tf_op jit(solution)/shard_map/ppermute | solution.py:264
  13.8 1.5 %shard_map.129.own = f32[32,512]{1,0:T(8,128)S(1)} custom-call(s32[2]{0:T(128)S(1)} %pad_add_fusion.place, s32[1]{0:T(128)S(6)} %copy.14.live, s32[40]{0:T(128)S(1)} %copy-done.7, s32[40]{0:T(128)S(1)} %copy-done.8, f32[32,512]{1,0:T(8,128)S(1)} %copy-done.4, f32[32,512]{1,0:T(8,128)S(1)} %collective-permute-done.near, ...), custom_call_target="tpu_custom_call" | custom-call | flops 1500000000 | bytes 5400000 | tf_op jit(solution)/shard_map/pallas_call | solution.py:252
  15.3 2.0 %collective-permute-start.3 = (f32[32,512]{1,0:T(8,128)S(1)}, f32[32,512]{1,0:T(8,128)S(1)}, u32[]{:S(2)}, u32[]{:S(2)}) collective-permute-start(f32[32,512]{1,0:T(8,128)S(1)} %shard_map.129.own), channel_id=1, source_target_pairs={{0,28},{1,29},{2,30},{3,31},{4,8},{5,9},{6,10},{7,11},{8,4},{9,5},... | collective-permute-start | bytes 196616 | tf_op jit(solution)/shard_map/ppermute | solution.py:289
  17.5 1.7 %collective-permute-done.12 = f32[176,128]{1,0:T(8,128)S(1)} collective-permute-done((f32[176,128]{1,0:T(8,128)S(1)}, f32[176,128]{1,0:T(8,128)S(1)}, u32[]{:S(2)}, u32[]{:S(2)}) %collective-permute-start.12) | collective-permute-done | bytes 90144 | tf_op jit(solution)/shard_map/ppermute | solution.py:264
  19.6 1.6 %collective-permute-start.14 = (f32[3,176,128]{2,1,0:T(8,128)S(1)}, f32[3,176,128]{2,1,0:T(8,128)S(1)}, u32[]{:S(2)}, u32[]{:S(2)}) collective-permute-start(f32[3,176,128]{2,1,0:T(8,128)S(1)} %pad_maximum_fusion.1), channel_id=1, source_target_pairs={{0,2},{1,3},{2,0},{3,1},{4,6},{5,7},{6,4},{7,5},{8,10},{9,11},{10,... | collective-permute-start | bytes 811016 | tf_op jit(solution)/shard_map/ppermute | solution.py:264
  21.2 1.3 %collective-permute-done.3.far = f32[32,512]{1,0:T(8,128)S(1)} collective-permute-done((f32[32,512]{1,0:T(8,128)S(1)}, f32[32,512]{1,0:T(8,128)S(1)}, u32[]{:S(2)}, u32[]{:S(2)}) %collective-permute-start.3) | collective-permute-done | bytes 65568 | tf_op jit(solution)/shard_map/ppermute | solution.py:289
  23.0 1.7 %shard_map.132 = (f32[32,256]{1,0:T(8,128)S(1)}, f32[32,256]{1,0:T(8,128)S(1)}) custom-call(s32[2]{0:T(128)S(1)} %pad_add_fusion.place, s32[1]{0:T(128)S(6)} %copy.14.live, s32[40]{0:T(128)S(1)} %copy-done.7, s32[40]{0:T(128)S(1)} %copy-done.8, f32[32,512]{1,0:T(8,128)S(1)} %shard_map.129.own, f32[32,512]{1,0:T(8,128)S(1)} %collective-permute-done.2.near, ...), custom_call_target="tpu_custom_call" | custom-call | flops 1500000000 | bytes 5400000 | tf_op jit(solution)/shard_map/pallas_call | solution.py:252
  24.7 1.5 %collective-permute-start.5 = (f32[32,256]{1,0:T(8,128)S(1)}, f32[32,256]{1,0:T(8,128)S(1)}, u32[]{:S(2)}, u32[]{:S(2)}) collective-permute-start(f32[32,256]{1,0:T(8,128)S(1)} %get-tuple-element.36), channel_id=1, source_target_pairs={{0,2},{1,3},{2,0},{3,1},{4,6},{5,7},{6,4},{7,5},{8,10},{9,11},{10,... | collective-permute-start | bytes 98312 | tf_op jit(solution)/shard_map/ppermute | solution.py:264
  26.8 1.8 %collective-permute-done.5 = f32[32,256]{1,0:T(8,128)S(1)} collective-permute-done((f32[32,256]{1,0:T(8,128)S(1)}, f32[32,256]{1,0:T(8,128)S(1)}, u32[]{:S(2)}, u32[]{:S(2)}) %collective-permute-start.5) | collective-permute-done | bytes 32800 | tf_op jit(solution)/shard_map/ppermute | solution.py:264
  28.6 0.9 %collective-permute-done.6 = f32[32,256]{1,0:T(8,128)S(1)} collective-permute-done((f32[32,256]{1,0:T(8,128)S(1)}, f32[32,256]{1,0:T(8,128)S(1)}, u32[]{:S(2)}, u32[]{:S(2)}) %collective-permute-start.6) | collective-permute-done | bytes 32800 | tf_op jit(solution)/shard_map/ppermute | solution.py:264
  29.5 1.0 %collective-permute-start.8 = (f32[4,32,256]{2,1,0:T(8,128)S(1)}, f32[4,32,256]{2,1,0:T(8,128)S(1)}, u32[]{:S(2)}, u32[]{:S(2)}) collective-permute-start(f32[4,32,256]{2,1,0:T(8,128)S(1)} %pad_maximum_fusion.4.refs_0_), channel_id=1, source_target_pairs={{0,8},{1,9},{2,10},{3,11},{4,12},{5,13},{6,14},{7,15},{8,0},{9,1},... | collective-permute-start | bytes 393224 | tf_op jit(solution)/shard_map/ppermute | solution.py:264
  30.7 2.7 %collective-permute-start.10 = (f32[4,32,256]{2,1,0:T(8,128)S(1)}, f32[4,32,256]{2,1,0:T(8,128)S(1)}, u32[]{:S(2)}, u32[]{:S(2)}) collective-permute-start(f32[4,32,256]{2,1,0:T(8,128)S(1)} %pad_maximum_fusion.4.refs_0_), channel_id=1, source_target_pairs={{0,16},{1,17},{2,18},{3,19},{4,20},{5,21},{6,22},{7,23},{8,24},{9,... | collective-permute-start | bytes 393224 | tf_op jit(solution)/shard_map/ppermute | solution.py:264
  34.2 1.8 %collective-permute-start.16 = (f32[3,176,128]{2,1,0:T(8,128)S(1)}, f32[3,176,128]{2,1,0:T(8,128)S(1)}, u32[]{:S(2)}, u32[]{:S(2)}) collective-permute-start(f32[3,176,128]{2,1,0:T(8,128)S(1)} %collective-permute-done.14.refs_1_), channel_id=1, source_target_pairs={{0,4},{1,5},{2,6},{3,7},{4,0},{5,1},{6,2},{7,3},{8,12},{9,13},{10,... | collective-permute-start | bytes 811016 | tf_op jit(solution)/shard_map/ppermute | solution.py:264
  36.1 1.4 %collective-permute-start.17 = (f32[2,176,128]{2,1,0:T(8,128)S(1)}, f32[2,176,128]{2,1,0:T(8,128)S(1)}, u32[]{:S(2)}, u32[]{:S(2)}) collective-permute-start(f32[2,176,128]{2,1,0:T(8,128)S(1)} %pad_maximum_fusion.3), channel_id=1, source_target_pairs={{0,2},{1,3},{2,0},{3,1},{4,6},{5,7},{6,4},{7,5},{8,10},{9,11},{10,... | collective-permute-start | bytes 540680 | tf_op jit(solution)/shard_map/ppermute | solution.py:264
  37.5 3.6 %shard_map.133 = (bf16[768,128]{1,0:T(8,128)(2,1)S(1)}, bf16[768,1024]{1,0:T(8,128)(2,1)S(1)}, f32[768,1024]{1,0:T(8,128)S(1)}, f32[768,1024]{1,0:T(8,128)S(1)}) custom-call(s32[2]{0:T(128)S(1)} %pad_add_fusion.place, f32[4,32,256]{2,1,0:T(8,128)S(1)} %pad_maximum_fusion.4.refs_0_, f32[4,32,256]{2,1,0:T(8,128)S(1)} %collective-permute-done.7.refs_1_, ...), custom_call_target="tpu_custom_call" | custom-call | flops 3700000000 | bytes 13320000 | tf_op jit(solution)/shard_map/pallas_call | solution.py:252
  42.0 1.3 %shard_map.134 = (bf16[8,256,172]{2,1,0:T(8,128)(2,1)S(1)}, f32[8,1,256]{2,1,0:T(1,128)S(1)}) custom-call(s32[2]{0:T(128)S(1)} %pad_add_fusion.place, f32[4,176,128]{2,1,0:T(8,128)S(1)} %pad_maximum_fusion.refs_0_, f32[3,176,128]{2,1,0:T(8,128)S(1)} %collective-permute-done.14.refs_1_, f32[4,176,128]{2,1,0:T(8,128)S(1)} %collective-permute-done.15.refs_2_, ...), custom_call_target="tpu_custom_call" | custom-call | flops 1500000000 | bytes 5400000 | tf_op jit(solution)/shard_map/pallas_call | solution.py:252
  43.4 1.3 %collective-permute-start.19 = (f32[2,4,32,256]{3,2,1,0:T(8,128)S(1)}, f32[2,4,32,256]{3,2,1,0:T(8,128)S(1)}, u32[]{:S(2)}, u32[]{:S(2)}) collective-permute-start(f32[2,4,32,256]{3,2,1,0:T(8,128)S(1)} %pad_maximum_fusion.2), channel_id=1, source_target_pairs={{0,4},{1,5},{2,6},{3,7},{4,0},{5,1},{6,2},{7,3},{8,12},{9,13},{10,... | collective-permute-start | bytes 786440 | tf_op jit(solution)/shard_map/ppermute | solution.py:264
  44.7 8.1 %shard_map.135 = (f32[300,1024]{1,0:T(8,128)S(1)}, f32[128,128]{1,0:T(8,128)S(1)}, f32[128,1024]{1,0:T(8,128)S(1)}) custom-call(s32[2]{0:T(128)S(1)} %pad_add_fusion.place, f32[4,32,256]{2,1,0:T(8,128)S(1)} %pad_maximum_fusion.4.refs_0_, f32[4,32,256]{2,1,0:T(8,128)S(1)} %collective-permute-done.7.refs_1_, f32[4,32,256]{2,1,0:T(8,128)S(1)} %collective-permute-done.8.refs_2_, ...), custom_call_target="tpu_custom_call" | custom-call | flops 12499999744 | bytes 45000000 | tf_op jit(solution)/shard_map/pallas_call | solution.py:252
  52.9 4.7 %shard_map.136 = (f32[300,1024]{1,0:T(8,128)S(1)}, f32[128,128]{1,0:T(8,128)}, bf16[128,768]{1,0:T(8,128)(2,1)S(1)}, bf16[768,1024]{1,0:T(8,128)(2,1)S(1)}, f32[768,1024]{1,0:T(8,128)S(1)}) custom-call(s32[2]{0:T(128)S(1)} %pad_add_fusion.place, f32[300,1024]{1,0:T(8,128)S(1)} %get-tuple-element.53.refs_0_, f32[128,128]{1,0:T(8,128)S(1)} %get-tuple-element.54.refs_1_, ...), custom_call_target="tpu_custom_call" | custom-call | flops 7500000256 | bytes 27000000 | tf_op jit(solution)/shard_map/pallas_call | solution.py:252
  57.7 2.1 %shard_map.137.mine = f32[128,1024]{1,0:T(8,128)S(1)} custom-call(f32[128,1024]{1,0:T(8,128)S(1)} %get-tuple-element.57.before, bf16[128,768]{1,0:T(8,128)(2,1)S(1)} %get-tuple-element.58.inputs, bf16[768,1024]{1,0:T(8,128)(2,1)S(1)} %get-tuple-element.59.delta_two, f32[768,1024]{1,0:T(8,128)S(1)} %get-tuple-element.60.slope_one, bf16[1024,1024]{1,0:T(8,128)(2,1)S(1)} %copy-done), custom_call_target="tpu_custom_call" | custom-call | flops 2500000000 | bytes 9000000 | tf_op jit(solution)/shard_map/pallas_call | solution.py:252
  60.6 1.2 %shard_map.138 = (f32[128,1024]{1,0:T(8,128)}, f32[172,1024]{1,0:T(8,128)}) custom-call(f32[300,1024]{1,0:T(8,128)S(1)} %get-tuple-element.61.mine, f32[300,1024]{1,0:T(8,128)S(1)} %collective-permute-done.21.theirs), custom_call_target="tpu_custom_call" | custom-call | flops 1500000000 | bytes 5400000 | tf_op jit(solution)/shard_map/pallas_call | solution.py:252
  (57 shorter events, 7.0 us)
Async XLA Ops:
  0.6 13.1 %collective-permute-start.1 = (f32[32,512]{1,0:T(8,128)}, f32[32,512]{1,0:T(8,128)S(1)}, u32[]{:S(2)}, u32[]{:S(2)}) collective-permute-start(f32[32,512]{1,0:T(8,128)} %features.1), channel_id=1, source_target_pairs={{0,28},{1,29},{2,30},{3,31},{4,8},{5,9},{6,10},{7,11},{8,4},{9,5},... | collective-permute-start | bytes 196616 | tf_op jit(solution)/shard_map/ppermute | solution.py:289
  6.7 7.1 %collective-permute-start = (f32[32,512]{1,0:T(8,128)}, f32[32,512]{1,0:T(8,128)S(1)}, u32[]{:S(2)}, u32[]{:S(2)}) collective-permute-start(f32[32,512]{1,0:T(8,128)} %features.1), channel_id=1, source_target_pairs={{0,4},{1,5},{2,6},{3,7},{4,0},{5,1},{6,2},{7,3},{8,12},{9,13},{10,... | collective-permute-start | bytes 196616 | tf_op jit(solution)/shard_map/ppermute | solution.py:264
  8.7 8.8 %collective-permute-start.13 = (f32[176,128]{1,0:T(8,128)S(1)}, f32[176,128]{1,0:T(8,128)S(1)}, u32[]{:S(2)}, u32[]{:S(2)}) collective-permute-start(f32[176,128]{1,0:T(8,128)S(1)} %get-tuple-element.43), channel_id=1, source_target_pairs={{0,24},{1,25},{2,26},{3,27},{4,28},{5,29},{6,30},{7,31},{8,16},{9,... | collective-permute-start | bytes 270344 | tf_op jit(solution)/shard_map/ppermute | solution.py:264
  9.4 9.8 %collective-permute-start.12 = (f32[176,128]{1,0:T(8,128)S(1)}, f32[176,128]{1,0:T(8,128)S(1)}, u32[]{:S(2)}, u32[]{:S(2)}) collective-permute-start(f32[176,128]{1,0:T(8,128)S(1)} %get-tuple-element.43), channel_id=1, source_target_pairs={{0,16},{1,17},{2,18},{3,19},{4,20},{5,21},{6,22},{7,23},{8,24},{9,... | collective-permute-start | bytes 270344 | tf_op jit(solution)/shard_map/ppermute | solution.py:264
  10.3 8.9 %collective-permute-start.11 = (f32[176,128]{1,0:T(8,128)S(1)}, f32[176,128]{1,0:T(8,128)S(1)}, u32[]{:S(2)}, u32[]{:S(2)}) collective-permute-start(f32[176,128]{1,0:T(8,128)S(1)} %get-tuple-element.43), channel_id=1, source_target_pairs={{0,8},{1,9},{2,10},{3,11},{4,12},{5,13},{6,14},{7,15},{8,0},{9,1},... | collective-permute-start | bytes 270344 | tf_op jit(solution)/shard_map/ppermute | solution.py:264
  15.3 7.1 %collective-permute-start.3 = (f32[32,512]{1,0:T(8,128)S(1)}, f32[32,512]{1,0:T(8,128)S(1)}, u32[]{:S(2)}, u32[]{:S(2)}) collective-permute-start(f32[32,512]{1,0:T(8,128)S(1)} %shard_map.129.own), channel_id=1, source_target_pairs={{0,28},{1,29},{2,30},{3,31},{4,8},{5,9},{6,10},{7,11},{8,4},{9,5},... | collective-permute-start | bytes 196616 | tf_op jit(solution)/shard_map/ppermute | solution.py:289
  17.3 5.7 %collective-permute-start.2 = (f32[32,512]{1,0:T(8,128)S(1)}, f32[32,512]{1,0:T(8,128)S(1)}, u32[]{:S(2)}, u32[]{:S(2)}) collective-permute-start(f32[32,512]{1,0:T(8,128)S(1)} %shard_map.129.own), channel_id=1, source_target_pairs={{0,4},{1,5},{2,6},{3,7},{4,0},{5,1},{6,2},{7,3},{8,12},{9,13},{10,... | collective-permute-start | bytes 196616 | tf_op jit(solution)/shard_map/ppermute | solution.py:264
  19.2 15.0 %collective-permute-start.15 = (f32[4,176,128]{2,1,0:T(8,128)S(1)}, f32[4,176,128]{2,1,0:T(8,128)S(1)}, u32[]{:S(2)}, u32[]{:S(2)}) collective-permute-start(f32[4,176,128]{2,1,0:T(8,128)S(1)} %pad_maximum_fusion.refs_0_), channel_id=1, source_target_pairs={{0,4},{1,5},{2,6},{3,7},{4,0},{5,1},{6,2},{7,3},{8,12},{9,13},{10,... | collective-permute-start | bytes 1081352 | tf_op jit(solution)/shard_map/ppermute | solution.py:264
  19.6 13.9 %collective-permute-start.14 = (f32[3,176,128]{2,1,0:T(8,128)S(1)}, f32[3,176,128]{2,1,0:T(8,128)S(1)}, u32[]{:S(2)}, u32[]{:S(2)}) collective-permute-start(f32[3,176,128]{2,1,0:T(8,128)S(1)} %pad_maximum_fusion.1), channel_id=1, source_target_pairs={{0,2},{1,3},{2,0},{3,1},{4,6},{5,7},{6,4},{7,5},{8,10},{9,11},{10,... | collective-permute-start | bytes 811016 | tf_op jit(solution)/shard_map/ppermute | solution.py:264
  23.0 14.6 %copy-start = (bf16[1024,1024]{1,0:T(8,128)(2,1)S(1)}, bf16[1024,1024]{1,0:T(8,128)(2,1)}, u32[]{:S(2)}) copy-start(bf16[1024,1024]{1,0:T(8,128)(2,1)} %w_mid.1) | copy-start | bytes 6291460
  23.0 14.6 %copy-start.3 = (bf16[128,1024]{1,0:T(8,128)(2,1)S(1)}, bf16[128,1024]{1,0:T(8,128)(2,1)}, u32[]{:S(2)}) copy-start(bf16[128,1024]{1,0:T(8,128)(2,1)} %refs_7_.1) | copy-start | bytes 786436
  24.7 3.9 %collective-permute-start.5 = (f32[32,256]{1,0:T(8,128)S(1)}, f32[32,256]{1,0:T(8,128)S(1)}, u32[]{:S(2)}, u32[]{:S(2)}) collective-permute-start(f32[32,256]{1,0:T(8,128)S(1)} %get-tuple-element.36), channel_id=1, source_target_pairs={{0,2},{1,3},{2,0},{3,1},{4,6},{5,7},{6,4},{7,5},{8,10},{9,11},{10,... | collective-permute-start | bytes 98312 | tf_op jit(solution)/shard_map/ppermute | solution.py:264
  26.2 3.3 %collective-permute-start.6 = (f32[32,256]{1,0:T(8,128)S(1)}, f32[32,256]{1,0:T(8,128)S(1)}, u32[]{:S(2)}, u32[]{:S(2)}) collective-permute-start(f32[32,256]{1,0:T(8,128)S(1)} %get-tuple-element.37), channel_id=1, source_target_pairs={{0,3},{1,2},{2,1},{3,0},{4,7},{5,6},{6,5},{7,4},{8,11},{9,10},{10,... | collective-permute-start | bytes 98312 | tf_op jit(solution)/shard_map/ppermute | solution.py:264
  26.2 3.3 %collective-permute-start.4 = (f32[32,256]{1,0:T(8,128)S(1)}, f32[32,256]{1,0:T(8,128)S(1)}, u32[]{:S(2)}, u32[]{:S(2)}) collective-permute-start(f32[32,256]{1,0:T(8,128)S(1)} %get-tuple-element.37), channel_id=1, source_target_pairs={{0,1},{1,0},{2,3},{3,2},{4,5},{5,4},{6,7},{7,6},{8,9},{9,8},{10,11... | collective-permute-start | bytes 98312 | tf_op jit(solution)/shard_map/ppermute | solution.py:264
  29.5 6.5 %collective-permute-start.8 = (f32[4,32,256]{2,1,0:T(8,128)S(1)}, f32[4,32,256]{2,1,0:T(8,128)S(1)}, u32[]{:S(2)}, u32[]{:S(2)}) collective-permute-start(f32[4,32,256]{2,1,0:T(8,128)S(1)} %pad_maximum_fusion.4.refs_0_), channel_id=1, source_target_pairs={{0,8},{1,9},{2,10},{3,11},{4,12},{5,13},{6,14},{7,15},{8,0},{9,1},... | collective-permute-start | bytes 393224 | tf_op jit(solution)/shard_map/ppermute | solution.py:264
  30.6 6.9 %collective-permute-start.7 = (f32[4,32,256]{2,1,0:T(8,128)S(1)}, f32[4,32,256]{2,1,0:T(8,128)S(1)}, u32[]{:S(2)}, u32[]{:S(2)}) collective-permute-start(f32[4,32,256]{2,1,0:T(8,128)S(1)} %pad_maximum_fusion.4.refs_0_), channel_id=1, source_target_pairs={{0,4},{1,5},{2,6},{3,7},{4,0},{5,1},{6,2},{7,3},{8,12},{9,13},{10,... | collective-permute-start | bytes 393224 | tf_op jit(solution)/shard_map/ppermute | solution.py:264
  30.7 12.6 %collective-permute-start.10 = (f32[4,32,256]{2,1,0:T(8,128)S(1)}, f32[4,32,256]{2,1,0:T(8,128)S(1)}, u32[]{:S(2)}, u32[]{:S(2)}) collective-permute-start(f32[4,32,256]{2,1,0:T(8,128)S(1)} %pad_maximum_fusion.4.refs_0_), channel_id=1, source_target_pairs={{0,16},{1,17},{2,18},{3,19},{4,20},{5,21},{6,22},{7,23},{8,24},{9,... | collective-permute-start | bytes 393224 | tf_op jit(solution)/shard_map/ppermute | solution.py:264
  33.5 9.9 %collective-permute-start.9 = (f32[4,32,256]{2,1,0:T(8,128)S(1)}, f32[4,32,256]{2,1,0:T(8,128)S(1)}, u32[]{:S(2)}, u32[]{:S(2)}) collective-permute-start(f32[4,32,256]{2,1,0:T(8,128)S(1)} %pad_maximum_fusion.4.refs_0_), channel_id=1, source_target_pairs={{0,24},{1,25},{2,26},{3,27},{4,28},{5,29},{6,30},{7,31},{8,16},{9,... | collective-permute-start | bytes 393224 | tf_op jit(solution)/shard_map/ppermute | solution.py:264
  34.2 7.8 %collective-permute-start.16 = (f32[3,176,128]{2,1,0:T(8,128)S(1)}, f32[3,176,128]{2,1,0:T(8,128)S(1)}, u32[]{:S(2)}, u32[]{:S(2)}) collective-permute-start(f32[3,176,128]{2,1,0:T(8,128)S(1)} %collective-permute-done.14.refs_1_), channel_id=1, source_target_pairs={{0,4},{1,5},{2,6},{3,7},{4,0},{5,1},{6,2},{7,3},{8,12},{9,13},{10,... | collective-permute-start | bytes 811016 | tf_op jit(solution)/shard_map/ppermute | solution.py:264
  36.1 6.0 %collective-permute-start.17 = (f32[2,176,128]{2,1,0:T(8,128)S(1)}, f32[2,176,128]{2,1,0:T(8,128)S(1)}, u32[]{:S(2)}, u32[]{:S(2)}) collective-permute-start(f32[2,176,128]{2,1,0:T(8,128)S(1)} %pad_maximum_fusion.3), channel_id=1, source_target_pairs={{0,2},{1,3},{2,0},{3,1},{4,6},{5,7},{6,4},{7,5},{8,10},{9,11},{10,... | collective-permute-start | bytes 540680 | tf_op jit(solution)/shard_map/ppermute | solution.py:264
  41.2 11.7 %collective-permute-start.18 = (f32[4,32,256]{2,1,0:T(8,128)S(1)}, f32[4,32,256]{2,1,0:T(8,128)S(1)}, u32[]{:S(2)}, u32[]{:S(2)}) collective-permute-start(f32[4,32,256]{2,1,0:T(8,128)S(1)} %collective-permute-done.8.refs_2_), channel_id=1, source_target_pairs={{0,4},{1,5},{2,6},{3,7},{4,0},{5,1},{6,2},{7,3},{8,12},{9,13},{10,... | collective-permute-start | bytes 393224 | tf_op jit(solution)/shard_map/ppermute | solution.py:264
  43.4 9.5 %collective-permute-start.19 = (f32[2,4,32,256]{3,2,1,0:T(8,128)S(1)}, f32[2,4,32,256]{3,2,1,0:T(8,128)S(1)}, u32[]{:S(2)}, u32[]{:S(2)}) collective-permute-start(f32[2,4,32,256]{3,2,1,0:T(8,128)S(1)} %pad_maximum_fusion.2), channel_id=1, source_target_pairs={{0,4},{1,5},{2,6},{3,7},{4,0},{5,1},{6,2},{7,3},{8,12},{9,13},{10,... | collective-permute-start | bytes 786440 | tf_op jit(solution)/shard_map/ppermute | solution.py:264
  57.6 3.0 %collective-permute-start.21 = (f32[300,1024]{1,0:T(8,128)S(1)}, f32[300,1024]{1,0:T(8,128)S(1)}, u32[]{:S(2)}, u32[]{:S(2)}) collective-permute-start(f32[300,1024]{1,0:T(8,128)S(1)} %get-tuple-element.61.mine), channel_id=1, source_target_pairs={{0,1},{1,0},{2,3},{3,2},{4,5},{5,4},{6,7},{7,6},{8,9},{9,8},{10,11... | collective-permute-start | bytes 3686408 | tf_op jit(solution)/shard_map/ppermute | solution.py:264
  59.8 2.1 %collective-permute-start.20 = (f32[128,1024]{1,0:T(8,128)S(1)}, f32[128,1024]{1,0:T(8,128)S(1)}, u32[]{:S(2)}, u32[]{:S(2)}) collective-permute-start(f32[128,1024]{1,0:T(8,128)S(1)} %shard_map.137.mine), channel_id=1, source_target_pairs={{0,1},{1,0},{2,3},{3,2},{4,5},{5,4},{6,7},{7,6},{8,9},{9,8},{10,11... | collective-permute-start | bytes 1572872 | tf_op jit(solution)/shard_map/ppermute | solution.py:264
  (7 other events, 30.1 us)
